TPU v7x, 512 devices: a whole 4x4x16 slice. The times are simulated.
512 devices in a mesh: pair: 64 (over x_lo, z, core), band: 8 (over x_hi, y).
Axes of the slice: x: 4 (x_hi: 2, x_lo: 2; x = x_hi * 2 + x_lo), y: 4, z: 16, core: 2. Of those that a mesh axis runs over, the one named last changes fastest.
Arguments:
- spectra: bfloat16 [64, 2, 384, 16384], P('band', None, None, 'pair'), may hold values from -1040 to 1040
- window_valid: int32 [384, 16384], P(None, 'pair'), may hold values 0 or 1
Outputs:
- correlation: bfloat16 [2, 32, 16384, 256], P(None, 'band', 'pair')
All inputs are finite; a program needn't handle non-finite values. No bound on the sum of `window_valid` on one device may be relied on, other than what follows from the above.
Results may differ from a plain program's by a relative error of at most 0.0067.
Values may be sent and summed in bfloat16 or wider, within the bound.
No kernel may reach another device: no remote copies, remote signals or barrier semaphores. Data moves between devices by JAX's collectives and lax.ppermute only.
A program may use at most 64 MiB of HBM per device.

v0:
```python
import math

import jax
import jax.numpy as jnp
from jax import lax
from jax.sharding import PartitionSpec as P

FREQS = 64
ROUNDS = 2
LAG_DEV = 4


EPSILON = 1e-06


def shifted(block, axis, distance):
    devices = range(lax.axis_size(axis))
    route = [((i - distance) % len(devices), i) for i in devices]
    return lax.ppermute(block, axis, route)


def window_factor(spectra, window_valid):
    values = spectra.astype(jnp.float32)
    partial_energy = jnp.sum(values * values, axis=(0, 1))
    energy = lax.psum(partial_energy, "band")
    return window_valid.astype(jnp.float32) * lax.rsqrt(energy / FREQS + EPSILON)


def whiten_local(spectra, factor):
    return (spectra.astype(jnp.float32) * factor[None, None]).astype(jnp.bfloat16)


def partner_stack(partner):
    bin_count = partner.shape[0]
    windows = partner.shape[2]
    channel_count = partner.shape[3]
    stacked = partner.reshape(bin_count, 2 * windows, channel_count)
    turned = jnp.concatenate([partner[:, 1], -partner[:, 0]], axis=1)
    return jnp.concatenate([stacked, turned], axis=2)


def cross_spectra(own_white, partner):
    bin_count = own_white.shape[0]
    windows = own_white.shape[2]
    channel_count = own_white.shape[3]
    own_rows = own_white.reshape(bin_count, 2 * windows, channel_count)
    product = jnp.einsum(
        "fka,fkc->fac", own_rows, partner_stack(partner), preferred_element_type=jnp.float32
    )
    return product.astype(jnp.bfloat16).reshape(bin_count, channel_count, 2, channel_count)


def lag_table(lag_total):
    lag_index = jnp.arange(lag_total, dtype=jnp.float32) - lag_total // 2
    bin_index = jnp.arange(FREQS, dtype=jnp.float32) + 1.0
    phase_angle = 2.0 * math.pi / (2 * FREQS) * lag_index[:, None] * bin_index[None, :]
    return jnp.stack([jnp.cos(phase_angle), -jnp.sin(phase_angle)], axis=2).astype(jnp.bfloat16)


def regroup(cross_stack, kernel, lag_scale):
    lagged = jnp.einsum(
        "jfp,rfapb->rjab",
        kernel,
        lax.all_to_all(cross_stack, "band", split_axis=2, concat_axis=1, tiled=True),
        preferred_element_type=jnp.float32,
    )
    lagged = (lagged * lag_scale).astype(jnp.bfloat16)
    return lax.all_to_all(lagged, "band", split_axis=1, concat_axis=2, tiled=True)


def shards(spectra, window_valid):
    factor = window_factor(spectra, window_valid)
    own_white = whiten_local(spectra, factor)
    pairings = []
    moved_white = own_white
    for distance in range(1, ROUNDS + 1):
        moved_white = shifted(own_white, "pair", -distance)
        pairings.append((own_white, moved_white))
    kernel = lag_table(LAG_DEV * lax.axis_size("band"))
    lag_scale = 1.0 / math.sqrt(FREQS * spectra.shape[2])
    crosses = [cross_spectra(left_side, right_side)[None] for left_side, right_side in pairings]
    lagged = jnp.concatenate([regroup(single, kernel, lag_scale) for single in crosses], axis=0)
    return lagged


def solution(mesh):
    return jax.shard_map(
        shards,
        mesh=mesh,
        in_specs=(P("band", None, None, "pair"), P(None, "pair")),
        out_specs=P(None, "band", "pair", None),
        check_vma=False,
    )
```

profile of v0, /device:TPU:480, one launch (start us, length us, event | category | flops | bytes accessed | tf_op | source)
XLA Modules:
  0.0 311.6 jit_solution(7416536570857357041)
XLA Ops:
  6.5 0.0 copy-start
  6.5 0.0 copy-start.3
  6.5 0.0 all-reduce.2.cloned.1.call-start
  6.5 3.5 %fusion = f32[384,256]{1,0:T(8,128)} fusion(bf16[8,2,384,256]{3,2,1,0:T(8,128)(2,1)} %param.2), kind=kLoop, calls=%fused_computation.2 | loop fusion | flops 4620288 | bytes 3538944 | tf_op jit(solution)/shard_map/reduce_sum | solution.py:24
  10.0 0.0 all-reduce.2.cloned.1.call-update
  10.0 99.7 %all-reduce.2.cloned.1.call-done = f32[384,256]{1,0:T(8,128)} async-done(((f32[384,256]{1,0:T(8,128)}), f32[384,256]{1,0:T(8,128)}) %all-reduce.2.cloned.1.call-update) | async-done | bytes 393232 | tf_op jit(solution)/shard_map/psum | solution.py:25
  109.7 0.0 copy-done.3
  109.7 1.1 rsqrt_multiply_fusion
  110.8 0.0 copy-done
  110.8 2.4 fusion.1
  113.2 1.9 collective-permute-start
  115.1 3.3 %collective-permute-start.1 = (bf16[8,2,384,256]{3,2,0,1:T(8,128)(2,1)}, bf16[8,2,384,256]{3,2,0,1:T(8,128)(2,1)S(1)}, u32[]{:S(2)}, u32[]{:S(2)}) collective-permute-start(bf16[8,2,384,256]{3,2,0,1:T(8,128)(2,1)} %fusion.1), channel_id=1, source_target_pairs={{16,0},{24,8},{32,16},{40,24},{48,32},{56,40},{64,48},{72,56},{80,... | collective-permute-start | bytes 9437192 | tf_op jit(solution)/shard_map/ppermute | solution.py:19
  118.4 2.1 copy.19
  120.5 0.0 copy-start.1
  120.5 60.5 %collective-permute-done = bf16[8,2,384,256]{3,2,0,1:T(8,128)(2,1)S(1)} collective-permute-done((bf16[8,2,384,256]{3,2,0,1:T(8,128)(2,1)}, bf16[8,2,384,256]{3,2,0,1:T(8,128)(2,1)S(1)}, u32[]{:S(2)}, u32[]{:S(2)}) %collective-permute-start) | collective-permute-done | bytes 3145760 | tf_op jit(solution)/shard_map/ppermute | solution.py:19
  181.0 0.3 copy.20
  181.3 0.2 slice_bitcast_fusion.1
  181.5 0.0 copy-done.1
  181.5 3.1 fusion.23
  184.6 4.0 %broadcast_in_dim_reshape.6 = bf16[1,8,256,2,256]{4,3,2,1,0:T(2,128)(2,1)} reshape(bf16[8,256,512]{2,1,0:T(8,128)(2,1)} %fusion.23) | data formatting | bytes 4194304 | tf_op jit(solution)/shard_map/broadcast_in_dim;reshape | solution.py:81
  188.6 4.4 %copy.22 = bf16[1,8,256,2,256]{4,3,1,0,2:T(2,128)(2,1)} copy(bf16[1,8,256,2,256]{4,3,2,1,0:T(2,128)(2,1)} %broadcast_in_dim_reshape.6) | data formatting | bytes 4194304 | tf_op jit(solution)/shard_map/broadcast_in_dim;reshape | solution.py:81
  193.0 4.4 %all-to-all-start = ((bf16[1,8,256,2,256]{4,3,1,0,2:T(2,128)(2,1)}), bf16[1,8,256,2,256]{4,3,1,0,2:T(2,128)(2,1)}, u32[]{:S(2)}, u32[]{:S(2)}) async-start(bf16[1,8,256,2,256]{4,3,1,0,2:T(2,128)(2,1)} %copy.22), calls=%async_computation | async-start | bytes 4194304 | tf_op jit(solution)/shard_map/all_to_all | solution.py:64
  197.4 20.2 %collective-permute-done.1 = bf16[8,2,384,256]{3,2,0,1:T(8,128)(2,1)S(1)} collective-permute-done((bf16[8,2,384,256]{3,2,0,1:T(8,128)(2,1)}, bf16[8,2,384,256]{3,2,0,1:T(8,128)(2,1)S(1)}, u32[]{:S(2)}, u32[]{:S(2)}) %collective-permute-start.1) | collective-permute-done | bytes 3145760 | tf_op jit(solution)/shard_map/ppermute | solution.py:19
  217.6 0.2 copy.26
  217.8 0.0 copy-start.2
  217.8 0.2 slice_bitcast_fusion
  218.0 1.7 copy-done.2
  219.7 3.1 fusion.20
  222.8 2.5 broadcast_in_dim_reshape.7
  225.3 2.8 copy.28
  228.1 13.3 %all-to-all-done = bf16[1,8,256,2,256]{4,3,1,0,2:T(2,128)(2,1)} async-done(((bf16[1,8,256,2,256]{4,3,1,0,2:T(2,128)(2,1)}), bf16[1,8,256,2,256]{4,3,1,0,2:T(2,128)(2,1)}, u32[]{:S(2)}, u32[]{:S(2)}) %all-to-all-start) | async-done | bytes 2097184 | tf_op jit(solution)/shard_map/all_to_all | solution.py:64
  241.4 5.3 %all-to-all-start.2 = ((bf16[1,8,256,2,256]{4,3,1,0,2:T(2,128)(2,1)}), bf16[1,8,256,2,256]{4,3,1,0,2:T(2,128)(2,1)S(1)}, u32[]{:S(2)}, u32[]{:S(2)}) async-start(bf16[1,8,256,2,256]{4,3,1,0,2:T(2,128)(2,1)} %copy.28), calls=%async_computation.2 | async-start | bytes 4194304 | tf_op jit(solution)/shard_map/all_to_all | solution.py:64
  246.8 0.1 fusion.52
  246.9 2.1 fusion.49
  249.0 1.1 copy.24
  250.1 23.2 %all-to-all-done.2 = bf16[1,8,256,2,256]{4,3,1,0,2:T(2,128)(2,1)S(1)} async-done(((bf16[1,8,256,2,256]{4,3,1,0,2:T(2,128)(2,1)}), bf16[1,8,256,2,256]{4,3,1,0,2:T(2,128)(2,1)S(1)}, u32[]{:S(2)}, u32[]{:S(2)}) %all-to-all-start.2) | async-done | bytes 2097184 | tf_op jit(solution)/shard_map/all_to_all | solution.py:64
  273.3 4.8 %all-to-all-start.1 = ((bf16[1,32,32,256]{3,2,0,1:T(8,128)(2,1)}), bf16[1,32,32,256]{3,2,0,1:T(8,128)(2,1)S(1)}, u32[]{:S(2)}, u32[]{:S(2)}) async-start(bf16[1,32,32,256]{3,2,0,1:T(8,128)(2,1)} %copy.24), calls=%async_computation.1 | async-start | bytes 1048576 | tf_op jit(solution)/shard_map/all_to_all | solution.py:68
  278.1 0.5 fusion.46
  278.5 1.1 copy.30
  279.6 9.5 %all-to-all-done.1 = bf16[1,32,32,256]{3,2,0,1:T(8,128)(2,1)S(1)} async-done(((bf16[1,32,32,256]{3,2,0,1:T(8,128)(2,1)}), bf16[1,32,32,256]{3,2,0,1:T(8,128)(2,1)S(1)}, u32[]{:S(2)}, u32[]{:S(2)}) %all-to-all-start.1) | async-done | bytes 524320 | tf_op jit(solution)/shard_map/all_to_all | solution.py:68
  289.1 3.5 %all-to-all-start.3 = ((bf16[1,32,32,256]{3,2,0,1:T(8,128)(2,1)}), bf16[1,32,32,256]{3,2,0,1:T(8,128)(2,1)S(1)}, u32[]{:S(2)}, u32[]{:S(2)}) async-start(bf16[1,32,32,256]{3,2,0,1:T(8,128)(2,1)} %copy.30), calls=%async_computation.3 | async-start | bytes 1048576 | tf_op jit(solution)/shard_map/all_to_all | solution.py:68
  292.7 11.0 %all-to-all-done.3 = bf16[1,32,32,256]{3,2,0,1:T(8,128)(2,1)S(1)} async-done(((bf16[1,32,32,256]{3,2,0,1:T(8,128)(2,1)}), bf16[1,32,32,256]{3,2,0,1:T(8,128)(2,1)S(1)}, u32[]{:S(2)}, u32[]{:S(2)}) %all-to-all-start.3) | async-done | bytes 524320 | tf_op jit(solution)/shard_map/all_to_all | solution.py:68
  303.7 1.1 pad_maximum_fusion
  (4 shorter events, 0.1 us)
Async XLA Ops:
  6.5 104.3 %copy-start = (bf16[8,2,384,256]{3,2,1,0:T(8,128)(2,1)S(1)}, bf16[8,2,384,256]{3,2,1,0:T(8,128)(2,1)}, u32[]{:S(2)}) copy-start(bf16[8,2,384,256]{3,2,1,0:T(8,128)(2,1)} %param.2) | copy-start | bytes 9437188
  6.5 103.2 %copy-start.3 = (s32[384,256]{1,0:T(8,128)S(1)}, s32[384,256]{1,0:T(8,128)}, u32[]{:S(2)}) copy-start(s32[384,256]{1,0:T(8,128)} %param.3) | copy-start | bytes 1179652
  6.5 103.2 %all-reduce.2.cloned.1.call-start = ((), (), s32[]{:S(2)}) async-start(), calls=%async_computation.4 | async-start | bytes 786432 | tf_op jit(solution)/shard_map/psum | solution.py:25
  113.2 67.8 %collective-permute-start = (bf16[8,2,384,256]{3,2,0,1:T(8,128)(2,1)}, bf16[8,2,384,256]{3,2,0,1:T(8,128)(2,1)S(1)}, u32[]{:S(2)}, u32[]{:S(2)}) collective-permute-start(bf16[8,2,384,256]{3,2,0,1:T(8,128)(2,1)} %fusion.1), channel_id=1, source_target_pairs={{8,0},{16,8},{24,16},{32,24},{40,32},{48,40},{56,48},{64,56},{72,6... | collective-permute-start | bytes 9437192 | tf_op jit(solution)/shard_map/ppermute | solution.py:19
  115.1 102.5 %collective-permute-start.1 = (bf16[8,2,384,256]{3,2,0,1:T(8,128)(2,1)}, bf16[8,2,384,256]{3,2,0,1:T(8,128)(2,1)S(1)}, u32[]{:S(2)}, u32[]{:S(2)}) collective-permute-start(bf16[8,2,384,256]{3,2,0,1:T(8,128)(2,1)} %fusion.1), channel_id=1, source_target_pairs={{16,0},{24,8},{32,16},{40,24},{48,32},{56,40},{64,48},{72,56},{80,... | collective-permute-start | bytes 9437192 | tf_op jit(solution)/shard_map/ppermute | solution.py:19
  120.5 61.0 %copy-start.1 = (bf16[8,2,384,256]{3,2,1,0:T(8,128)(2,1)}, bf16[8,2,384,256]{3,2,1,0:T(8,128)(2,1)S(1)}, u32[]{:S(2)}) copy-start(bf16[8,2,384,256]{3,2,1,0:T(8,128)(2,1)S(1)} %copy.19) | copy-start | bytes 9437188
  193.0 48.5 %all-to-all-start = ((bf16[1,8,256,2,256]{4,3,1,0,2:T(2,128)(2,1)}), bf16[1,8,256,2,256]{4,3,1,0,2:T(2,128)(2,1)}, u32[]{:S(2)}, u32[]{:S(2)}) async-start(bf16[1,8,256,2,256]{4,3,1,0,2:T(2,128)(2,1)} %copy.22), calls=%async_computation | async-start | bytes 4194304 | tf_op jit(solution)/shard_map/all_to_all | solution.py:64
  217.8 1.9 copy-start.2
  241.4 31.9 %all-to-all-start.2 = ((bf16[1,8,256,2,256]{4,3,1,0,2:T(2,128)(2,1)}), bf16[1,8,256,2,256]{4,3,1,0,2:T(2,128)(2,1)S(1)}, u32[]{:S(2)}, u32[]{:S(2)}) async-start(bf16[1,8,256,2,256]{4,3,1,0,2:T(2,128)(2,1)} %copy.28), calls=%async_computation.2 | async-start | bytes 4194304 | tf_op jit(solution)/shard_map/all_to_all | solution.py:64
  273.3 15.8 %all-to-all-start.1 = ((bf16[1,32,32,256]{3,2,0,1:T(8,128)(2,1)}), bf16[1,32,32,256]{3,2,0,1:T(8,128)(2,1)S(1)}, u32[]{:S(2)}, u32[]{:S(2)}) async-start(bf16[1,32,32,256]{3,2,0,1:T(8,128)(2,1)} %copy.24), calls=%async_computation.1 | async-start | bytes 1048576 | tf_op jit(solution)/shard_map/all_to_all | solution.py:68
  289.1 14.5 %all-to-all-start.3 = ((bf16[1,32,32,256]{3,2,0,1:T(8,128)(2,1)}), bf16[1,32,32,256]{3,2,0,1:T(8,128)(2,1)S(1)}, u32[]{:S(2)}, u32[]{:S(2)}) async-start(bf16[1,32,32,256]{3,2,0,1:T(8,128)(2,1)} %copy.30), calls=%async_computation.3 | async-start | bytes 1048576 | tf_op jit(solution)/shard_map/all_to_all | solution.py:68
Sparse Core Ops, SparseCore 0:
  10.3 99.4 all-reduce.1
where the time goes:
time: 312 us
  waiting for transfers between devices  237 us (76%)
  starting transfers between devices  23.1 us (7%)
  local copies, waits for them, and re-layouts  20.2 us (6%)
  between operations  13.5 us (4%)
  matrix products  8.71 us (3%)
  other arithmetic  8.51 us (3%)
    psum x1, waiting for transfers between devices, window_factor(): energy = lax.psum(partial_energy, 'band')  99.7 us
    ppermute x2, waiting for transfers between devices, shifted(): return lax.ppermute(block, axis, route)  80.7 us
    all_to_all x2, waiting for transfers between devices, regroup(): lax.all_to_all(cross_stack, 'band', split_axis=2, concat_axis=1, tiled=True)  36.5 us
    all_to_all x2, waiting for transfers between devices, regroup(): lax.all_to_all(lagged, 'band', split_axis=1, concat_axis=2, tiled=True)  20.5 us
    another operation x4, local copies, waits for them, and re-layouts, shards(): cross_spectra(left_side, right_side)[None]  13.7 us
    all_to_all x2, starting transfers between devices, regroup(): lax.all_to_all(cross_stack, 'band', split_axis=2, concat_axis=1, tiled=True)  9.69 us
    all_to_all x2, starting transfers between devices, regroup(): lax.all_to_all(lagged, 'band', split_axis=1, concat_axis=2, tiled=True)  8.26 us
  transfers between devices with their start and end apart: 7, of which 7 were waited for; matrix products, arithmetic and copies ran while one was open for 9% of the time, Pallas kernels for 0%

commit v1 on v0

v1 whole, which is shorter than its diff:
```python
import math

import jax
import jax.numpy as jnp
import numpy as np
from jax import lax
from jax.experimental import pallas as pl
from jax.experimental.pallas import tpu as pltpu
from jax.sharding import PartitionSpec as P

FREQS = 64
KEEP = 32
WIN = 384
EPSILON = 1e-06
HALF = 128
SUB = 16
VMEM_LIMIT = 48 * 1024 * 1024

BF16 = jnp.bfloat16
F32 = jnp.float32


def params():
    return pltpu.CompilerParams(vmem_limit_bytes=VMEM_LIMIT)


def lag_matrix():
    lag_index = np.arange(KEEP, dtype=np.float32) - np.float32(KEEP // 2)
    bin_index = np.arange(FREQS, dtype=np.float32) + np.float32(1.0)
    step = np.float32(2.0 * math.pi / (2 * FREQS))
    phase = (step * lag_index)[:, None] * bin_index[None, :]
    table = np.stack([np.cos(phase), -np.sin(phase)], axis=2).reshape(KEEP, 2 * FREQS)
    return jnp.asarray(np.kron(table, np.eye(SUB, dtype=np.float32)), dtype=BF16)


def whiten(raw, factor):
    return (raw.astype(F32) * factor.astype(F32)[None]).astype(BF16)


def product(left, right):
    windows = left.shape[1]
    rows = left.reshape(2 * windows, left.shape[2])
    top = jnp.concatenate([right[0], right[1]], axis=1)
    low = jnp.concatenate([right[1], -right[0]], axis=1)
    cols = jnp.concatenate([top, low], axis=0)
    return lax.dot_general(rows, cols, (((0,), (0,)), ((), ())), preferred_element_type=F32)


def store_tall(out_ref, result):
    for part in range(2):
        piece = result[:, part * HALF : (part + 1) * HALF]
        out_ref[:, part] = piece.astype(BF16).reshape(8, 32, HALF)


def store_wide(out_ref, result):
    for part in range(2):
        for half in range(2):
            start = part * 2 * HALF + half * HALF
            piece = result[:, start : start + HALF]
            out_ref[half * 4 : half * 4 + 4, part] = piece.astype(BF16).reshape(4, 32, HALF)


def early_kernel(odd_ref, s_ref, t_ref, fs_ref, ft_ref, sw_ref, tw_ref, out_ref):
    sw_ref[0] = whiten(s_ref[0], fs_ref[...])
    tw_ref[0] = whiten(t_ref[0], ft_ref[...])

    @pl.when(odd_ref[0] == 0)
    def _():
        store_tall(out_ref, product(sw_ref[0], tw_ref[0, :, :, :HALF]))

    @pl.when(odd_ref[0] != 0)
    def _():
        store_tall(out_ref, product(tw_ref[0], sw_ref[0, :, :, HALF:]))


def first_kernel(odd_ref, s_ref, u_ref, fu_ref, uw_ref, out_ref):
    uw_ref[0] = whiten(u_ref[0], fu_ref[...])

    @pl.when(odd_ref[0] == 0)
    def _():
        store_tall(out_ref, product(s_ref[0], uw_ref[0]))

    @pl.when(odd_ref[0] != 0)
    def _():
        store_wide(out_ref, product(uw_ref[0], s_ref[0]))


def second_kernel(odd_ref, s_ref, t_ref, u_ref, fu_ref, v_ref, out_ref, mid_ref):
    uw = whiten(u_ref[0], fu_ref[...])

    @pl.when(odd_ref[0] == 0)
    def _():
        store_tall(out_ref, product(s_ref[0], uw))
        store_tall(mid_ref, product(t_ref[0], uw))

    @pl.when(odd_ref[0] != 0)
    def _():
        store_wide(out_ref, product(uw, s_ref[0]))
        store_tall(mid_ref, product(s_ref[0], v_ref[0]))


def bin_spec(channels):
    return pl.BlockSpec((1, 2, WIN, channels), lambda f: (f, 0, 0, 0))


def factor_spec(channels):
    return pl.BlockSpec((WIN, channels), lambda f: (0, 0))


def flag_spec():
    return pl.BlockSpec(memory_space=pltpu.SMEM)


def send_spec():
    return pl.BlockSpec((8, 2, 32, HALF), lambda f: (0, f, 0, 0))


SEND = jax.ShapeDtypeStruct((8, 16, 32, HALF), BF16)


def cost(products, nbytes):
    return pl.CostEstimate(
        flops=int(products * 2 * 8 * 768 * 256 * 256), bytes_accessed=int(nbytes), transcendentals=0
    )


def early(odd, s, t, fs, ft):
    whole = jax.ShapeDtypeStruct(s.shape, BF16)
    return pl.pallas_call(
        early_kernel,
        grid=(8,),
        in_specs=[flag_spec(), bin_spec(256), bin_spec(256), factor_spec(256), factor_spec(256)],
        out_specs=[bin_spec(256), bin_spec(256), send_spec()],
        out_shape=[whole, whole, SEND],
        compiler_params=params(),
        cost_estimate=cost(1, 13 << 20),
        name="early",
    )(odd, s, t, fs, ft)


def first(odd, sw, u, fu):
    return pl.pallas_call(
        first_kernel,
        grid=(8,),
        in_specs=[flag_spec(), bin_spec(256), bin_spec(HALF), factor_spec(HALF)],
        out_specs=[bin_spec(HALF), send_spec()],
        out_shape=[jax.ShapeDtypeStruct(u.shape, BF16), SEND],
        compiler_params=params(),
        cost_estimate=cost(1, 7 << 20),
        name="first",
    )(odd, sw, u, fu)


def second(odd, sw, tw, u, fu, vw):
    return pl.pallas_call(
        second_kernel,
        grid=(8,),
        in_specs=[flag_spec(), bin_spec(256), bin_spec(256), bin_spec(HALF), factor_spec(HALF), bin_spec(HALF)],
        out_specs=[send_spec(), send_spec()],
        out_shape=[SEND, SEND],
        compiler_params=params(),
        cost_estimate=cost(2, 11 << 20),
        name="second",
    )(odd, sw, tw, u, fu, vw)


def lags_kernel(scale, matrix_ref, cross_ref, out_ref):
    cross = cross_ref[...].reshape(2 * FREQS, 32, HALF)
    pair = jnp.concatenate([cross[:, :SUB], cross[:, SUB:]], axis=2)
    lagged = lax.dot_general(
        matrix_ref[...],
        pair.reshape(2 * FREQS * SUB, 2 * HALF),
        (((1,), (0,)), ((), ())),
        preferred_element_type=F32,
    )
    lagged = (lagged * scale).astype(BF16)
    for half in range(2):
        piece = lagged[:, half * HALF : (half + 1) * HALF].reshape(8, 4, SUB, HALF)
        out_ref[:, :, half * SUB : (half + 1) * SUB] = piece


def to_lags(matrix, cross, scale):
    def kernel(matrix_ref, cross_ref, out_ref):
        lags_kernel(scale, matrix_ref, cross_ref, out_ref)

    return pl.pallas_call(
        kernel,
        in_specs=[pl.BlockSpec(memory_space=pltpu.VMEM)] * 2,
        out_specs=pl.BlockSpec(memory_space=pltpu.VMEM),
        out_shape=jax.ShapeDtypeStruct((8, 4, 32, HALF), BF16),
        compiler_params=params(),
        cost_estimate=pl.CostEstimate(
            flops=2 * 512 * 2048 * 256, bytes_accessed=4 << 20, transcendentals=0
        ),
        name="to_lags",
    )(matrix, cross)


def assemble_kernel(odd_ref, own_ref, got_ref, x0_ref, x1_ref, out_ref):
    for src in range(8):
        rows = slice(src * 32, src * 32 + 32)
        out_ref[0, :, rows, :HALF] = own_ref[src]
        out_ref[0, :, rows, HALF:] = got_ref[src]

    @pl.when(odd_ref[0] == 0)
    def _():
        for src in range(8):
            rows = slice(src * 32, src * 32 + 32)
            out_ref[1, :, rows, :HALF] = x0_ref[src]
            out_ref[1, :, rows, HALF:] = x1_ref[src]

    @pl.when(odd_ref[0] != 0)
    def _():
        for index, ref in enumerate((x0_ref, x1_ref)):
            for src in range(8):
                half, row = src // 4, index * HALF + (src % 4) * 32
                out_ref[1, :, row : row + 32, half * HALF : (half + 1) * HALF] = ref[src]


def assemble(odd, own, got, x0, x1):
    return pl.pallas_call(
        assemble_kernel,
        in_specs=[flag_spec()] + [pl.BlockSpec(memory_space=pltpu.VMEM)] * 4,
        out_specs=pl.BlockSpec(memory_space=pltpu.VMEM),
        out_shape=jax.ShapeDtypeStruct((2, 4, 256, 256), BF16),
        compiler_params=params(),
        cost_estimate=pl.CostEstimate(flops=0, bytes_accessed=2 << 20, transcendentals=0),
        name="assemble",
    )(odd, own, got, x0, x1)


def band_sum(value):
    exchanges = (lambda b: b ^ 1, lambda b: (b // 4) * 4 + 3 - b % 4, lambda b: (b + 4) % 8)
    for partner in exchanges:
        route = [(b, partner(b)) for b in range(8)]
        value = value + lax.ppermute(value.astype(BF16), "band", route).astype(F32)
    return value


def regroup(block):
    return lax.all_to_all(block, "band", split_axis=0, concat_axis=0, tiled=True)


def shards(spectra, window_valid):
    blocks = lax.axis_size("pair")
    odd = lax.axis_index("pair") % 2
    flag = odd.astype(jnp.int32).reshape(1)
    across = [((p + 2) % blocks, p) if p % 2 == 0 else ((p - 2) % blocks, p) for p in range(blocks)]
    swap = [(p ^ 1, p) for p in range(blocks)]
    back = [(p, p) if p % 2 == 0 else ((p + 2) % blocks, p) for p in range(blocks)]

    u0 = lax.ppermute(spectra[..., :HALF], "pair", across)
    t = lax.ppermute(spectra, "pair", swap)
    u1 = lax.ppermute(spectra[..., HALF:], "pair", across)

    values = spectra.astype(F32)
    energy = band_sum(jnp.sum(values * values, axis=(0, 1)))
    fs = window_valid.astype(F32) * lax.rsqrt(energy / FREQS + EPSILON)
    fs16 = fs.astype(BF16)
    ft = lax.ppermute(fs16, "pair", swap)
    fu = lax.ppermute(fs16, "pair", across)

    matrix = lag_matrix()
    scale = 1.0 / math.sqrt(FREQS * WIN)

    sw, tw, cross_e = early(flag, spectra, t, fs, ft)
    got_e = regroup(cross_e)
    uw0, cross_f0 = first(flag, sw, u0, fu[:, :HALF])
    vw = lax.ppermute(uw0, "pair", swap)
    got_f0 = regroup(cross_f0)
    cross_f1, cross_g = second(flag, sw, tw, u1, fu[:, HALF:], vw)
    got_f1 = regroup(cross_f1)
    got_g = regroup(cross_g)

    lag_e = regroup(to_lags(matrix, got_e, scale))
    lag_f0 = lax.ppermute(regroup(to_lags(matrix, got_f0, scale)), "pair", back)
    lag_f1 = lax.ppermute(regroup(to_lags(matrix, got_f1, scale)), "pair", back)
    lag_g = regroup(to_lags(matrix, got_g, scale))
    own = jnp.where(odd == 0, lag_e, lag_g)
    got = lax.ppermute(jnp.where(odd == 0, lag_g, lag_e), "pair", swap)
    return assemble(flag, own, got, lag_f0, lag_f1)


def solution(mesh):
    return jax.shard_map(
        shards,
        mesh=mesh,
        in_specs=(P("band", None, None, "pair"), P(None, "pair")),
        out_specs=P(None, "band", "pair", None),
        check_vma=False,
    )
```

time: 312 us -> 229 us (0.73)
  the two profiles are of different devices: /device:TPU:480 before, /device:TPU:1 now
where the time goes in v1:
time: 229 us; the launch traced here: 227 us
  waiting for transfers between devices  86.6 us (38%)
  starting transfers between devices  76.4 us (33%)
  Pallas kernels  31.2 us (14%)
  blocking collectives  20.6 us (9%)
  local copies, waits for them, and re-layouts  8.44 us (4%)
  other arithmetic  3.92 us (2%)
    all_to_all x7, waiting for transfers between devices, regroup(): lax.all_to_all(block, 'band', split_axis=0, concat_axis=0, tiled=True)  42.7 us
    all_to_all x7, starting transfers between devices, regroup(): lax.all_to_all(block, 'band', split_axis=0, concat_axis=0, tiled=True)  36.7 us
    ppermute x3, waiting for transfers between devices, band_sum(): value = value + lax.ppermute(value.astype(BF16), 'band', route).astype(F32)  31.7 us
    all_to_all x1, blocking collectives, regroup(): lax.all_to_all(block, 'band', split_axis=0, concat_axis=0, tiled=True)  20.6 us
    ppermute x1, starting transfers between devices, shards(): t = lax.ppermute(spectra, 'pair', swap)  9.04 us
    pallas_call x1, Pallas kernels, early(): pl.pallas_call(early_kernel, grid=(8,), in_specs=[flag_spec(), bin_spec(2...  8.33 us
    pallas_call x1, Pallas kernels, second(): pl.pallas_call(second_kernel, grid=(8,), in_specs=[flag_spec(), bin_spec(...  7.79 us
    ppermute x1, starting transfers between devices, shards(): lag_f0 = lax.ppermute(regroup(to_lags(matrix, got_f0, scale)), 'pair', back)  7.11 us
  transfers between devices with their start and end apart: 19, of which 11 were waited for; matrix products, arithmetic and copies ran while one was open for 3% of the time, Pallas kernels for 13%

profile of v1, /device:TPU:1, one launch (start us, length us, event | category | flops | bytes accessed | tf_op | source)
XLA Modules:
  0.0 227.3 jit_solution(833479937356539392)
XLA Ops:
  0.0 9.0 %collective-permute-start = (bf16[8,2,384,256]{3,2,1,0:T(8,128)(2,1)}, bf16[8,2,384,256]{3,2,1,0:T(8,128)(2,1)}, u32[]{:S(2)}, u32[]{:S(2)}) collective-permute-start(bf16[8,2,384,256]{3,2,1,0:T(8,128)(2,1)} %s_ref.1), channel_id=1, source_target_pairs={{8,0},{0,8},{24,16},{16,24},{40,32},{32,40},{56,48},{48,56},{72,64... | collective-permute-start | bytes 9437192 | tf_op jit(solution)/shard_map/ppermute | solution.py:253
  9.1 2.5 %multiply_reduce_fusion = f32[384,256]{1,0:T(8,128)S(1)} fusion(bf16[8,2,384,256]{3,2,1,0:T(8,128)(2,1)} %s_ref.1), kind=kLoop, calls=%fused_computation | loop fusion | flops 4620288 | bytes 3538944 | tf_op jit(solution)/shard_map/reduce_sum | solution.py:257
  11.6 1.9 collective-permute-start.1
  13.6 6.5 %collective-permute-done.1 = bf16[384,256]{1,0:T(8,128)(2,1)S(1)} collective-permute-done((bf16[384,256]{1,0:T(8,128)(2,1)S(1)}, bf16[384,256]{1,0:T(8,128)(2,1)S(1)}, u32[]{:S(2)}, u32[]{:S(2)}) %collective-permute-start.1) | collective-permute-done | bytes 196640 | tf_op jit(solution)/shard_map/ppermute | solution.py:236
  20.1 2.1 collective-permute-start.2
  22.2 2.5 %fusion.3 = (bf16[8,2,384,128]{3,2,1,0:T(8,128)(2,1)}, bf16[8,2,384,128]{3,2,1,0:T(8,128)(2,1)}) fusion(bf16[8,2,384,256]{3,2,1,0:T(8,128)(2,1)S(1)} %copy-done.6), kind=kLoop, calls=%fused_computation.9 | loop fusion | bytes 6291456 | tf_op jit(solution)/shard_map/slice | solution.py:252
  24.7 1.9 collective-permute-start.7
  26.6 2.3 %collective-permute-done.2 = bf16[384,256]{1,0:T(8,128)(2,1)S(1)} collective-permute-done((bf16[384,256]{1,0:T(8,128)(2,1)S(1)}, bf16[384,256]{1,0:T(8,128)(2,1)S(1)}, u32[]{:S(2)}, u32[]{:S(2)}) %collective-permute-start.2) | collective-permute-done | bytes 196640 | tf_op jit(solution)/shard_map/ppermute | solution.py:236
  29.0 1.9 collective-permute-start.3
  31.0 22.8 %collective-permute-done.3 = bf16[384,256]{1,0:T(8,128)(2,1)S(1)} collective-permute-done((bf16[384,256]{1,0:T(8,128)(2,1)S(1)}, bf16[384,256]{1,0:T(8,128)(2,1)S(1)}, u32[]{:S(2)}, u32[]{:S(2)}) %collective-permute-start.3) | collective-permute-done | bytes 196640 | tf_op jit(solution)/shard_map/ppermute | solution.py:236
  53.8 0.2 fusion.2
  54.0 4.7 %collective-permute-start.4 = (bf16[384,256]{1,0:T(8,128)(2,1)S(1)}, bf16[384,256]{1,0:T(8,128)(2,1)S(1)}, u32[]{:S(2)}, u32[]{:S(2)}) collective-permute-start(bf16[384,256]{1,0:T(8,128)(2,1)S(1)} %get-tuple-element.19), channel_id=1, source_target_pairs={{8,0},{0,8},{24,16},{16,24},{40,32},{32,40},{56,48},{48,56},{72,64... | collective-permute-start | bytes 589832 | tf_op jit(solution)/shard_map/ppermute | solution.py:260
  58.7 1.0 collective-permute-done.4.ft_ref
  59.8 8.3 %early.1 = (bf16[8,2,384,256]{3,2,1,0:T(8,128)(2,1)S(1)}, bf16[8,2,384,256]{3,2,1,0:T(8,128)(2,1)}, bf16[8,16,32,128]{3,2,1,0:T(8,128)(2,1)S(1)}) custom-call(s32[1]{0:T(128)} %bitcast.odd_ref, bf16[8,2,384,256]{3,2,1,0:T(8,128)(2,1)} %s_ref.1, bf16[8,2,384,256]{3,2,1,0:T(8,128)(2,1)} %collective-permute-done.t_ref, ...), custom_call_target="tpu_custom_call" | custom-call | flops 805306368 | bytes 13631488 | tf_op jit(solution)/shard_map/early/pallas_call | solution.py:129
  68.1 1.7 copy-done.1
  69.8 1.0 copy-done.3
  70.8 3.6 %all-to-all-start = ((bf16[8,16,32,128]{3,2,1,0:T(8,128)(2,1)}), bf16[8,16,32,128]{3,2,1,0:T(8,128)(2,1)S(1)}, u32[]{:S(2)}, u32[]{:S(2)}) async-start(bf16[8,16,32,128]{3,2,1,0:T(8,128)(2,1)} %copy-done.3), calls=%async_computation | async-start | bytes 2097152 | tf_op jit(solution)/shard_map/all_to_all | solution.py:241
  74.3 1.9 collective-permute-start.6
  76.2 1.9 collective-permute-start.5
  78.2 6.6 %collective-permute-done.6 = bf16[384,256]{1,0:T(8,128)(2,1)S(1)} collective-permute-done((bf16[384,256]{1,0:T(8,128)(2,1)S(1)}, bf16[384,256]{1,0:T(8,128)(2,1)S(1)}, u32[]{:S(2)}, u32[]{:S(2)}) %collective-permute-start.6) | collective-permute-done | bytes 196640 | tf_op jit(solution)/shard_map/ppermute | solution.py:261
  84.8 7.0 %first.1 = (bf16[8,2,384,128]{3,2,1,0:T(8,128)(2,1)}, bf16[8,16,32,128]{3,2,1,0:T(8,128)(2,1)S(1)}) custom-call(s32[1]{0:T(128)} %bitcast.odd_ref, bf16[8,2,384,256]{3,2,1,0:T(8,128)(2,1)} %copy-done.1, bf16[8,2,384,128]{3,2,1,0:T(8,128)(2,1)S(1)} %collective-permute-done.7.u_ref, bf16[384,128]{1,0:T(8,128)(2,1)S(1)} %get-tuple-element.25.fu_ref), custom_call_target="tpu_custom_call" | custom-call | flops 805306368 | bytes 7340032 | tf_op jit(solution)/shard_map/first/pallas_call | solution.py:142
  91.8 1.0 copy-done.4
  92.8 2.7 %collective-permute-start.8 = (bf16[8,2,384,128]{3,2,1,0:T(8,128)(2,1)}, bf16[8,2,384,128]{3,2,1,0:T(8,128)(2,1)}, u32[]{:S(2)}, u32[]{:S(2)}) collective-permute-start(bf16[8,2,384,128]{3,2,1,0:T(8,128)(2,1)} %get-tuple-element.15), channel_id=1, source_target_pairs={{8,0},{0,8},{24,16},{16,24},{40,32},{32,40},{56,48},{48,56},{72,64... | collective-permute-start | bytes 4718600 | tf_op jit(solution)/shard_map/ppermute | solution.py:269
  95.5 12.5 %all-to-all-done.cross_ref = bf16[8,16,32,128]{3,2,1,0:T(8,128)(2,1)S(1)} async-done(((bf16[8,16,32,128]{3,2,1,0:T(8,128)(2,1)}), bf16[8,16,32,128]{3,2,1,0:T(8,128)(2,1)S(1)}, u32[]{:S(2)}, u32[]{:S(2)}) %all-to-all-start) | async-done | bytes 1048608 | tf_op jit(solution)/shard_map/all_to_all | solution.py:241
  108.0 4.2 %all-to-all-start.4 = ((bf16[8,16,32,128]{3,2,1,0:T(8,128)(2,1)}), bf16[8,16,32,128]{3,2,1,0:T(8,128)(2,1)}, u32[]{:S(2)}, u32[]{:S(2)}) async-start(bf16[8,16,32,128]{3,2,1,0:T(8,128)(2,1)} %copy-done.4), calls=%async_computation.4 | async-start | bytes 2097152 | tf_op jit(solution)/shard_map/all_to_all | solution.py:241
  112.3 1.4 to_lags.4
  113.7 12.3 %all-to-all-done.4.cross_ref = bf16[8,16,32,128]{3,2,1,0:T(8,128)(2,1)} async-done(((bf16[8,16,32,128]{3,2,1,0:T(8,128)(2,1)}), bf16[8,16,32,128]{3,2,1,0:T(8,128)(2,1)}, u32[]{:S(2)}, u32[]{:S(2)}) %all-to-all-start.4) | async-done | bytes 1048608 | tf_op jit(solution)/shard_map/all_to_all | solution.py:241
  126.0 6.3 %all-to-all-start.1 = ((bf16[8,4,32,128]{3,2,1,0:T(8,128)(2,1)}), bf16[8,4,32,128]{3,2,1,0:T(8,128)(2,1)S(1)}, u32[]{:S(2)}, u32[]{:S(2)}) async-start(bf16[8,4,32,128]{3,2,1,0:T(8,128)(2,1)} %to_lags.4), calls=%async_computation.1 | async-start | bytes 524288 | tf_op jit(solution)/shard_map/all_to_all | solution.py:241
  132.4 2.6 %to_lags.6 = bf16[8,4,32,128]{3,2,1,0:T(8,128)(2,1)} custom-call(bf16[512,2048]{1,0:T(8,128)(2,1)S(1)} %copy-done, bf16[8,16,32,128]{3,2,1,0:T(8,128)(2,1)} %all-to-all-done.4.cross_ref), custom_call_target="tpu_custom_call" | custom-call | flops 536870912 | bytes 4194304 | tf_op jit(solution)/shard_map/to_lags/pallas_call | solution.py:186
  135.0 4.9 %all-to-all-done.1 = bf16[8,4,32,128]{3,2,1,0:T(8,128)(2,1)S(1)} async-done(((bf16[8,4,32,128]{3,2,1,0:T(8,128)(2,1)}), bf16[8,4,32,128]{3,2,1,0:T(8,128)(2,1)S(1)}, u32[]{:S(2)}, u32[]{:S(2)}) %all-to-all-start.1) | async-done | bytes 262176 | tf_op jit(solution)/shard_map/all_to_all | solution.py:241
  140.0 3.5 %all-to-all-start.5 = ((bf16[8,4,32,128]{3,2,1,0:T(8,128)(2,1)}), bf16[8,4,32,128]{3,2,1,0:T(8,128)(2,1)S(1)}, u32[]{:S(2)}, u32[]{:S(2)}) async-start(bf16[8,4,32,128]{3,2,1,0:T(8,128)(2,1)} %to_lags.6), calls=%async_computation.5 | async-start | bytes 524288 | tf_op jit(solution)/shard_map/all_to_all | solution.py:241
  143.5 7.8 %second.1 = (bf16[8,16,32,128]{3,2,1,0:T(8,128)(2,1)S(1)}, bf16[8,16,32,128]{3,2,1,0:T(8,128)(2,1)S(1)}) custom-call(s32[1]{0:T(128)} %bitcast.odd_ref, bf16[8,2,384,256]{3,2,1,0:T(8,128)(2,1)} %copy-done.1, bf16[8,2,384,256]{3,2,1,0:T(8,128)(2,1)} %get-tuple-element.14.t_ref, bf16[8,2,384,128]{3,2,1,0:T(8,128)(2,1)} %collective-permute-done.5.u_ref, ...), custom_call_target="tpu_custom_call" | custom-call | flops 1610612736 | bytes 11534336 | tf_op jit(solution)/shard_map/second/pallas_call | solution.py:155
  151.3 1.0 copy-done.5
  152.3 20.6 %all_to_all.40.cross_ref = bf16[8,16,32,128]{3,2,1,0:T(8,128)(2,1)} all-to-all(bf16[8,16,32,128]{3,2,1,0:T(8,128)(2,1)S(1)} %get-tuple-element.16), channel_id=1, replica_groups=mesh['pair'=64,'band'=8] {'band'}, dimensions={0} | all-to-all | bytes 2097152 | tf_op jit(solution)/shard_map/all_to_all | solution.py:241
  172.9 3.6 %all-to-all-start.6 = ((bf16[8,16,32,128]{3,2,1,0:T(8,128)(2,1)}), bf16[8,16,32,128]{3,2,1,0:T(8,128)(2,1)S(1)}, u32[]{:S(2)}, u32[]{:S(2)}) async-start(bf16[8,16,32,128]{3,2,1,0:T(8,128)(2,1)} %copy-done.5), calls=%async_computation.6 | async-start | bytes 2097152 | tf_op jit(solution)/shard_map/all_to_all | solution.py:241
  176.4 1.2 copy-done.2
  177.6 1.4 to_lags.5
  179.1 8.3 %all-to-all-done.6.cross_ref = bf16[8,16,32,128]{3,2,1,0:T(8,128)(2,1)S(1)} async-done(((bf16[8,16,32,128]{3,2,1,0:T(8,128)(2,1)}), bf16[8,16,32,128]{3,2,1,0:T(8,128)(2,1)S(1)}, u32[]{:S(2)}, u32[]{:S(2)}) %all-to-all-start.6) | async-done | bytes 1048608 | tf_op jit(solution)/shard_map/all_to_all | solution.py:241
  187.4 8.2 %all-to-all-start.3 = ((bf16[8,4,32,128]{3,2,1,0:T(8,128)(2,1)}), bf16[8,4,32,128]{3,2,1,0:T(8,128)(2,1)}, u32[]{:S(2)}, u32[]{:S(2)}) async-start(bf16[8,4,32,128]{3,2,1,0:T(8,128)(2,1)} %to_lags.5), calls=%async_computation.3 | async-start | bytes 524288 | tf_op jit(solution)/shard_map/all_to_all | solution.py:241
  195.6 7.1 %collective-permute-start.10 = (bf16[8,4,32,128]{3,2,1,0:T(8,128)(2,1)}, bf16[8,4,32,128]{3,2,1,0:T(8,128)(2,1)S(1)}, u32[]{:S(2)}, u32[]{:S(2)}) collective-permute-start(bf16[8,4,32,128]{3,2,1,0:T(8,128)(2,1)} %copy-done.9), channel_id=1, source_target_pairs={{0,0},{24,8},{16,16},{40,24},{32,32},{56,40},{48,48},{72,56},{64,6... | collective-permute-start | bytes 786440 | tf_op jit(solution)/shard_map/ppermute | solution.py:276
  202.8 1.4 to_lags.7
  204.2 7.3 %all-to-all-start.7 = ((bf16[8,4,32,128]{3,2,1,0:T(8,128)(2,1)}), bf16[8,4,32,128]{3,2,1,0:T(8,128)(2,1)S(1)}, u32[]{:S(2)}, u32[]{:S(2)}) async-start(bf16[8,4,32,128]{3,2,1,0:T(8,128)(2,1)} %to_lags.7), calls=%async_computation.7 | async-start | bytes 524288 | tf_op jit(solution)/shard_map/all_to_all | solution.py:241
  211.4 1.1 broadcast_select_fusion
  212.5 1.9 collective-permute-start.9
  214.4 4.6 %all-to-all-done.7 = bf16[8,4,32,128]{3,2,1,0:T(8,128)(2,1)S(1)} async-done(((bf16[8,4,32,128]{3,2,1,0:T(8,128)(2,1)}), bf16[8,4,32,128]{3,2,1,0:T(8,128)(2,1)S(1)}, u32[]{:S(2)}, u32[]{:S(2)}) %all-to-all-start.7) | async-done | bytes 262176 | tf_op jit(solution)/shard_map/all_to_all | solution.py:241
  219.0 2.5 %collective-permute-start.11 = (bf16[8,4,32,128]{3,2,1,0:T(8,128)(2,1)S(1)}, bf16[8,4,32,128]{3,2,1,0:T(8,128)(2,1)S(1)}, u32[]{:S(2)}, u32[]{:S(2)}) collective-permute-start(bf16[8,4,32,128]{3,2,1,0:T(8,128)(2,1)S(1)} %all-to-all-done.7), channel_id=1, source_target_pairs={{0,0},{24,8},{16,16},{40,24},{32,32},{56,40},{48,48},{72,56},{64,6... | collective-permute-start | bytes 786440 | tf_op jit(solution)/shard_map/ppermute | solution.py:277
  221.6 4.5 %collective-permute-done.11.x1_ref = bf16[8,4,32,128]{3,2,1,0:T(8,128)(2,1)S(1)} collective-permute-done((bf16[8,4,32,128]{3,2,1,0:T(8,128)(2,1)S(1)}, bf16[8,4,32,128]{3,2,1,0:T(8,128)(2,1)S(1)}, u32[]{:S(2)}, u32[]{:S(2)}) %collective-permute-start.11) | collective-permute-done | bytes 262176 | tf_op jit(solution)/shard_map/ppermute | solution.py:277
  226.1 1.2 assemble.1
  (27 shorter events, 0.2 us)
Async XLA Ops:
  0.0 22.2 %copy-start.6 = (bf16[8,2,384,256]{3,2,1,0:T(8,128)(2,1)S(1)}, bf16[8,2,384,256]{3,2,1,0:T(8,128)(2,1)}, u32[]{:S(2)}) copy-start(bf16[8,2,384,256]{3,2,1,0:T(8,128)(2,1)} %s_ref.1) | copy-start | bytes 9437188
  0.0 59.8 %collective-permute-start = (bf16[8,2,384,256]{3,2,1,0:T(8,128)(2,1)}, bf16[8,2,384,256]{3,2,1,0:T(8,128)(2,1)}, u32[]{:S(2)}, u32[]{:S(2)}) collective-permute-start(bf16[8,2,384,256]{3,2,1,0:T(8,128)(2,1)} %s_ref.1), channel_id=1, source_target_pairs={{8,0},{0,8},{24,16},{16,24},{40,32},{32,40},{56,48},{48,56},{72,64... | collective-permute-start | bytes 9437192 | tf_op jit(solution)/shard_map/ppermute | solution.py:253
  11.6 8.4 %collective-permute-start.1 = (bf16[384,256]{1,0:T(8,128)(2,1)S(1)}, bf16[384,256]{1,0:T(8,128)(2,1)S(1)}, u32[]{:S(2)}, u32[]{:S(2)}) collective-permute-start(bf16[384,256]{1,0:T(8,128)(2,1)S(1)} %convert_element_type.29), channel_id=1, source_target_pairs={{0,1},{1,0},{2,3},{3,2},{4,5},{5,4},{6,7},{7,6},{8,9},{9,8},{10,11... | collective-permute-start | bytes 589832 | tf_op jit(solution)/shard_map/ppermute | solution.py:236
  20.1 33.7 %copy-start.8 = (s32[384,256]{1,0:T(8,128)S(1)}, s32[384,256]{1,0:T(8,128)}, u32[]{:S(2)}) copy-start(s32[384,256]{1,0:T(8,128)} %param.4) | copy-start | bytes 1179652
  20.1 8.9 %collective-permute-start.2 = (bf16[384,256]{1,0:T(8,128)(2,1)S(1)}, bf16[384,256]{1,0:T(8,128)(2,1)S(1)}, u32[]{:S(2)}, u32[]{:S(2)}) collective-permute-start(bf16[384,256]{1,0:T(8,128)(2,1)S(1)} %fusion), channel_id=1, source_target_pairs={{0,3},{1,2},{2,1},{3,0},{4,7},{5,6},{6,5},{7,4},{8,11},{9,10},{10,... | collective-permute-start | bytes 589832 | tf_op jit(solution)/shard_map/ppermute | solution.py:236
  24.7 60.0 %collective-permute-start.7 = (bf16[8,2,384,128]{3,2,1,0:T(8,128)(2,1)}, bf16[8,2,384,128]{3,2,1,0:T(8,128)(2,1)S(1)}, u32[]{:S(2)}, u32[]{:S(2)}) collective-permute-start(bf16[8,2,384,128]{3,2,1,0:T(8,128)(2,1)} %get-tuple-element.21), channel_id=1, source_target_pairs={{16,0},{504,8},{32,16},{8,24},{48,32},{24,40},{64,48},{40,56},{80,... | collective-permute-start | bytes 4718600 | tf_op jit(solution)/shard_map/ppermute | solution.py:252
  29.0 24.8 %collective-permute-start.3 = (bf16[384,256]{1,0:T(8,128)(2,1)S(1)}, bf16[384,256]{1,0:T(8,128)(2,1)S(1)}, u32[]{:S(2)}, u32[]{:S(2)}) collective-permute-start(bf16[384,256]{1,0:T(8,128)(2,1)S(1)} %fusion.1), channel_id=1, source_target_pairs={{0,4},{1,5},{2,6},{3,7},{4,0},{5,1},{6,2},{7,3},{8,12},{9,13},{10,... | collective-permute-start | bytes 589832 | tf_op jit(solution)/shard_map/ppermute | solution.py:236
  54.0 5.8 %collective-permute-start.4 = (bf16[384,256]{1,0:T(8,128)(2,1)S(1)}, bf16[384,256]{1,0:T(8,128)(2,1)S(1)}, u32[]{:S(2)}, u32[]{:S(2)}) collective-permute-start(bf16[384,256]{1,0:T(8,128)(2,1)S(1)} %get-tuple-element.19), channel_id=1, source_target_pairs={{8,0},{0,8},{24,16},{16,24},{40,32},{32,40},{56,48},{48,56},{72,64... | collective-permute-start | bytes 589832 | tf_op jit(solution)/shard_map/ppermute | solution.py:260
  68.1 1.7 copy-start.1
  69.8 1.0 copy-start.3
  70.8 37.3 %all-to-all-start = ((bf16[8,16,32,128]{3,2,1,0:T(8,128)(2,1)}), bf16[8,16,32,128]{3,2,1,0:T(8,128)(2,1)S(1)}, u32[]{:S(2)}, u32[]{:S(2)}) async-start(bf16[8,16,32,128]{3,2,1,0:T(8,128)(2,1)} %copy-done.3), calls=%async_computation | async-start | bytes 2097152 | tf_op jit(solution)/shard_map/all_to_all | solution.py:241
  74.3 10.4 %collective-permute-start.6 = (bf16[384,256]{1,0:T(8,128)(2,1)S(1)}, bf16[384,256]{1,0:T(8,128)(2,1)S(1)}, u32[]{:S(2)}, u32[]{:S(2)}) collective-permute-start(bf16[384,256]{1,0:T(8,128)(2,1)S(1)} %get-tuple-element.19), channel_id=1, source_target_pairs={{16,0},{504,8},{32,16},{8,24},{48,32},{24,40},{64,48},{40,56},{80,... | collective-permute-start | bytes 589832 | tf_op jit(solution)/shard_map/ppermute | solution.py:261
  76.2 67.2 %collective-permute-start.5 = (bf16[8,2,384,128]{3,2,1,0:T(8,128)(2,1)}, bf16[8,2,384,128]{3,2,1,0:T(8,128)(2,1)}, u32[]{:S(2)}, u32[]{:S(2)}) collective-permute-start(bf16[8,2,384,128]{3,2,1,0:T(8,128)(2,1)} %get-tuple-element.22), channel_id=1, source_target_pairs={{16,0},{504,8},{32,16},{8,24},{48,32},{24,40},{64,48},{40,56},{80,... | collective-permute-start | bytes 4718600 | tf_op jit(solution)/shard_map/ppermute | solution.py:254
  91.8 1.0 copy-start.4
  92.8 19.5 %copy-start = (bf16[512,2048]{1,0:T(8,128)(2,1)S(1)}, bf16[512,2048]{1,0:T(8,128)(2,1)}, u32[]{:S(2)}) copy-start(bf16[512,2048]{1,0:T(8,128)(2,1)} %constant.29.clone.matrix_ref) | copy-start | bytes 6291460
  92.8 50.7 %collective-permute-start.8 = (bf16[8,2,384,128]{3,2,1,0:T(8,128)(2,1)}, bf16[8,2,384,128]{3,2,1,0:T(8,128)(2,1)}, u32[]{:S(2)}, u32[]{:S(2)}) collective-permute-start(bf16[8,2,384,128]{3,2,1,0:T(8,128)(2,1)} %get-tuple-element.15), channel_id=1, source_target_pairs={{8,0},{0,8},{24,16},{16,24},{40,32},{32,40},{56,48},{48,56},{72,64... | collective-permute-start | bytes 4718600 | tf_op jit(solution)/shard_map/ppermute | solution.py:269
  108.0 18.0 %all-to-all-start.4 = ((bf16[8,16,32,128]{3,2,1,0:T(8,128)(2,1)}), bf16[8,16,32,128]{3,2,1,0:T(8,128)(2,1)}, u32[]{:S(2)}, u32[]{:S(2)}) async-start(bf16[8,16,32,128]{3,2,1,0:T(8,128)(2,1)} %copy-done.4), calls=%async_computation.4 | async-start | bytes 2097152 | tf_op jit(solution)/shard_map/all_to_all | solution.py:241
  126.0 13.9 %all-to-all-start.1 = ((bf16[8,4,32,128]{3,2,1,0:T(8,128)(2,1)}), bf16[8,4,32,128]{3,2,1,0:T(8,128)(2,1)S(1)}, u32[]{:S(2)}, u32[]{:S(2)}) async-start(bf16[8,4,32,128]{3,2,1,0:T(8,128)(2,1)} %to_lags.4), calls=%async_computation.1 | async-start | bytes 524288 | tf_op jit(solution)/shard_map/all_to_all | solution.py:241
  140.0 3.5 %copy-start.7 = (bf16[8,4,32,128]{3,2,1,0:T(8,128)(2,1)}, bf16[8,4,32,128]{3,2,1,0:T(8,128)(2,1)S(1)}, u32[]{:S(2)}) copy-start(bf16[8,4,32,128]{3,2,1,0:T(8,128)(2,1)S(1)} %all-to-all-done.1) | copy-start | bytes 786436
  140.0 12.3 %all-to-all-start.5 = ((bf16[8,4,32,128]{3,2,1,0:T(8,128)(2,1)}), bf16[8,4,32,128]{3,2,1,0:T(8,128)(2,1)S(1)}, u32[]{:S(2)}, u32[]{:S(2)}) async-start(bf16[8,4,32,128]{3,2,1,0:T(8,128)(2,1)} %to_lags.6), calls=%async_computation.5 | async-start | bytes 524288 | tf_op jit(solution)/shard_map/all_to_all | solution.py:241
  151.3 1.0 copy-start.5
  152.3 20.6 %copy-start.9 = (bf16[8,4,32,128]{3,2,1,0:T(8,128)(2,1)}, bf16[8,4,32,128]{3,2,1,0:T(8,128)(2,1)S(1)}, u32[]{:S(2)}) copy-start(bf16[8,4,32,128]{3,2,1,0:T(8,128)(2,1)S(1)} %all-to-all-done.5) | copy-start | bytes 786436
  172.9 14.6 %all-to-all-start.6 = ((bf16[8,16,32,128]{3,2,1,0:T(8,128)(2,1)}), bf16[8,16,32,128]{3,2,1,0:T(8,128)(2,1)S(1)}, u32[]{:S(2)}, u32[]{:S(2)}) async-start(bf16[8,16,32,128]{3,2,1,0:T(8,128)(2,1)} %copy-done.5), calls=%async_computation.6 | async-start | bytes 2097152 | tf_op jit(solution)/shard_map/all_to_all | solution.py:241
  176.4 1.2 copy-start.2
  187.4 16.8 %all-to-all-start.3 = ((bf16[8,4,32,128]{3,2,1,0:T(8,128)(2,1)}), bf16[8,4,32,128]{3,2,1,0:T(8,128)(2,1)}, u32[]{:S(2)}, u32[]{:S(2)}) async-start(bf16[8,4,32,128]{3,2,1,0:T(8,128)(2,1)} %to_lags.5), calls=%async_computation.3 | async-start | bytes 524288 | tf_op jit(solution)/shard_map/all_to_all | solution.py:241
  195.6 25.9 %collective-permute-start.10 = (bf16[8,4,32,128]{3,2,1,0:T(8,128)(2,1)}, bf16[8,4,32,128]{3,2,1,0:T(8,128)(2,1)S(1)}, u32[]{:S(2)}, u32[]{:S(2)}) collective-permute-start(bf16[8,4,32,128]{3,2,1,0:T(8,128)(2,1)} %copy-done.9), channel_id=1, source_target_pairs={{0,0},{24,8},{16,16},{40,24},{32,32},{56,40},{48,48},{72,56},{64,6... | collective-permute-start | bytes 786440 | tf_op jit(solution)/shard_map/ppermute | solution.py:276
  204.2 14.8 %all-to-all-start.7 = ((bf16[8,4,32,128]{3,2,1,0:T(8,128)(2,1)}), bf16[8,4,32,128]{3,2,1,0:T(8,128)(2,1)S(1)}, u32[]{:S(2)}, u32[]{:S(2)}) async-start(bf16[8,4,32,128]{3,2,1,0:T(8,128)(2,1)} %to_lags.7), calls=%async_computation.7 | async-start | bytes 524288 | tf_op jit(solution)/shard_map/all_to_all | solution.py:241
  212.5 9.1 %collective-permute-start.9 = (bf16[8,4,32,128]{3,2,1,0:T(8,128)(2,1)S(1)}, bf16[8,4,32,128]{3,2,1,0:T(8,128)(2,1)S(1)}, u32[]{:S(2)}, u32[]{:S(2)}) collective-permute-start(bf16[8,4,32,128]{3,2,1,0:T(8,128)(2,1)S(1)} %get-tuple-element.23), channel_id=1, source_target_pairs={{8,0},{0,8},{24,16},{16,24},{40,32},{32,40},{56,48},{48,56},{72,64... | collective-permute-start | bytes 786440 | tf_op jit(solution)/shard_map/ppermute | solution.py:280
  219.0 7.1 %collective-permute-start.11 = (bf16[8,4,32,128]{3,2,1,0:T(8,128)(2,1)S(1)}, bf16[8,4,32,128]{3,2,1,0:T(8,128)(2,1)S(1)}, u32[]{:S(2)}, u32[]{:S(2)}) collective-permute-start(bf16[8,4,32,128]{3,2,1,0:T(8,128)(2,1)S(1)} %all-to-all-done.7), channel_id=1, source_target_pairs={{0,0},{24,8},{16,16},{40,24},{32,32},{56,40},{48,48},{72,56},{64,6... | collective-permute-start | bytes 786440 | tf_op jit(solution)/shard_map/ppermute | solution.py:277

commit v2 on v0

v2 whole, which is shorter than its diff:
```python
import functools
import math

import jax
import jax.numpy as jnp
import numpy as np
from jax import lax
from jax.experimental import pallas as pl
from jax.experimental.pallas import tpu as pltpu
from jax.sharding import PartitionSpec as P

FREQS = 64
KEEP = 32
WIN = 384
EPSILON = 1e-06
BLOCK = 256
SUB = 16
VMEM_LIMIT = 28 * 1024 * 1024

BF16 = jnp.bfloat16
F32 = jnp.float32


def params():
    return pltpu.CompilerParams(vmem_limit_bytes=VMEM_LIMIT)


def lag_matrix(first, bins):
    lag_index = np.arange(KEEP, dtype=np.float32) - np.float32(KEEP // 2)
    bin_index = np.arange(FREQS, dtype=np.float32) + np.float32(1.0)
    step = np.float32(2.0 * math.pi / (2 * FREQS))
    phase = (step * lag_index)[:, None] * bin_index[None, :]
    table = np.stack([np.cos(phase), -np.sin(phase)], axis=2).reshape(KEEP, 8, 8, 2)
    table = table[:, :, first : first + bins].reshape(KEEP, 16 * bins)
    return jnp.asarray(np.kron(table, np.eye(SUB, dtype=np.float32)), dtype=BF16)


def whiten(raw, factor):
    return raw * factor[None]


def product(left, right):
    windows = left.shape[1]
    rows = left.reshape(2 * windows, left.shape[2])
    top = jnp.concatenate([right[0], right[1]], axis=1)
    low = jnp.concatenate([right[1], -right[0]], axis=1)
    cols = jnp.concatenate([top, low], axis=0)
    return lax.dot_general(rows, cols, (((0,), (0,)), ((), ())), preferred_element_type=F32)


def store(out_ref, result, start):
    for part in range(2):
        piece = result[:, part * BLOCK : (part + 1) * BLOCK]
        out_ref[:, part, :, start : start + BLOCK] = piece.astype(BF16).reshape(8, 32, BLOCK)


def cross_kernel(odd_ref, s_ref, n_ref, u_ref, fs_ref, fn_ref, fu_ref, out_ref):
    own = whiten(s_ref[0], fs_ref[...])
    near = whiten(n_ref[0], fn_ref[...])
    far = whiten(u_ref[0], fu_ref[...])

    @pl.when(odd_ref[0] == 0)
    def _():
        store(out_ref, product(near, far), 0)
        store(out_ref, product(own, far), BLOCK)

    @pl.when(odd_ref[0] != 0)
    def _():
        store(out_ref, product(near, own), 0)
        store(out_ref, product(far, own), BLOCK)


def flag_spec():
    return pl.BlockSpec(memory_space=pltpu.SMEM)


def held_spec():
    return pl.BlockSpec(memory_space=pltpu.VMEM)


def cross_spectra(first, odd, s, n, u, fs, fn, fu):
    bins = u.shape[0]
    factor = pl.BlockSpec((WIN, BLOCK), lambda f: (0, 0))
    shifted = pl.BlockSpec((1, 2, WIN, BLOCK), lambda f: (first + f, 0, 0, 0))
    plain = pl.BlockSpec((1, 2, WIN, BLOCK), lambda f: (f, 0, 0, 0))
    return pl.pallas_call(
        cross_kernel,
        grid=(bins,),
        in_specs=[flag_spec(), shifted, shifted, plain, factor, factor, factor],
        out_specs=pl.BlockSpec((8, 2, 32, 2 * BLOCK), lambda f: (0, f, 0, 0)),
        out_shape=pltpu.HBM((8, 2 * bins, 32, 2 * BLOCK), BF16),
        compiler_params=params(),
        cost_estimate=pl.CostEstimate(
            flops=bins * 2 * 2 * 768 * 256 * 512, bytes_accessed=bins * 5 << 18, transcendentals=0
        ),
        name="cross" + str(first),
    )(odd, s, n, u, fs, fn, fu)


def lag_sums(matrix_ref, cross_ref):
    cross = cross_ref[...].reshape(-1, 32, BLOCK)
    pair = jnp.concatenate([cross[:, :SUB], cross[:, SUB:]], axis=2)
    return lax.dot_general(
        matrix_ref[...],
        pair.reshape(cross.shape[0] * SUB, 2 * BLOCK),
        (((1,), (0,)), ((), ())),
        preferred_element_type=F32,
    )


def lags_kernel(scale, matrix_ref, cross_ref, out_ref):
    lagged = (lag_sums(matrix_ref, cross_ref) * scale).astype(BF16)
    for half in range(2):
        piece = lagged[:, half * BLOCK : (half + 1) * BLOCK].reshape(8, 4, SUB, BLOCK)
        out_ref[:, 0, :, half * SUB : (half + 1) * SUB] = piece


def to_lags(cross):
    return pl.pallas_call(
        functools.partial(lags_kernel, 1.0 / math.sqrt(FREQS * WIN)),
        grid=(2,),
        in_specs=[
            pl.BlockSpec((512, 2048), lambda c: (0, 0)),
            pl.BlockSpec((8, 16, 32, BLOCK), lambda c: (0, 0, 0, c)),
        ],
        out_specs=pl.BlockSpec((8, 1, 4, 32, BLOCK), lambda c: (0, c, 0, 0, 0)),
        out_shape=pltpu.HBM((8, 2, 4, 32, BLOCK), BF16),
        compiler_params=params(),
        cost_estimate=pl.CostEstimate(
            flops=2 * 512 * 2048 * 1024, bytes_accessed=7 << 20, transcendentals=0
        ),
        name="to_lags",
    )(lag_matrix(0, 8), cross)


def assemble_kernel(one_ref, two_ref, out_ref):
    for src in range(8):
        rows = slice(src * 32, src * 32 + 32)
        out_ref[0, :, rows] = one_ref[src]
        out_ref[1, :, rows] = two_ref[src]


def assemble(one, two):
    return pl.pallas_call(
        assemble_kernel,
        in_specs=[held_spec()] * 2,
        out_specs=held_spec(),
        out_shape=jax.ShapeDtypeStruct((2, 4, BLOCK, BLOCK), BF16),
        compiler_params=params(),
        cost_estimate=pl.CostEstimate(flops=0, bytes_accessed=2 << 20, transcendentals=0),
        name="assemble",
    )(one, two)


def exchange(value, partner):
    route = [(b, partner(b)) for b in range(8)]
    return lax.ppermute(value, "band", route)


def regroup(block):
    return lax.all_to_all(block, "band", split_axis=0, concat_axis=0, tiled=True)


def shards(spectra, window_valid):
    blocks = lax.axis_size("pair")
    flag = (lax.axis_index("pair") % 2).astype(jnp.int32).reshape(1)
    across = [((p + 2) % blocks, p) if p % 2 == 0 else ((p - 2) % blocks, p) for p in range(blocks)]
    swap = [(p ^ 1, p) for p in range(blocks)]
    back = [(p, p) if p % 2 == 0 else ((p + 2) % blocks, p) for p in range(blocks)]
    other = [((p + 3) % blocks, p) if p % 2 == 0 else ((p - 3) % blocks, p) for p in range(blocks)]
    barrier = lax.optimization_barrier

    values = spectra.astype(F32)
    energy = jnp.sum(values * values, axis=(0, 1))
    met, moved = barrier((exchange(energy.astype(BF16), lambda b: (b + 4) % 8), spectra))
    u = lax.ppermute(moved, "pair", across)
    energy = energy + met.astype(F32)
    energy = energy + exchange(energy.astype(BF16), lambda b: b ^ 1).astype(F32)
    energy, moved = barrier((energy, moved))
    n = lax.ppermute(moved, "pair", swap)
    energy = energy + exchange(energy.astype(BF16), lambda b: (b // 4) * 4 + 3 - b % 4).astype(F32)
    fs = (window_valid.astype(F32) * lax.rsqrt(energy / FREQS + EPSILON)).astype(BF16)
    fn = lax.ppermute(fs, "pair", swap)
    fu = lax.ppermute(fn, "pair", other)

    cross = cross_spectra(0, flag, spectra, n, u, fs, fn, fu)
    own = regroup(to_lags(regroup(cross)))
    return assemble(lax.ppermute(own[:, 0], "pair", swap), lax.ppermute(own[:, 1], "pair", back))


def solution(mesh):
    return jax.shard_map(
        shards,
        mesh=mesh,
        in_specs=(P("band", None, None, "pair"), P(None, "pair")),
        out_specs=P(None, "band", "pair", None),
        check_vma=False,
    )
```

time: 312 us -> 160 us (0.51)
  the two profiles are of different devices: /device:TPU:480 before, /device:TPU:1 now
where the time goes in v2:
time: 160 us; the launch traced here: 159 us
  blocking collectives  70 us (44%)
  starting transfers between devices  45 us (28%)
  waiting for transfers between devices  26.7 us (17%)
  Pallas kernels  14.3 us (9%)
  other arithmetic  2.95 us (2%)
    all_to_all x2, blocking collectives, regroup(): lax.all_to_all(block, 'band', split_axis=0, concat_axis=0, tiled=True)  70 us
    ppermute x3, starting transfers between devices, exchange(): return lax.ppermute(value, 'band', route)  14 us
    ppermute x1, starting transfers between devices, shards(): n = lax.ppermute(moved, 'pair', swap)  12.5 us
    pallas_call x1, Pallas kernels, cross_spectra(): pl.pallas_call(cross_kernel, grid=(bins,), in_specs=[flag_spec(), shifted...  9.7 us
    ppermute x3, waiting for transfers between devices, exchange(): return lax.ppermute(value, 'band', route)  8.86 us
    ppermute x1, waiting for transfers between devices, shards(): u = lax.ppermute(moved, 'pair', across)  7.87 us
    ppermute x1, waiting for transfers between devices, shards(): fu = lax.ppermute(fn, 'pair', other)  7.17 us
    ppermute x1, starting transfers between devices, shards(): lax.ppermute(own[:, 0], 'pair', swap)  6.22 us
  transfers between devices with their start and end apart: 9, of which 6 were waited for; matrix products, arithmetic and copies ran while one was open for 0% of the time, Pallas kernels for 0%

profile of v2, /device:TPU:1, one launch (start us, length us, event | category | flops | bytes accessed | tf_op | source)
XLA Modules:
  0.0 159.3 jit_solution(8225595764481398528)
XLA Ops:
  0.0 0.0 copy-start
  0.0 0.0 copy-start.2
  0.0 2.7 %multiply_reduce_fusion = f32[384,256]{1,0:T(8,128)S(1)} fusion(bf16[8,2,384,256]{3,2,1,0:T(8,128)(2,1)} %s_ref.1), kind=kLoop, calls=%fused_computation | loop fusion | flops 4620288 | bytes 3538944 | tf_op jit(solution)/shard_map/reduce_sum | solution.py:174
  2.7 5.5 %collective-permute-start = (bf16[384,256]{1,0:T(8,128)(2,1)S(1)}, bf16[384,256]{1,0:T(8,128)(2,1)S(1)}, u32[]{:S(2)}, u32[]{:S(2)}) collective-permute-start(bf16[384,256]{1,0:T(8,128)(2,1)S(1)} %convert_element_type.28), channel_id=1, source_target_pairs={{0,4},{1,5},{2,6},{3,7},{4,0},{5,1},{6,2},{7,3},{8,12},{9,13},{10,... | collective-permute-start | bytes 589832 | tf_op jit(solution)/shard_map/ppermute | solution.py:157
  8.2 3.0 %collective-permute-done = bf16[384,256]{1,0:T(8,128)(2,1)S(1)} collective-permute-done((bf16[384,256]{1,0:T(8,128)(2,1)S(1)}, bf16[384,256]{1,0:T(8,128)(2,1)S(1)}, u32[]{:S(2)}, u32[]{:S(2)}) %collective-permute-start) | collective-permute-done | bytes 196640 | tf_op jit(solution)/shard_map/ppermute | solution.py:157
  11.3 4.7 %collective-permute-start.1 = (bf16[384,256]{1,0:T(8,128)(2,1)S(1)}, bf16[384,256]{1,0:T(8,128)(2,1)S(1)}, u32[]{:S(2)}, u32[]{:S(2)}) collective-permute-start(bf16[384,256]{1,0:T(8,128)(2,1)S(1)} %fusion), channel_id=1, source_target_pairs={{0,1},{1,0},{2,3},{3,2},{4,5},{5,4},{6,7},{7,6},{8,9},{9,8},{10,11... | collective-permute-start | bytes 589832 | tf_op jit(solution)/shard_map/ppermute | solution.py:157
  16.0 0.0 copy-done
  16.0 3.5 %collective-permute-start.3 = (bf16[8,2,384,256]{3,2,1,0:T(8,128)(2,1)S(1)}, bf16[8,2,384,256]{3,2,1,0:T(8,128)(2,1)}, u32[]{:S(2)}, u32[]{:S(2)}) collective-permute-start(bf16[8,2,384,256]{3,2,1,0:T(8,128)(2,1)S(1)} %copy-done), channel_id=1, source_target_pairs={{16,0},{504,8},{32,16},{8,24},{48,32},{24,40},{64,48},{40,56},{80,... | collective-permute-start | bytes 9437192 | tf_op jit(solution)/shard_map/ppermute | solution.py:176
  19.6 0.0 collective-permute-done.1
  19.6 0.1 convert_add_fusion
  19.6 12.5 %collective-permute-start.2 = (bf16[8,2,384,256]{3,2,1,0:T(8,128)(2,1)S(1)}, bf16[8,2,384,256]{3,2,1,0:T(8,128)(2,1)}, u32[]{:S(2)}, u32[]{:S(2)}) collective-permute-start(bf16[8,2,384,256]{3,2,1,0:T(8,128)(2,1)S(1)} %copy-done), channel_id=1, source_target_pairs={{8,0},{0,8},{24,16},{16,24},{40,32},{32,40},{56,48},{48,56},{72,64... | collective-permute-start | bytes 9437192 | tf_op jit(solution)/shard_map/ppermute | solution.py:180
  32.2 3.8 %collective-permute-start.4 = (bf16[384,256]{1,0:T(8,128)(2,1)S(1)}, bf16[384,256]{1,0:T(8,128)(2,1)S(1)}, u32[]{:S(2)}, u32[]{:S(2)}) collective-permute-start(bf16[384,256]{1,0:T(8,128)(2,1)S(1)} %convert_element_type.33), channel_id=1, source_target_pairs={{0,3},{1,2},{2,1},{3,0},{4,7},{5,6},{6,5},{7,4},{8,11},{9,10},{10,... | collective-permute-start | bytes 589832 | tf_op jit(solution)/shard_map/ppermute | solution.py:157
  36.0 5.8 %collective-permute-done.4 = bf16[384,256]{1,0:T(8,128)(2,1)S(1)} collective-permute-done((bf16[384,256]{1,0:T(8,128)(2,1)S(1)}, bf16[384,256]{1,0:T(8,128)(2,1)S(1)}, u32[]{:S(2)}, u32[]{:S(2)}) %collective-permute-start.4) | collective-permute-done | bytes 196640 | tf_op jit(solution)/shard_map/ppermute | solution.py:157
  41.8 0.0 copy-done.2
  41.8 0.1 multiply_convert_fusion.fs_ref
  41.9 2.7 %collective-permute-start.5 = (bf16[384,256]{1,0:T(8,128)(2,1)S(1)}, bf16[384,256]{1,0:T(8,128)(2,1)S(1)}, u32[]{:S(2)}, u32[]{:S(2)}) collective-permute-start(bf16[384,256]{1,0:T(8,128)(2,1)S(1)} %multiply_convert_fusion.fs_ref), channel_id=1, source_target_pairs={{8,0},{0,8},{24,16},{16,24},{40,32},{32,40},{56,48},{48,56},{72,64... | collective-permute-start | bytes 589832 | tf_op jit(solution)/shard_map/ppermute | solution.py:183
  44.6 1.0 collective-permute-done.5.fn_ref
  45.7 4.2 %collective-permute-start.6 = (bf16[384,256]{1,0:T(8,128)(2,1)S(1)}, bf16[384,256]{1,0:T(8,128)(2,1)}, u32[]{:S(2)}, u32[]{:S(2)}) collective-permute-start(bf16[384,256]{1,0:T(8,128)(2,1)S(1)} %collective-permute-done.5.fn_ref), channel_id=1, source_target_pairs={{24,0},{496,8},{40,16},{0,24},{56,32},{16,40},{72,48},{32,56},{88,... | collective-permute-start | bytes 589832 | tf_op jit(solution)/shard_map/ppermute | solution.py:184
  49.9 7.2 %collective-permute-done.6.fu_ref = bf16[384,256]{1,0:T(8,128)(2,1)} collective-permute-done((bf16[384,256]{1,0:T(8,128)(2,1)S(1)}, bf16[384,256]{1,0:T(8,128)(2,1)}, u32[]{:S(2)}, u32[]{:S(2)}) %collective-permute-start.6) | collective-permute-done | bytes 196640 | tf_op jit(solution)/shard_map/ppermute | solution.py:184
  57.0 7.9 %collective-permute-done.3.u_ref = bf16[8,2,384,256]{3,2,1,0:T(8,128)(2,1)} collective-permute-done((bf16[8,2,384,256]{3,2,1,0:T(8,128)(2,1)S(1)}, bf16[8,2,384,256]{3,2,1,0:T(8,128)(2,1)}, u32[]{:S(2)}, u32[]{:S(2)}) %collective-permute-start.3) | collective-permute-done | bytes 3145760 | tf_op jit(solution)/shard_map/ppermute | solution.py:176
  64.9 0.0 collective-permute-done.2.n_ref
  64.9 9.7 %cross0.1 = bf16[8,16,32,512]{3,2,1,0:T(8,128)(2,1)} custom-call(s32[1]{0:T(128)} %bitcast.odd_ref, bf16[8,2,384,256]{3,2,1,0:T(8,128)(2,1)S(1)} %copy-done, bf16[8,2,384,256]{3,2,1,0:T(8,128)(2,1)} %collective-permute-done.2.n_ref, bf16[8,2,384,256]{3,2,1,0:T(8,128)(2,1)} %collective-permute-done.3.u_ref, bf16[384,256]{1,0:T(8,128)(2,1)S(1)} %multiply_convert_fusion.fs_ref, ...), custom_call_target="tpu_custom_call" | custom-call | flops 3221225472 | bytes 10485760 | tf_op jit(solution)/shard_map/cross0/pallas_call | solution.py:86
  74.6 0.0 copy-start.1
  74.6 54.0 %all_to_all.10.cross_ref = bf16[8,16,32,512]{3,2,1,0:T(8,128)(2,1)S(1)} all-to-all(bf16[8,16,32,512]{3,2,1,0:T(8,128)(2,1)} %cross0.1), channel_id=1, replica_groups=mesh['pair'=64,'band'=8] {'band'}, dimensions={0} | all-to-all | bytes 8388608 | tf_op jit(solution)/shard_map/all_to_all | solution.py:161
  128.6 0.0 copy-done.1
  128.6 3.6 %to_lags.1 = bf16[8,2,4,32,256]{4,3,2,1,0:T(8,128)(2,1)} custom-call(bf16[512,2048]{1,0:T(8,128)(2,1)S(1)} %copy-done.1, bf16[8,16,32,512]{3,2,1,0:T(8,128)(2,1)S(1)} %all_to_all.10.cross_ref), custom_call_target="tpu_custom_call" | custom-call | flops 2147483648 | bytes 7340032 | tf_op jit(solution)/shard_map/to_lags/pallas_call | solution.py:119
  132.2 16.0 %all_to_all.11 = bf16[8,2,4,32,256]{4,3,2,1,0:T(8,128)(2,1)S(1)} all-to-all(bf16[8,2,4,32,256]{4,3,2,1,0:T(8,128)(2,1)} %to_lags.1), channel_id=1, replica_groups=mesh['pair'=64,'band'=8] {'band'}, dimensions={0} | all-to-all | bytes 2097152 | tf_op jit(solution)/shard_map/all_to_all | solution.py:161
  148.3 0.1 slice_bitcast_fusion
  148.4 1.9 %collective-permute-start.8 = (bf16[8,4,32,256]{3,2,1,0:T(8,128)(2,1)S(1)}, bf16[8,4,32,256]{3,2,1,0:T(8,128)(2,1)S(1)}, u32[]{:S(2)}, u32[]{:S(2)}) collective-permute-start(bf16[8,4,32,256]{3,2,1,0:T(8,128)(2,1)S(1)} %get-tuple-element.13), channel_id=1, source_target_pairs={{0,0},{24,8},{16,16},{40,24},{32,32},{56,40},{48,48},{72,56},{64,6... | collective-permute-start | bytes 1572872 | tf_op jit(solution)/shard_map/ppermute | solution.py:188
  150.3 6.2 %collective-permute-start.7 = (bf16[8,4,32,256]{3,2,1,0:T(8,128)(2,1)S(1)}, bf16[8,4,32,256]{3,2,1,0:T(8,128)(2,1)S(1)}, u32[]{:S(2)}, u32[]{:S(2)}) collective-permute-start(bf16[8,4,32,256]{3,2,1,0:T(8,128)(2,1)S(1)} %get-tuple-element.14), channel_id=1, source_target_pairs={{8,0},{0,8},{24,16},{16,24},{40,32},{32,40},{56,48},{48,56},{72,64... | collective-permute-start | bytes 1572872 | tf_op jit(solution)/shard_map/ppermute | solution.py:188
  156.5 1.8 %collective-permute-done.8.two_ref = bf16[8,4,32,256]{3,2,1,0:T(8,128)(2,1)S(1)} collective-permute-done((bf16[8,4,32,256]{3,2,1,0:T(8,128)(2,1)S(1)}, bf16[8,4,32,256]{3,2,1,0:T(8,128)(2,1)S(1)}, u32[]{:S(2)}, u32[]{:S(2)}) %collective-permute-start.8) | collective-permute-done | bytes 524320 | tf_op jit(solution)/shard_map/ppermute | solution.py:188
  158.3 0.0 collective-permute-done.7.one_ref
  158.3 1.0 assemble.1
  (3 shorter events, 0.1 us)
Async XLA Ops:
  0.0 16.0 %copy-start = (bf16[8,2,384,256]{3,2,1,0:T(8,128)(2,1)S(1)}, bf16[8,2,384,256]{3,2,1,0:T(8,128)(2,1)}, u32[]{:S(2)}) copy-start(bf16[8,2,384,256]{3,2,1,0:T(8,128)(2,1)} %s_ref.1) | copy-start | bytes 9437188
  0.0 41.8 %copy-start.2 = (s32[384,256]{1,0:T(8,128)S(1)}, s32[384,256]{1,0:T(8,128)}, u32[]{:S(2)}) copy-start(s32[384,256]{1,0:T(8,128)} %param.4) | copy-start | bytes 1179652
  2.7 8.5 %collective-permute-start = (bf16[384,256]{1,0:T(8,128)(2,1)S(1)}, bf16[384,256]{1,0:T(8,128)(2,1)S(1)}, u32[]{:S(2)}, u32[]{:S(2)}) collective-permute-start(bf16[384,256]{1,0:T(8,128)(2,1)S(1)} %convert_element_type.28), channel_id=1, source_target_pairs={{0,4},{1,5},{2,6},{3,7},{4,0},{5,1},{6,2},{7,3},{8,12},{9,13},{10,... | collective-permute-start | bytes 589832 | tf_op jit(solution)/shard_map/ppermute | solution.py:157
  11.3 8.2 %collective-permute-start.1 = (bf16[384,256]{1,0:T(8,128)(2,1)S(1)}, bf16[384,256]{1,0:T(8,128)(2,1)S(1)}, u32[]{:S(2)}, u32[]{:S(2)}) collective-permute-start(bf16[384,256]{1,0:T(8,128)(2,1)S(1)} %fusion), channel_id=1, source_target_pairs={{0,1},{1,0},{2,3},{3,2},{4,5},{5,4},{6,7},{7,6},{8,9},{9,8},{10,11... | collective-permute-start | bytes 589832 | tf_op jit(solution)/shard_map/ppermute | solution.py:157
  16.0 48.9 %collective-permute-start.3 = (bf16[8,2,384,256]{3,2,1,0:T(8,128)(2,1)S(1)}, bf16[8,2,384,256]{3,2,1,0:T(8,128)(2,1)}, u32[]{:S(2)}, u32[]{:S(2)}) collective-permute-start(bf16[8,2,384,256]{3,2,1,0:T(8,128)(2,1)S(1)} %copy-done), channel_id=1, source_target_pairs={{16,0},{504,8},{32,16},{8,24},{48,32},{24,40},{64,48},{40,56},{80,... | collective-permute-start | bytes 9437192 | tf_op jit(solution)/shard_map/ppermute | solution.py:176
  19.6 45.3 %collective-permute-start.2 = (bf16[8,2,384,256]{3,2,1,0:T(8,128)(2,1)S(1)}, bf16[8,2,384,256]{3,2,1,0:T(8,128)(2,1)}, u32[]{:S(2)}, u32[]{:S(2)}) collective-permute-start(bf16[8,2,384,256]{3,2,1,0:T(8,128)(2,1)S(1)} %copy-done), channel_id=1, source_target_pairs={{8,0},{0,8},{24,16},{16,24},{40,32},{32,40},{56,48},{48,56},{72,64... | collective-permute-start | bytes 9437192 | tf_op jit(solution)/shard_map/ppermute | solution.py:180
  32.2 9.6 %collective-permute-start.4 = (bf16[384,256]{1,0:T(8,128)(2,1)S(1)}, bf16[384,256]{1,0:T(8,128)(2,1)S(1)}, u32[]{:S(2)}, u32[]{:S(2)}) collective-permute-start(bf16[384,256]{1,0:T(8,128)(2,1)S(1)} %convert_element_type.33), channel_id=1, source_target_pairs={{0,3},{1,2},{2,1},{3,0},{4,7},{5,6},{6,5},{7,4},{8,11},{9,10},{10,... | collective-permute-start | bytes 589832 | tf_op jit(solution)/shard_map/ppermute | solution.py:157
  41.9 3.8 %collective-permute-start.5 = (bf16[384,256]{1,0:T(8,128)(2,1)S(1)}, bf16[384,256]{1,0:T(8,128)(2,1)S(1)}, u32[]{:S(2)}, u32[]{:S(2)}) collective-permute-start(bf16[384,256]{1,0:T(8,128)(2,1)S(1)} %multiply_convert_fusion.fs_ref), channel_id=1, source_target_pairs={{8,0},{0,8},{24,16},{16,24},{40,32},{32,40},{56,48},{48,56},{72,64... | collective-permute-start | bytes 589832 | tf_op jit(solution)/shard_map/ppermute | solution.py:183
  45.7 11.4 %collective-permute-start.6 = (bf16[384,256]{1,0:T(8,128)(2,1)S(1)}, bf16[384,256]{1,0:T(8,128)(2,1)}, u32[]{:S(2)}, u32[]{:S(2)}) collective-permute-start(bf16[384,256]{1,0:T(8,128)(2,1)S(1)} %collective-permute-done.5.fn_ref), channel_id=1, source_target_pairs={{24,0},{496,8},{40,16},{0,24},{56,32},{16,40},{72,48},{32,56},{88,... | collective-permute-start | bytes 589832 | tf_op jit(solution)/shard_map/ppermute | solution.py:184
  74.6 54.0 %copy-start.1 = (bf16[512,2048]{1,0:T(8,128)(2,1)S(1)}, bf16[512,2048]{1,0:T(8,128)(2,1)}, u32[]{:S(2)}) copy-start(bf16[512,2048]{1,0:T(8,128)(2,1)} %constant.28.clone.matrix_ref) | copy-start | bytes 6291460
  148.4 9.9 %collective-permute-start.8 = (bf16[8,4,32,256]{3,2,1,0:T(8,128)(2,1)S(1)}, bf16[8,4,32,256]{3,2,1,0:T(8,128)(2,1)S(1)}, u32[]{:S(2)}, u32[]{:S(2)}) collective-permute-start(bf16[8,4,32,256]{3,2,1,0:T(8,128)(2,1)S(1)} %get-tuple-element.13), channel_id=1, source_target_pairs={{0,0},{24,8},{16,16},{40,24},{32,32},{56,40},{48,48},{72,56},{64,6... | collective-permute-start | bytes 1572872 | tf_op jit(solution)/shard_map/ppermute | solution.py:188
  150.3 8.0 %collective-permute-start.7 = (bf16[8,4,32,256]{3,2,1,0:T(8,128)(2,1)S(1)}, bf16[8,4,32,256]{3,2,1,0:T(8,128)(2,1)S(1)}, u32[]{:S(2)}, u32[]{:S(2)}) collective-permute-start(bf16[8,4,32,256]{3,2,1,0:T(8,128)(2,1)S(1)} %get-tuple-element.14), channel_id=1, source_target_pairs={{8,0},{0,8},{24,16},{16,24},{40,32},{32,40},{56,48},{48,56},{72,64... | collective-permute-start | bytes 1572872 | tf_op jit(solution)/shard_map/ppermute | solution.py:188

commit v3 on v2

v3 whole, which is shorter than its diff:
```python
import functools
import math

import jax
import jax.numpy as jnp
import numpy as np
from jax import lax
from jax.experimental import pallas as pl
from jax.experimental.pallas import tpu as pltpu
from jax.sharding import PartitionSpec as P

FREQS = 64
KEEP = 32
WIN = 384
EPSILON = 1e-06
BLOCK = 256
SUB = 16
STEP = 2
VMEM_LIMIT = 28 * 1024 * 1024

BF16 = jnp.bfloat16
F32 = jnp.float32


def params():
    return pltpu.CompilerParams(vmem_limit_bytes=VMEM_LIMIT)


def lag_matrix(first, bins):
    lag_index = np.arange(KEEP, dtype=np.float32) - np.float32(KEEP // 2)
    bin_index = np.arange(FREQS, dtype=np.float32) + np.float32(1.0)
    step = np.float32(2.0 * math.pi / (2 * FREQS))
    phase = (step * lag_index)[:, None] * bin_index[None, :]
    table = np.stack([np.cos(phase), -np.sin(phase)], axis=2).reshape(KEEP, 8, 8, 2)
    table = table[:, :, first : first + bins].reshape(KEEP, 16 * bins)
    return jnp.asarray(np.kron(table, np.eye(SUB, dtype=np.float32)), dtype=BF16)


def whiten(raw, factor):
    if factor.dtype == BF16:
        return raw * factor[None]
    return (raw.astype(F32) * factor[None]).astype(BF16)


def product(left, right):
    windows = left.shape[1]
    rows = left.reshape(2 * windows, left.shape[2])
    top = jnp.concatenate([right[0], right[1]], axis=1)
    low = jnp.concatenate([right[1], -right[0]], axis=1)
    cols = jnp.concatenate([top, low], axis=0)
    return lax.dot_general(rows, cols, (((0,), (0,)), ((), ())), preferred_element_type=F32)


def store(out_ref, result):
    for part in range(2):
        piece = result[:, part * BLOCK : (part + 1) * BLOCK]
        out_ref[:, part] = piece.astype(BF16).reshape(8, 32, BLOCK)


def near_kernel(odd_ref, s_ref, n_ref, fs_ref, fn_ref, sw_ref, nw_ref, out_ref):
    for index in range(STEP):
        f = pl.program_id(0) * STEP + index
        sw_ref[f] = whiten(s_ref[f], fs_ref[...])
        nw_ref[f] = whiten(n_ref[index], fn_ref[...])

        @pl.when(odd_ref[0] != 0)
        def _():
            store(out_ref.at[:, 2 * index : 2 * index + 2], product(nw_ref[f], sw_ref[f]))


def far_kernel(first, odd_ref, own_ref, near_ref, u_ref, fu_ref, _, out_ref, held_ref, send_ref, in_sem, out_sem):
    bins = u_ref.shape[0]
    odd = odd_ref[0]

    def fetch(f):
        return pltpu.make_async_copy(u_ref.at[f], held_ref.at[f], in_sem.at[f])

    def put(f, part):
        rows, columns = pl.ds(2 * f, 2), pl.ds(part * BLOCK, BLOCK)
        return pltpu.make_async_copy(
            send_ref.at[:, rows, :, columns],
            out_ref.at[:, pl.ds(2 * (first + f), 2), :, columns],
            out_sem.at[part, f],
        )

    def made(f, part, left, right):
        store(send_ref.at[:, pl.ds(2 * f, 2), :, pl.ds(part * BLOCK, BLOCK)], product(left, right))
        put(f, part).start()

    for f in range(bins):
        fetch(f).start()

    def step(f, carry):
        fetch(f).wait()
        far = whiten(held_ref[f], fu_ref[...])
        own = own_ref[first + f]

        @pl.when(odd == 0)
        def _():
            made(f, 0, near_ref[first + f], far)
            made(f, 1, own, far)

        @pl.when(odd != 0)
        def _():
            made(f, 1, far, own)

        return carry

    lax.fori_loop(0, bins, step, 0)
    for f in range(bins):
        put(f, 1).wait()

    @pl.when(odd == 0)
    def _():
        for f in range(bins):
            put(f, 0).wait()


def flag_spec():
    return pl.BlockSpec(memory_space=pltpu.SMEM)


def held_spec():
    return pl.BlockSpec(memory_space=pltpu.VMEM)


SEND = (8, 16, 32, 2 * BLOCK)
SEND_BLOCK = (8, 2 * STEP, 32, BLOCK)
BINS_BLOCK = (STEP, 2, WIN, BLOCK)


def near_spectra(odd, s, n, fs, fn):
    shape = jax.ShapeDtypeStruct(s.shape, BF16)
    return pl.pallas_call(
        near_kernel,
        grid=(8 // STEP,),
        in_specs=[flag_spec(), held_spec(), pl.BlockSpec(BINS_BLOCK, lambda g: (g, 0, 0, 0)), held_spec(), held_spec()],
        out_specs=[held_spec(), held_spec(), pl.BlockSpec(SEND_BLOCK, lambda g: (0, g, 0, 0))],
        out_shape=[shape, shape, pltpu.HBM(SEND, BF16)],
        compiler_params=params(),
        cost_estimate=pl.CostEstimate(flops=0, bytes_accessed=0, transcendentals=0),
        name="near_spectra",
    )(odd, s, n, fs, fn)


def far_spectra(first, odd, own, near, u, fu, filled):
    bins = u.shape[0]
    anywhere = pl.BlockSpec(memory_space=pl.ANY)
    return pl.pallas_call(
        functools.partial(far_kernel, first),
        in_specs=[flag_spec(), held_spec(), held_spec(), anywhere, held_spec(), anywhere],
        out_specs=anywhere,
        out_shape=pltpu.HBM(SEND, BF16),
        scratch_shapes=[
            pltpu.VMEM((bins, 2, WIN, BLOCK), BF16),
            pltpu.VMEM((8, 2 * bins, 32, 2 * BLOCK), BF16),
            pltpu.SemaphoreType.DMA((bins,)),
            pltpu.SemaphoreType.DMA((2, bins)),
        ],
        input_output_aliases={5: 0},
        compiler_params=params(),
        cost_estimate=pl.CostEstimate(
            flops=bins * 2 * 2 * 768 * 256 * 512, bytes_accessed=bins << 20, transcendentals=0
        ),
        name="far" + str(first),
    )(odd, own, near, u, fu, filled)


def lags_kernel(scale, matrix_ref, cross_ref, out_ref):
    for part in range(2):
        columns = slice(part * BLOCK, (part + 1) * BLOCK)
        cross = cross_ref[:, :, :, columns].reshape(2 * FREQS, 32, BLOCK)
        pair = jnp.concatenate([cross[:, :SUB], cross[:, SUB:]], axis=2)
        lagged = lax.dot_general(
            matrix_ref[...],
            pair.reshape(2 * FREQS * SUB, 2 * BLOCK),
            (((1,), (0,)), ((), ())),
            preferred_element_type=F32,
        )
        lagged = (lagged * scale).astype(BF16)
        for half in range(2):
            piece = lagged[:, half * BLOCK : (half + 1) * BLOCK].reshape(8, 4, SUB, BLOCK)
            out_ref[:, part, :, half * SUB : (half + 1) * SUB] = piece


def to_lags(cross):
    return pl.pallas_call(
        functools.partial(lags_kernel, 1.0 / math.sqrt(FREQS * WIN)),
        in_specs=[held_spec()] * 2,
        out_specs=held_spec(),
        out_shape=jax.ShapeDtypeStruct((8, 2, 4, 32, BLOCK), BF16),
        compiler_params=params(),
        cost_estimate=pl.CostEstimate(
            flops=2 * 512 * 2048 * 1024, bytes_accessed=7 << 20, transcendentals=0
        ),
        name="to_lags",
    )(lag_matrix(0, 8), cross)


def assemble_kernel(one_ref, two_ref, out_ref):
    for src in range(8):
        rows = slice(src * 32, src * 32 + 32)
        out_ref[0, :, rows] = one_ref[src]
        out_ref[1, :, rows] = two_ref[src]


def assemble(one, two):
    return pl.pallas_call(
        assemble_kernel,
        in_specs=[held_spec()] * 2,
        out_specs=held_spec(),
        out_shape=jax.ShapeDtypeStruct((2, 4, BLOCK, BLOCK), BF16),
        compiler_params=params(),
        cost_estimate=pl.CostEstimate(flops=0, bytes_accessed=2 << 20, transcendentals=0),
        name="assemble",
    )(one, two)


def exchange(value, partner):
    route = [(b, partner(b)) for b in range(8)]
    return lax.ppermute(value, "band", route)


def regroup(block):
    return lax.all_to_all(block, "band", split_axis=0, concat_axis=0, tiled=True)


def shards(spectra, window_valid):
    blocks = lax.axis_size("pair")
    flag = (lax.axis_index("pair") % 2).astype(jnp.int32).reshape(1)
    across = [((p + 2) % blocks, p) if p % 2 == 0 else ((p - 2) % blocks, p) for p in range(blocks)]
    swap = [(p ^ 1, p) for p in range(blocks)]
    back = [(p, p) if p % 2 == 0 else ((p + 2) % blocks, p) for p in range(blocks)]
    other = [((p + 3) % blocks, p) if p % 2 == 0 else ((p - 3) % blocks, p) for p in range(blocks)]
    barrier = lax.optimization_barrier

    values = spectra.astype(F32)
    energy = jnp.sum(values * values, axis=(0, 1))
    met, whole = barrier((exchange(energy.astype(BF16), lambda b: (b + 4) % 8), spectra))
    n = lax.ppermute(whole, "pair", swap)
    u = lax.ppermute(whole, "pair", across)
    energy = energy + met.astype(F32)
    energy = energy + exchange(energy.astype(BF16), lambda b: b ^ 1).astype(F32)
    energy = energy + exchange(energy.astype(BF16), lambda b: (b // 4) * 4 + 3 - b % 4).astype(F32)
    fs = window_valid.astype(F32) * lax.rsqrt(energy / FREQS + EPSILON)
    fn = lax.ppermute(fs.astype(BF16), "pair", swap)
    fu = lax.ppermute(fn, "pair", other)

    sw, nw, cross = near_spectra(flag, spectra, n, fs, fn)
    cross = far_spectra(0, flag, sw, nw, u, fu, cross)
    own = regroup(to_lags(regroup(cross)))
    return assemble(lax.ppermute(own[:, 0], "pair", swap), lax.ppermute(own[:, 1], "pair", back))


def solution(mesh):
    return jax.shard_map(
        shards,
        mesh=mesh,
        in_specs=(P("band", None, None, "pair"), P(None, "pair")),
        out_specs=P(None, "band", "pair", None),
        check_vma=False,
    )
```

time: 160 us -> 156 us (0.975)
  starting transfers between devices: 45 us -> 41.7 us
  waiting for transfers between devices: 26.7 us -> 23.8 us
  Pallas kernels: 14.3 us -> 16.4 us
    ppermute x1, waiting for transfers between devices: 7.17 us -> 1.6 us  [shards(): fu = lax.ppermute(fn, 'pair', other)]
    ppermute x3, waiting for transfers between devices: 8.86 us -> 13.6 us  [exchange(): return lax.ppermute(value, 'band', route)]
    ppermute x3, starting transfers between devices: 14 us -> 9.32 us  [exchange(): return lax.ppermute(value, 'band', route)]
    pallas_call x1 -> x2, Pallas kernels: 9.7 us -> 13 us  [the longest x1 6.61 us: far_spectra(): pl.pallas_call(functools.partial(far_kernel, first), in_specs=[flag_spec(...]
    ppermute x3, waiting for transfers between devices: 8.92 us -> 6.42 us  [the longest x1 5.24 us: shards(): u = lax.ppermute(whole, 'pair', across)]
    ppermute x3, starting transfers between devices: 18.8 us -> 21.1 us  [the longest x1 9.83 us: shards(): fn = lax.ppermute(fs.astype(BF16), 'pair', swap)]
  transfers between devices with their start and end apart: 9 -> 9, of which waited for: 6 -> 7; matrix products, arithmetic and copies ran while one was open for 0% -> 0% of each run, Pallas kernels for 0% -> 4%
where the time goes in v3:
time: 156 us
  blocking collectives  70.4 us (45%)
  starting transfers between devices  41.7 us (27%)
  waiting for transfers between devices  23.8 us (15%)
  Pallas kernels  16.4 us (11%)
  other arithmetic  3.02 us (2%)
    all_to_all x2, blocking collectives, regroup(): lax.all_to_all(block, 'band', split_axis=0, concat_axis=0, tiled=True)  70.4 us
    ppermute x3, waiting for transfers between devices, exchange(): return lax.ppermute(value, 'band', route)  13.6 us
    ppermute x1, starting transfers between devices, shards(): fn = lax.ppermute(fs.astype(BF16), 'pair', swap)  9.83 us
    ppermute x3, starting transfers between devices, exchange(): return lax.ppermute(value, 'band', route)  9.32 us
    ppermute x1, starting transfers between devices, shards(): n = lax.ppermute(whole, 'pair', swap)  9.31 us
    pallas_call x1, Pallas kernels, far_spectra(): pl.pallas_call(functools.partial(far_kernel, first), in_specs=[flag_spec(...  6.61 us
    pallas_call x1, Pallas kernels, near_spectra(): pl.pallas_call(near_kernel, grid=(8 // STEP,), in_specs=[flag_spec(), hel...  6.42 us
    ppermute x1, starting transfers between devices, shards(): lax.ppermute(own[:, 0], 'pair', swap)  5.86 us
  transfers between devices with their start and end apart: 9, of which 7 were waited for; matrix products, arithmetic and copies ran while one was open for 0% of the time, Pallas kernels for 4%

profile of v3, /device:TPU:1, one launch (start us, length us, event | category | flops | bytes accessed | tf_op | source)
XLA Modules:
  0.0 155.6 jit_solution(8009676309004747814)
XLA Ops:
  0.0 0.0 copy-start
  0.0 0.0 copy-start.2
  0.0 2.7 %multiply_reduce_fusion = f32[384,256]{1,0:T(8,128)S(1)} fusion(bf16[8,2,384,256]{3,2,1,0:T(8,128)(2,1)} %s_ref.1), kind=kLoop, calls=%fused_computation | loop fusion | flops 4620288 | bytes 3538944 | tf_op jit(solution)/shard_map/reduce_sum | solution.py:238
  2.7 5.5 %collective-permute-start = (bf16[384,256]{1,0:T(8,128)(2,1)S(1)}, bf16[384,256]{1,0:T(8,128)(2,1)S(1)}, u32[]{:S(2)}, u32[]{:S(2)}) collective-permute-start(bf16[384,256]{1,0:T(8,128)(2,1)S(1)} %convert_element_type.28), channel_id=1, source_target_pairs={{0,4},{1,5},{2,6},{3,7},{4,0},{5,1},{6,2},{7,3},{8,12},{9,13},{10,... | collective-permute-start | bytes 589832 | tf_op jit(solution)/shard_map/ppermute | solution.py:221
  8.2 3.0 %collective-permute-done = bf16[384,256]{1,0:T(8,128)(2,1)S(1)} collective-permute-done((bf16[384,256]{1,0:T(8,128)(2,1)S(1)}, bf16[384,256]{1,0:T(8,128)(2,1)S(1)}, u32[]{:S(2)}, u32[]{:S(2)}) %collective-permute-start) | collective-permute-done | bytes 196640 | tf_op jit(solution)/shard_map/ppermute | solution.py:221
  11.3 0.0 copy-done
  11.3 9.3 %collective-permute-start.1 = (bf16[8,2,384,256]{3,2,1,0:T(8,128)(2,1)S(1)}, bf16[8,2,384,256]{3,2,1,0:T(8,128)(2,1)}, u32[]{:S(2)}, u32[]{:S(2)}) collective-permute-start(bf16[8,2,384,256]{3,2,1,0:T(8,128)(2,1)S(1)} %copy-done), channel_id=1, source_target_pairs={{8,0},{0,8},{24,16},{16,24},{40,32},{32,40},{56,48},{48,56},{72,64... | collective-permute-start | bytes 9437192 | tf_op jit(solution)/shard_map/ppermute | solution.py:240
  20.6 1.9 %collective-permute-start.5 = (bf16[8,2,384,256]{3,2,1,0:T(8,128)(2,1)S(1)}, bf16[8,2,384,256]{3,2,1,0:T(8,128)(2,1)}, u32[]{:S(2)}, u32[]{:S(2)}) collective-permute-start(bf16[8,2,384,256]{3,2,1,0:T(8,128)(2,1)S(1)} %copy-done), channel_id=1, source_target_pairs={{16,0},{504,8},{32,16},{8,24},{48,32},{24,40},{64,48},{40,56},{80,... | collective-permute-start | bytes 9437192 | tf_op jit(solution)/shard_map/ppermute | solution.py:241
  22.5 0.1 fusion
  22.6 1.9 %collective-permute-start.2 = (bf16[384,256]{1,0:T(8,128)(2,1)S(1)}, bf16[384,256]{1,0:T(8,128)(2,1)S(1)}, u32[]{:S(2)}, u32[]{:S(2)}) collective-permute-start(bf16[384,256]{1,0:T(8,128)(2,1)S(1)} %fusion), channel_id=1, source_target_pairs={{0,1},{1,0},{2,3},{3,2},{4,5},{5,4},{6,7},{7,6},{8,9},{9,8},{10,11... | collective-permute-start | bytes 589832 | tf_op jit(solution)/shard_map/ppermute | solution.py:221
  24.5 4.9 %collective-permute-done.2 = bf16[384,256]{1,0:T(8,128)(2,1)S(1)} collective-permute-done((bf16[384,256]{1,0:T(8,128)(2,1)S(1)}, bf16[384,256]{1,0:T(8,128)(2,1)S(1)}, u32[]{:S(2)}, u32[]{:S(2)}) %collective-permute-start.2) | collective-permute-done | bytes 196640 | tf_op jit(solution)/shard_map/ppermute | solution.py:221
  29.4 0.1 fusion.1
  29.5 1.9 %collective-permute-start.3 = (bf16[384,256]{1,0:T(8,128)(2,1)S(1)}, bf16[384,256]{1,0:T(8,128)(2,1)S(1)}, u32[]{:S(2)}, u32[]{:S(2)}) collective-permute-start(bf16[384,256]{1,0:T(8,128)(2,1)S(1)} %fusion.1), channel_id=1, source_target_pairs={{0,3},{1,2},{2,1},{3,0},{4,7},{5,6},{6,5},{7,4},{8,11},{9,10},{10,... | collective-permute-start | bytes 589832 | tf_op jit(solution)/shard_map/ppermute | solution.py:221
  31.4 5.7 %collective-permute-done.3 = bf16[384,256]{1,0:T(8,128)(2,1)S(1)} collective-permute-done((bf16[384,256]{1,0:T(8,128)(2,1)S(1)}, bf16[384,256]{1,0:T(8,128)(2,1)S(1)}, u32[]{:S(2)}, u32[]{:S(2)}) %collective-permute-start.3) | collective-permute-done | bytes 196640 | tf_op jit(solution)/shard_map/ppermute | solution.py:221
  37.1 0.0 copy-done.2
  37.1 0.2 fusion.2
  37.3 9.8 %collective-permute-start.4 = (bf16[384,256]{1,0:T(8,128)(2,1)S(1)}, bf16[384,256]{1,0:T(8,128)(2,1)}, u32[]{:S(2)}, u32[]{:S(2)}) collective-permute-start(bf16[384,256]{1,0:T(8,128)(2,1)S(1)} %get-tuple-element.15), channel_id=1, source_target_pairs={{8,0},{0,8},{24,16},{16,24},{40,32},{32,40},{56,48},{48,56},{72,64... | collective-permute-start | bytes 589832 | tf_op jit(solution)/shard_map/ppermute | solution.py:246
  47.1 1.2 collective-permute-done.4.fn_ref
  48.3 3.5 %collective-permute-start.6 = (bf16[384,256]{1,0:T(8,128)(2,1)}, bf16[384,256]{1,0:T(8,128)(2,1)}, u32[]{:S(2)}, u32[]{:S(2)}) collective-permute-start(bf16[384,256]{1,0:T(8,128)(2,1)} %collective-permute-done.4.fn_ref), channel_id=1, source_target_pairs={{24,0},{496,8},{40,16},{0,24},{56,32},{16,40},{72,48},{32,56},{88,... | collective-permute-start | bytes 589832 | tf_op jit(solution)/shard_map/ppermute | solution.py:247
  51.8 0.0 collective-permute-done.1.n_ref
  51.8 6.4 %near_spectra.1 = (bf16[8,2,384,256]{3,2,1,0:T(8,128)(2,1)S(1)}, bf16[8,2,384,256]{3,2,1,0:T(8,128)(2,1)S(1)}, bf16[8,16,32,512]{3,2,1,0:T(8,128)(2,1)}) custom-call(s32[1]{0:T(128)} %bitcast.odd_ref, bf16[8,2,384,256]{3,2,1,0:T(8,128)(2,1)S(1)} %copy-done, bf16[8,2,384,256]{3,2,1,0:T(8,128)(2,1)} %collective-permute-done.1.n_ref, ...), custom_call_target="tpu_custom_call" | custom-call | tf_op jit(solution)/shard_map/near_spectra/pallas_call | solution.py:134
  58.3 1.6 %collective-permute-done.6.fu_ref = bf16[384,256]{1,0:T(8,128)(2,1)} collective-permute-done((bf16[384,256]{1,0:T(8,128)(2,1)}, bf16[384,256]{1,0:T(8,128)(2,1)}, u32[]{:S(2)}, u32[]{:S(2)}) %collective-permute-start.6) | collective-permute-done | bytes 196640 | tf_op jit(solution)/shard_map/ppermute | solution.py:247
  59.9 5.2 %collective-permute-done.5.u_ref = bf16[8,2,384,256]{3,2,1,0:T(8,128)(2,1)} collective-permute-done((bf16[8,2,384,256]{3,2,1,0:T(8,128)(2,1)S(1)}, bf16[8,2,384,256]{3,2,1,0:T(8,128)(2,1)}, u32[]{:S(2)}, u32[]{:S(2)}) %collective-permute-start.5) | collective-permute-done | bytes 3145760 | tf_op jit(solution)/shard_map/ppermute | solution.py:241
  65.1 6.6 %far0.1 = bf16[8,16,32,512]{3,2,1,0:T(8,128)(2,1)} custom-call(s32[1]{0:T(128)} %bitcast.odd_ref, bf16[8,2,384,256]{3,2,1,0:T(8,128)(2,1)S(1)} %get-tuple-element.12.own_ref, bf16[8,2,384,256]{3,2,1,0:T(8,128)(2,1)S(1)} %get-tuple-element.13.near_ref, bf16[8,2,384,256]{3,2,1,0:T(8,128)(2,1)} %collective-permute-done.5.u_ref, ...), custom_call_target="tpu_custom_call", output_to_operand_aliasing={{}: (5, {})} | custom-call | flops 3221225472 | bytes 8388608 | tf_op jit(solution)/shard_map/far0/pallas_call | solution.py:149
  71.7 0.0 copy-start.1
  71.7 54.5 %all_to_all.10.cross_ref = bf16[8,16,32,512]{3,2,1,0:T(8,128)(2,1)S(1)} all-to-all(bf16[8,16,32,512]{3,2,1,0:T(8,128)(2,1)} %far0.1), channel_id=1, replica_groups=mesh['pair'=64,'band'=8] {'band'}, dimensions={0} | all-to-all | bytes 8388608 | tf_op jit(solution)/shard_map/all_to_all | solution.py:225
  126.2 0.0 copy-done.1
  126.2 2.3 %to_lags.1 = bf16[8,2,4,32,256]{4,3,2,1,0:T(8,128)(2,1)S(1)} custom-call(bf16[512,2048]{1,0:T(8,128)(2,1)S(1)} %copy-done.1, bf16[8,16,32,512]{3,2,1,0:T(8,128)(2,1)S(1)} %all_to_all.10.cross_ref), custom_call_target="tpu_custom_call" | custom-call | flops 2147483648 | bytes 7340032 | tf_op jit(solution)/shard_map/to_lags/pallas_call | solution.py:187
  128.5 16.0 %all_to_all.11 = bf16[8,2,4,32,256]{4,3,2,1,0:T(8,128)(2,1)S(1)} all-to-all(bf16[8,2,4,32,256]{4,3,2,1,0:T(8,128)(2,1)S(1)} %to_lags.1), channel_id=1, replica_groups=mesh['pair'=64,'band'=8] {'band'}, dimensions={0} | all-to-all | bytes 2097152 | tf_op jit(solution)/shard_map/all_to_all | solution.py:225
  144.5 0.1 slice_bitcast_fusion
  144.6 1.9 %collective-permute-start.8 = (bf16[8,4,32,256]{3,2,1,0:T(8,128)(2,1)S(1)}, bf16[8,4,32,256]{3,2,1,0:T(8,128)(2,1)S(1)}, u32[]{:S(2)}, u32[]{:S(2)}) collective-permute-start(bf16[8,4,32,256]{3,2,1,0:T(8,128)(2,1)S(1)} %get-tuple-element.17), channel_id=1, source_target_pairs={{0,0},{24,8},{16,16},{40,24},{32,32},{56,40},{48,48},{72,56},{64,6... | collective-permute-start | bytes 1572872 | tf_op jit(solution)/shard_map/ppermute | solution.py:252
  146.5 5.9 %collective-permute-start.7 = (bf16[8,4,32,256]{3,2,1,0:T(8,128)(2,1)S(1)}, bf16[8,4,32,256]{3,2,1,0:T(8,128)(2,1)S(1)}, u32[]{:S(2)}, u32[]{:S(2)}) collective-permute-start(bf16[8,4,32,256]{3,2,1,0:T(8,128)(2,1)S(1)} %get-tuple-element.18), channel_id=1, source_target_pairs={{8,0},{0,8},{24,16},{16,24},{40,32},{32,40},{56,48},{48,56},{72,64... | collective-permute-start | bytes 1572872 | tf_op jit(solution)/shard_map/ppermute | solution.py:252
  152.4 2.1 %collective-permute-done.8.two_ref = bf16[8,4,32,256]{3,2,1,0:T(8,128)(2,1)S(1)} collective-permute-done((bf16[8,4,32,256]{3,2,1,0:T(8,128)(2,1)S(1)}, bf16[8,4,32,256]{3,2,1,0:T(8,128)(2,1)S(1)}, u32[]{:S(2)}, u32[]{:S(2)}) %collective-permute-start.8) | collective-permute-done | bytes 524320 | tf_op jit(solution)/shard_map/ppermute | solution.py:252
  154.5 0.0 collective-permute-done.7.one_ref
  154.5 1.0 assemble.1
  (1 shorter events, 0.0 us)
Async XLA Ops:
  0.0 11.3 %copy-start = (bf16[8,2,384,256]{3,2,1,0:T(8,128)(2,1)S(1)}, bf16[8,2,384,256]{3,2,1,0:T(8,128)(2,1)}, u32[]{:S(2)}) copy-start(bf16[8,2,384,256]{3,2,1,0:T(8,128)(2,1)} %s_ref.1) | copy-start | bytes 9437188
  0.0 37.1 %copy-start.2 = (s32[384,256]{1,0:T(8,128)S(1)}, s32[384,256]{1,0:T(8,128)}, u32[]{:S(2)}) copy-start(s32[384,256]{1,0:T(8,128)} %param.4) | copy-start | bytes 1179652
  2.7 8.5 %collective-permute-start = (bf16[384,256]{1,0:T(8,128)(2,1)S(1)}, bf16[384,256]{1,0:T(8,128)(2,1)S(1)}, u32[]{:S(2)}, u32[]{:S(2)}) collective-permute-start(bf16[384,256]{1,0:T(8,128)(2,1)S(1)} %convert_element_type.28), channel_id=1, source_target_pairs={{0,4},{1,5},{2,6},{3,7},{4,0},{5,1},{6,2},{7,3},{8,12},{9,13},{10,... | collective-permute-start | bytes 589832 | tf_op jit(solution)/shard_map/ppermute | solution.py:221
  11.3 40.6 %collective-permute-start.1 = (bf16[8,2,384,256]{3,2,1,0:T(8,128)(2,1)S(1)}, bf16[8,2,384,256]{3,2,1,0:T(8,128)(2,1)}, u32[]{:S(2)}, u32[]{:S(2)}) collective-permute-start(bf16[8,2,384,256]{3,2,1,0:T(8,128)(2,1)S(1)} %copy-done), channel_id=1, source_target_pairs={{8,0},{0,8},{24,16},{16,24},{40,32},{32,40},{56,48},{48,56},{72,64... | collective-permute-start | bytes 9437192 | tf_op jit(solution)/shard_map/ppermute | solution.py:240
  20.6 44.5 %collective-permute-start.5 = (bf16[8,2,384,256]{3,2,1,0:T(8,128)(2,1)S(1)}, bf16[8,2,384,256]{3,2,1,0:T(8,128)(2,1)}, u32[]{:S(2)}, u32[]{:S(2)}) collective-permute-start(bf16[8,2,384,256]{3,2,1,0:T(8,128)(2,1)S(1)} %copy-done), channel_id=1, source_target_pairs={{16,0},{504,8},{32,16},{8,24},{48,32},{24,40},{64,48},{40,56},{80,... | collective-permute-start | bytes 9437192 | tf_op jit(solution)/shard_map/ppermute | solution.py:241
  22.6 6.8 %collective-permute-start.2 = (bf16[384,256]{1,0:T(8,128)(2,1)S(1)}, bf16[384,256]{1,0:T(8,128)(2,1)S(1)}, u32[]{:S(2)}, u32[]{:S(2)}) collective-permute-start(bf16[384,256]{1,0:T(8,128)(2,1)S(1)} %fusion), channel_id=1, source_target_pairs={{0,1},{1,0},{2,3},{3,2},{4,5},{5,4},{6,7},{7,6},{8,9},{9,8},{10,11... | collective-permute-start | bytes 589832 | tf_op jit(solution)/shard_map/ppermute | solution.py:221
  29.5 7.6 %collective-permute-start.3 = (bf16[384,256]{1,0:T(8,128)(2,1)S(1)}, bf16[384,256]{1,0:T(8,128)(2,1)S(1)}, u32[]{:S(2)}, u32[]{:S(2)}) collective-permute-start(bf16[384,256]{1,0:T(8,128)(2,1)S(1)} %fusion.1), channel_id=1, source_target_pairs={{0,3},{1,2},{2,1},{3,0},{4,7},{5,6},{6,5},{7,4},{8,11},{9,10},{10,... | collective-permute-start | bytes 589832 | tf_op jit(solution)/shard_map/ppermute | solution.py:221
  37.3 11.0 %collective-permute-start.4 = (bf16[384,256]{1,0:T(8,128)(2,1)S(1)}, bf16[384,256]{1,0:T(8,128)(2,1)}, u32[]{:S(2)}, u32[]{:S(2)}) collective-permute-start(bf16[384,256]{1,0:T(8,128)(2,1)S(1)} %get-tuple-element.15), channel_id=1, source_target_pairs={{8,0},{0,8},{24,16},{16,24},{40,32},{32,40},{56,48},{48,56},{72,64... | collective-permute-start | bytes 589832 | tf_op jit(solution)/shard_map/ppermute | solution.py:246
  48.3 11.6 %collective-permute-start.6 = (bf16[384,256]{1,0:T(8,128)(2,1)}, bf16[384,256]{1,0:T(8,128)(2,1)}, u32[]{:S(2)}, u32[]{:S(2)}) collective-permute-start(bf16[384,256]{1,0:T(8,128)(2,1)} %collective-permute-done.4.fn_ref), channel_id=1, source_target_pairs={{24,0},{496,8},{40,16},{0,24},{56,32},{16,40},{72,48},{32,56},{88,... | collective-permute-start | bytes 589832 | tf_op jit(solution)/shard_map/ppermute | solution.py:247
  71.7 54.5 %copy-start.1 = (bf16[512,2048]{1,0:T(8,128)(2,1)S(1)}, bf16[512,2048]{1,0:T(8,128)(2,1)}, u32[]{:S(2)}) copy-start(bf16[512,2048]{1,0:T(8,128)(2,1)} %constant.28.clone.matrix_ref) | copy-start | bytes 6291460
  144.6 9.9 %collective-permute-start.8 = (bf16[8,4,32,256]{3,2,1,0:T(8,128)(2,1)S(1)}, bf16[8,4,32,256]{3,2,1,0:T(8,128)(2,1)S(1)}, u32[]{:S(2)}, u32[]{:S(2)}) collective-permute-start(bf16[8,4,32,256]{3,2,1,0:T(8,128)(2,1)S(1)} %get-tuple-element.17), channel_id=1, source_target_pairs={{0,0},{24,8},{16,16},{40,24},{32,32},{56,40},{48,48},{72,56},{64,6... | collective-permute-start | bytes 1572872 | tf_op jit(solution)/shard_map/ppermute | solution.py:252
  146.5 8.0 %collective-permute-start.7 = (bf16[8,4,32,256]{3,2,1,0:T(8,128)(2,1)S(1)}, bf16[8,4,32,256]{3,2,1,0:T(8,128)(2,1)S(1)}, u32[]{:S(2)}, u32[]{:S(2)}) collective-permute-start(bf16[8,4,32,256]{3,2,1,0:T(8,128)(2,1)S(1)} %get-tuple-element.18), channel_id=1, source_target_pairs={{8,0},{0,8},{24,16},{16,24},{40,32},{32,40},{56,48},{48,56},{72,64... | collective-permute-start | bytes 1572872 | tf_op jit(solution)/shard_map/ppermute | solution.py:252

commit v4 on v3

--- a/solution.py
+++ b/solution.py
@@ -16,6 +16,7 @@
 BLOCK = 256
 SUB = 16
 STEP = 2
+CUTS = (0, 6, 8)
 VMEM_LIMIT = 28 * 1024 * 1024
 
 BF16 = jnp.bfloat16
@@ -57,18 +58,29 @@
         out_ref[:, part] = piece.astype(BF16).reshape(8, 32, BLOCK)
 
 
-def near_kernel(odd_ref, s_ref, n_ref, fs_ref, fn_ref, sw_ref, nw_ref, out_ref):
+def near_kernel(starts, odd_ref, s_ref, fs_ref, fn_ref, *refs):
+    pieces, (sw_ref, nw_ref, out_ref) = refs[:-3], refs[-3:]
+    step = pl.program_id(0)
     for index in range(STEP):
-        f = pl.program_id(0) * STEP + index
-        sw_ref[f] = whiten(s_ref[f], fs_ref[...])
-        nw_ref[f] = whiten(n_ref[index], fn_ref[...])
+        f = step * STEP + index
+        for n_ref, first, last in zip(pieces, starts, starts[1:]):
+
+            @pl.when((step >= first // STEP) & (step < last // STEP))
+            def _():
+                nw_ref[f] = n_ref[index]
+
+        @pl.when(odd_ref[0] == 0)
+        def _():
+            sw_ref[f] = s_ref[f]
 
         @pl.when(odd_ref[0] != 0)
         def _():
+            sw_ref[f] = whiten(s_ref[f], fs_ref[...])
+            nw_ref[f] = whiten(nw_ref[f], fn_ref[...])
             store(out_ref.at[:, 2 * index : 2 * index + 2], product(nw_ref[f], sw_ref[f]))
 
 
-def far_kernel(first, odd_ref, own_ref, near_ref, u_ref, fu_ref, _, out_ref, held_ref, send_ref, in_sem, out_sem):
+def far_kernel(first, odd_ref, own_ref, near_ref, u_ref, fs_ref, fn_ref, fu_ref, _, out_ref, held_ref, send_ref, in_sem, out_sem):
     bins = u_ref.shape[0]
     odd = odd_ref[0]
 
@@ -93,16 +105,15 @@
     def step(f, carry):
         fetch(f).wait()
         far = whiten(held_ref[f], fu_ref[...])
-        own = own_ref[first + f]
 
         @pl.when(odd == 0)
         def _():
-            made(f, 0, near_ref[first + f], far)
-            made(f, 1, own, far)
+            made(f, 0, whiten(near_ref[first + f], fn_ref[...]), far)
+            made(f, 1, whiten(own_ref[first + f], fs_ref[...]), far)
 
         @pl.when(odd != 0)
         def _():
-            made(f, 1, far, own)
+            made(f, 1, far, own_ref[first + f])
 
         return carry
 
@@ -129,26 +140,36 @@
 BINS_BLOCK = (STEP, 2, WIN, BLOCK)
 
 
-def near_spectra(odd, s, n, fs, fn):
+def near_spectra(odd, s, fs, fn, pieces):
     shape = jax.ShapeDtypeStruct(s.shape, BF16)
-    return pl.pallas_call(
-        near_kernel,
+    starts = [0]
+    for piece in pieces:
+        starts.append(starts[-1] + piece.shape[0])
+
+    def piece_spec(first, last):
+        return pl.BlockSpec(
+            BINS_BLOCK, lambda g: (jnp.clip(g - first // STEP, 0, (last - first) // STEP - 1), 0, 0, 0)
+        )
+
+    return pl.pallas_call(
+        functools.partial(near_kernel, starts),
         grid=(8 // STEP,),
-        in_specs=[flag_spec(), held_spec(), pl.BlockSpec(BINS_BLOCK, lambda g: (g, 0, 0, 0)), held_spec(), held_spec()],
+        in_specs=[flag_spec(), held_spec(), held_spec(), held_spec()]
+        + [piece_spec(first, last) for first, last in zip(starts, starts[1:])],
         out_specs=[held_spec(), held_spec(), pl.BlockSpec(SEND_BLOCK, lambda g: (0, g, 0, 0))],
         out_shape=[shape, shape, pltpu.HBM(SEND, BF16)],
         compiler_params=params(),
         cost_estimate=pl.CostEstimate(flops=0, bytes_accessed=0, transcendentals=0),
         name="near_spectra",
-    )(odd, s, n, fs, fn)
-
-
-def far_spectra(first, odd, own, near, u, fu, filled):
+    )(odd, s, fs, fn, *pieces)
+
+
+def far_spectra(first, odd, own, near, u, fs, fn, fu, filled):
     bins = u.shape[0]
     anywhere = pl.BlockSpec(memory_space=pl.ANY)
     return pl.pallas_call(
         functools.partial(far_kernel, first),
-        in_specs=[flag_spec(), held_spec(), held_spec(), anywhere, held_spec(), anywhere],
+        in_specs=[flag_spec(), held_spec(), held_spec(), anywhere] + [held_spec()] * 3 + [anywhere],
         out_specs=anywhere,
         out_shape=pltpu.HBM(SEND, BF16),
         scratch_shapes=[
@@ -157,13 +178,13 @@
             pltpu.SemaphoreType.DMA((bins,)),
             pltpu.SemaphoreType.DMA((2, bins)),
         ],
-        input_output_aliases={5: 0},
+        input_output_aliases={7: 0},
         compiler_params=params(),
         cost_estimate=pl.CostEstimate(
             flops=bins * 2 * 2 * 768 * 256 * 512, bytes_accessed=bins << 20, transcendentals=0
         ),
         name="far" + str(first),
-    )(odd, own, near, u, fu, filled)
+    )(odd, own, near, u, fs, fn, fu, filled)
 
 
 def lags_kernel(scale, matrix_ref, cross_ref, out_ref):
@@ -231,23 +252,23 @@
     across = [((p + 2) % blocks, p) if p % 2 == 0 else ((p - 2) % blocks, p) for p in range(blocks)]
     swap = [(p ^ 1, p) for p in range(blocks)]
     back = [(p, p) if p % 2 == 0 else ((p + 2) % blocks, p) for p in range(blocks)]
-    other = [((p + 3) % blocks, p) if p % 2 == 0 else ((p - 3) % blocks, p) for p in range(blocks)]
     barrier = lax.optimization_barrier
 
     values = spectra.astype(F32)
     energy = jnp.sum(values * values, axis=(0, 1))
-    met, whole = barrier((exchange(energy.astype(BF16), lambda b: (b + 4) % 8), spectra))
-    n = lax.ppermute(whole, "pair", swap)
+    pieces = [spectra[first:last] for first, last in zip(CUTS, CUTS[1:])]
+    met, whole, pieces = barrier((exchange(energy.astype(BF16), lambda b: (b + 4) % 8), spectra, pieces))
     u = lax.ppermute(whole, "pair", across)
+    pieces = [lax.ppermute(piece, "pair", swap) for piece in pieces]
     energy = energy + met.astype(F32)
     energy = energy + exchange(energy.astype(BF16), lambda b: b ^ 1).astype(F32)
     energy = energy + exchange(energy.astype(BF16), lambda b: (b // 4) * 4 + 3 - b % 4).astype(F32)
     fs = window_valid.astype(F32) * lax.rsqrt(energy / FREQS + EPSILON)
     fn = lax.ppermute(fs.astype(BF16), "pair", swap)
-    fu = lax.ppermute(fn, "pair", other)
-
-    sw, nw, cross = near_spectra(flag, spectra, n, fs, fn)
-    cross = far_spectra(0, flag, sw, nw, u, fu, cross)
+    fu = lax.ppermute(fs.astype(BF16), "pair", across)
+
+    sw, nw, cross = near_spectra(flag, spectra, fs, fn, pieces)
+    cross = far_spectra(0, flag, sw, nw, u, fs, fn, fu, cross)
     own = regroup(to_lags(regroup(cross)))
     return assemble(lax.ppermute(own[:, 0], "pair", swap), lax.ppermute(own[:, 1], "pair", back))
 

time: 156 us -> 150 us (0.962)
  waiting for transfers between devices: 23.8 us -> 12.4 us
  starting transfers between devices: 41.7 us -> 48.2 us
  blocking collectives: 70.4 us -> 66.4 us
  local copies, waits for them, and re-layouts: 0.1 us -> 2.61 us
    ppermute x1, starting transfers between devices: 9.83 us -> 3.38 us  [shards(): fn = lax.ppermute(fs.astype(BF16), 'pair', swap)]
    ppermute x3, waiting for transfers between devices: 13.6 us -> 7.97 us  [exchange(): return lax.ppermute(value, 'band', route)]
    ppermute x1, waiting for transfers between devices: 5.24 us -> 0.01 us  [shards(): u = lax.ppermute(whole, 'pair', across)]
    all_to_all x2, blocking collectives: 70.4 us -> 66.4 us  [regroup(): lax.all_to_all(block, 'band', split_axis=0, concat_axis=0, tiled=True)]
    ppermute x3, starting transfers between devices: 9.32 us -> 13.3 us  [exchange(): return lax.ppermute(value, 'band', route)]
    ppermute x2 -> x3, starting transfers between devices: 12.8 us -> 16.4 us  [the longest x2 14.4 us: shards(): pieces = [lax.ppermute(piece, 'pair', swap) for piece in pieces]]
    ppermute x1, starting transfers between devices: 1.92 us -> 5 us  [shards(): u = lax.ppermute(whole, 'pair', across)]
    slice x0 -> x2, local copies, waits for them, and re-layouts: none -> 2.51 us  [shards(): pieces = [spectra[first:last] for first, last in zip(CUTS, CUTS[1:])]]
  transfers between devices with their start and end apart: 9 -> 10, of which waited for: 7 -> 5; matrix products, arithmetic and copies ran while one was open for 0% -> 2% of each run, Pallas kernels for 4% -> 4%
where the time goes in v4:
time: 150 us
  blocking collectives  66.4 us (44%)
  starting transfers between devices  48.2 us (32%)
  Pallas kernels  16.2 us (11%)
  waiting for transfers between devices  12.4 us (8%)
  other arithmetic  3.7 us (2%)
  local copies, waits for them, and re-layouts  2.61 us (2%)
    all_to_all x2, blocking collectives, regroup(): lax.all_to_all(block, 'band', split_axis=0, concat_axis=0, tiled=True)  66.4 us
    ppermute x2, starting transfers between devices, shards(): pieces = [lax.ppermute(piece, 'pair', swap) for piece in pieces]  14.4 us
    ppermute x3, starting transfers between devices, exchange(): return lax.ppermute(value, 'band', route)  13.3 us
    ppermute x1, starting transfers between devices, shards(): lax.ppermute(own[:, 0], 'pair', swap)  8.16 us
    ppermute x3, waiting for transfers between devices, exchange(): return lax.ppermute(value, 'band', route)  7.97 us
    pallas_call x1, Pallas kernels, far_spectra(): pl.pallas_call(functools.partial(far_kernel, first), in_specs=[flag_spec(...  6.49 us
    pallas_call x1, Pallas kernels, near_spectra(): pl.pallas_call(functools.partial(near_kernel, starts), grid=(8 // STEP,),...  6.35 us
    ppermute x1, starting transfers between devices, shards(): u = lax.ppermute(whole, 'pair', across)  5 us
  transfers between devices with their start and end apart: 10, of which 5 were waited for; matrix products, arithmetic and copies ran while one was open for 2% of the time, Pallas kernels for 4%

profile of v4, /device:TPU:1, one launch (start us, length us, event | category | flops | bytes accessed | tf_op | source)
XLA Modules:
  0.0 149.6 jit_solution(4000494506853283831)
XLA Ops:
  0.0 0.0 copy-start
  0.0 2.7 %multiply_reduce_fusion = f32[384,256]{1,0:T(8,128)S(1)} fusion(bf16[8,2,384,256]{3,2,1,0:T(8,128)(2,1)} %s_ref.1), kind=kLoop, calls=%fused_computation | loop fusion | flops 4620288 | bytes 3538944 | tf_op jit(solution)/shard_map/reduce_sum | solution.py:258
  2.7 5.5 %collective-permute-start = (bf16[384,256]{1,0:T(8,128)(2,1)S(1)}, bf16[384,256]{1,0:T(8,128)(2,1)S(1)}, u32[]{:S(2)}, u32[]{:S(2)}) collective-permute-start(bf16[384,256]{1,0:T(8,128)(2,1)S(1)} %convert_element_type.30), channel_id=1, source_target_pairs={{0,4},{1,5},{2,6},{3,7},{4,0},{5,1},{6,2},{7,3},{8,12},{9,13},{10,... | collective-permute-start | bytes 589832 | tf_op jit(solution)/shard_map/ppermute | solution.py:242
  8.2 0.0 copy-done
  8.2 0.9 slice.13
  9.2 0.0 copy-start.2
  9.2 1.6 %slice.12 = bf16[6,2,384,256]{3,2,1,0:T(8,128)(2,1)} slice(bf16[8,2,384,256]{3,2,1,0:T(8,128)(2,1)S(1)} %copy-done), slice={[0:6], [0:2], [0:384], [0:256]} | slice | bytes 4718592 | tf_op jit(solution)/shard_map/slice | solution.py:259
  10.7 0.5 collective-permute-done
  11.3 5.0 %collective-permute-start.6 = (bf16[8,2,384,256]{3,2,1,0:T(8,128)(2,1)S(1)}, bf16[8,2,384,256]{3,2,1,0:T(8,128)(2,1)}, u32[]{:S(2)}, u32[]{:S(2)}) collective-permute-start(bf16[8,2,384,256]{3,2,1,0:T(8,128)(2,1)S(1)} %copy-done), channel_id=1, source_target_pairs={{16,0},{504,8},{32,16},{8,24},{48,32},{24,40},{64,48},{40,56},{80,... | collective-permute-start | bytes 9437192 | tf_op jit(solution)/shard_map/ppermute | solution.py:261
  16.3 12.2 %collective-permute-start.4 = (bf16[6,2,384,256]{3,2,1,0:T(8,128)(2,1)}, bf16[6,2,384,256]{3,2,1,0:T(8,128)(2,1)}, u32[]{:S(2)}, u32[]{:S(2)}) collective-permute-start(bf16[6,2,384,256]{3,2,1,0:T(8,128)(2,1)} %slice.12), channel_id=1, source_target_pairs={{8,0},{0,8},{24,16},{16,24},{40,32},{32,40},{56,48},{48,56},{72,64... | collective-permute-start | bytes 7077896 | tf_op jit(solution)/shard_map/ppermute | solution.py:262
  28.6 3.2 %collective-permute-start.1 = (bf16[384,256]{1,0:T(8,128)(2,1)S(1)}, bf16[384,256]{1,0:T(8,128)(2,1)S(1)}, u32[]{:S(2)}, u32[]{:S(2)}) collective-permute-start(bf16[384,256]{1,0:T(8,128)(2,1)S(1)} %fusion), channel_id=1, source_target_pairs={{0,1},{1,0},{2,3},{3,2},{4,5},{5,4},{6,7},{7,6},{8,9},{9,8},{10,11... | collective-permute-start | bytes 589832 | tf_op jit(solution)/shard_map/ppermute | solution.py:242
  31.8 2.2 %collective-permute-start.5 = (bf16[2,2,384,256]{3,2,1,0:T(8,128)(2,1)}, bf16[2,2,384,256]{3,2,1,0:T(8,128)(2,1)}, u32[]{:S(2)}, u32[]{:S(2)}) collective-permute-start(bf16[2,2,384,256]{3,2,1,0:T(8,128)(2,1)} %slice.13), channel_id=1, source_target_pairs={{8,0},{0,8},{24,16},{16,24},{40,32},{32,40},{56,48},{48,56},{72,64... | collective-permute-start | bytes 2359304 | tf_op jit(solution)/shard_map/ppermute | solution.py:262
  34.0 3.1 %collective-permute-done.1 = bf16[384,256]{1,0:T(8,128)(2,1)S(1)} collective-permute-done((bf16[384,256]{1,0:T(8,128)(2,1)S(1)}, bf16[384,256]{1,0:T(8,128)(2,1)S(1)}, u32[]{:S(2)}, u32[]{:S(2)}) %collective-permute-start.1) | collective-permute-done | bytes 196640 | tf_op jit(solution)/shard_map/ppermute | solution.py:242
  37.1 0.1 fusion.1
  37.2 4.6 %collective-permute-start.2 = (bf16[384,256]{1,0:T(8,128)(2,1)S(1)}, bf16[384,256]{1,0:T(8,128)(2,1)S(1)}, u32[]{:S(2)}, u32[]{:S(2)}) collective-permute-start(bf16[384,256]{1,0:T(8,128)(2,1)S(1)} %fusion.1), channel_id=1, source_target_pairs={{0,3},{1,2},{2,1},{3,0},{4,7},{5,6},{6,5},{7,4},{8,11},{9,10},{10,... | collective-permute-start | bytes 589832 | tf_op jit(solution)/shard_map/ppermute | solution.py:242
  41.8 4.4 %collective-permute-done.2 = bf16[384,256]{1,0:T(8,128)(2,1)S(1)} collective-permute-done((bf16[384,256]{1,0:T(8,128)(2,1)S(1)}, bf16[384,256]{1,0:T(8,128)(2,1)S(1)}, u32[]{:S(2)}, u32[]{:S(2)}) %collective-permute-start.2) | collective-permute-done | bytes 196640 | tf_op jit(solution)/shard_map/ppermute | solution.py:242
  46.2 0.0 copy-done.2
  46.2 0.9 fusion.2
  47.0 3.4 %collective-permute-start.3 = (bf16[384,256]{1,0:T(8,128)(2,1)}, bf16[384,256]{1,0:T(8,128)(2,1)}, u32[]{:S(2)}, u32[]{:S(2)}) collective-permute-start(bf16[384,256]{1,0:T(8,128)(2,1)} %get-tuple-element.19), channel_id=1, source_target_pairs={{8,0},{0,8},{24,16},{16,24},{40,32},{32,40},{56,48},{48,56},{72,64... | collective-permute-start | bytes 589832 | tf_op jit(solution)/shard_map/ppermute | solution.py:267
  50.4 1.9 %collective-permute-start.7 = (bf16[384,256]{1,0:T(8,128)(2,1)}, bf16[384,256]{1,0:T(8,128)(2,1)}, u32[]{:S(2)}, u32[]{:S(2)}) collective-permute-start(bf16[384,256]{1,0:T(8,128)(2,1)} %get-tuple-element.19), channel_id=1, source_target_pairs={{16,0},{504,8},{32,16},{8,24},{48,32},{24,40},{64,48},{40,56},{80,... | collective-permute-start | bytes 589832 | tf_op jit(solution)/shard_map/ppermute | solution.py:268
  52.4 0.0 collective-permute-done.3.fn_ref
  52.4 0.0 collective-permute-done.5.refs_1_
  52.4 0.0 collective-permute-done.4.refs_0_
  52.4 6.3 %near_spectra.1 = (bf16[8,2,384,256]{3,2,1,0:T(8,128)(2,1)S(1)}, bf16[8,2,384,256]{3,2,1,0:T(8,128)(2,1)S(1)}, bf16[8,16,32,512]{3,2,1,0:T(8,128)(2,1)}) custom-call(s32[1]{0:T(128)} %bitcast.odd_ref, bf16[8,2,384,256]{3,2,1,0:T(8,128)(2,1)S(1)} %copy-done, f32[384,256]{1,0:T(8,128)S(1)} %get-tuple-element.20.fs_ref, ...), custom_call_target="tpu_custom_call" | custom-call | tf_op jit(solution)/shard_map/near_spectra/pallas_call | solution.py:154
  58.7 2.9 %collective-permute-done.7.fu_ref = bf16[384,256]{1,0:T(8,128)(2,1)} collective-permute-done((bf16[384,256]{1,0:T(8,128)(2,1)}, bf16[384,256]{1,0:T(8,128)(2,1)}, u32[]{:S(2)}, u32[]{:S(2)}) %collective-permute-start.7) | collective-permute-done | bytes 196640 | tf_op jit(solution)/shard_map/ppermute | solution.py:268
  61.6 0.0 collective-permute-done.6.u_ref
  61.6 6.5 %far0.1 = bf16[8,16,32,512]{3,2,1,0:T(8,128)(2,1)} custom-call(s32[1]{0:T(128)} %bitcast.odd_ref, bf16[8,2,384,256]{3,2,1,0:T(8,128)(2,1)S(1)} %get-tuple-element.15.own_ref, bf16[8,2,384,256]{3,2,1,0:T(8,128)(2,1)S(1)} %get-tuple-element.16.near_ref, bf16[8,2,384,256]{3,2,1,0:T(8,128)(2,1)} %collective-permute-done.6.u_ref, ...), custom_call_target="tpu_custom_call", output_to_operand_aliasing={{}: (7, {})} | custom-call | flops 3221225472 | bytes 8388608 | tf_op jit(solution)/shard_map/far0/pallas_call | solution.py:170
  68.1 0.0 copy-start.1
  68.1 51.2 %all_to_all.10.cross_ref = bf16[8,16,32,512]{3,2,1,0:T(8,128)(2,1)S(1)} all-to-all(bf16[8,16,32,512]{3,2,1,0:T(8,128)(2,1)} %far0.1), channel_id=1, replica_groups=mesh['pair'=64,'band'=8] {'band'}, dimensions={0} | all-to-all | bytes 8388608 | tf_op jit(solution)/shard_map/all_to_all | solution.py:246
  119.3 0.0 copy-done.1
  119.3 2.3 %to_lags.1 = bf16[8,2,4,32,256]{4,3,2,1,0:T(8,128)(2,1)S(1)} custom-call(bf16[512,2048]{1,0:T(8,128)(2,1)S(1)} %copy-done.1, bf16[8,16,32,512]{3,2,1,0:T(8,128)(2,1)S(1)} %all_to_all.10.cross_ref), custom_call_target="tpu_custom_call" | custom-call | flops 2147483648 | bytes 7340032 | tf_op jit(solution)/shard_map/to_lags/pallas_call | solution.py:208
  121.6 15.2 %all_to_all.11 = bf16[8,2,4,32,256]{4,3,2,1,0:T(8,128)(2,1)S(1)} all-to-all(bf16[8,2,4,32,256]{4,3,2,1,0:T(8,128)(2,1)S(1)} %to_lags.1), channel_id=1, replica_groups=mesh['pair'=64,'band'=8] {'band'}, dimensions={0} | all-to-all | bytes 2097152 | tf_op jit(solution)/shard_map/all_to_all | solution.py:246
  136.8 0.1 slice_bitcast_fusion
  136.9 1.9 %collective-permute-start.9 = (bf16[8,4,32,256]{3,2,1,0:T(8,128)(2,1)S(1)}, bf16[8,4,32,256]{3,2,1,0:T(8,128)(2,1)S(1)}, u32[]{:S(2)}, u32[]{:S(2)}) collective-permute-start(bf16[8,4,32,256]{3,2,1,0:T(8,128)(2,1)S(1)} %get-tuple-element.21), channel_id=1, source_target_pairs={{0,0},{24,8},{16,16},{40,24},{32,32},{56,40},{48,48},{72,56},{64,6... | collective-permute-start | bytes 1572872 | tf_op jit(solution)/shard_map/ppermute | solution.py:273
  138.9 8.2 %collective-permute-start.8 = (bf16[8,4,32,256]{3,2,1,0:T(8,128)(2,1)S(1)}, bf16[8,4,32,256]{3,2,1,0:T(8,128)(2,1)S(1)}, u32[]{:S(2)}, u32[]{:S(2)}) collective-permute-start(bf16[8,4,32,256]{3,2,1,0:T(8,128)(2,1)S(1)} %get-tuple-element.22), channel_id=1, source_target_pairs={{8,0},{0,8},{24,16},{16,24},{40,32},{32,40},{56,48},{48,56},{72,64... | collective-permute-start | bytes 1572872 | tf_op jit(solution)/shard_map/ppermute | solution.py:273
  147.0 0.0 collective-permute-done.9.two_ref
  147.0 1.5 %collective-permute-done.8.one_ref = bf16[8,4,32,256]{3,2,1,0:T(8,128)(2,1)S(1)} collective-permute-done((bf16[8,4,32,256]{3,2,1,0:T(8,128)(2,1)S(1)}, bf16[8,4,32,256]{3,2,1,0:T(8,128)(2,1)S(1)}, u32[]{:S(2)}, u32[]{:S(2)}) %collective-permute-start.8) | collective-permute-done | bytes 524320 | tf_op jit(solution)/shard_map/ppermute | solution.py:273
  148.5 1.0 assemble.1
  (2 shorter events, 0.1 us)
Async XLA Ops:
  0.0 8.2 %copy-start = (bf16[8,2,384,256]{3,2,1,0:T(8,128)(2,1)S(1)}, bf16[8,2,384,256]{3,2,1,0:T(8,128)(2,1)}, u32[]{:S(2)}) copy-start(bf16[8,2,384,256]{3,2,1,0:T(8,128)(2,1)} %s_ref.1) | copy-start | bytes 9437188
  2.7 8.5 %collective-permute-start = (bf16[384,256]{1,0:T(8,128)(2,1)S(1)}, bf16[384,256]{1,0:T(8,128)(2,1)S(1)}, u32[]{:S(2)}, u32[]{:S(2)}) collective-permute-start(bf16[384,256]{1,0:T(8,128)(2,1)S(1)} %convert_element_type.30), channel_id=1, source_target_pairs={{0,4},{1,5},{2,6},{3,7},{4,0},{5,1},{6,2},{7,3},{8,12},{9,13},{10,... | collective-permute-start | bytes 589832 | tf_op jit(solution)/shard_map/ppermute | solution.py:242
  9.2 37.0 %copy-start.2 = (s32[384,256]{1,0:T(8,128)S(1)}, s32[384,256]{1,0:T(8,128)}, u32[]{:S(2)}) copy-start(s32[384,256]{1,0:T(8,128)} %param.4) | copy-start | bytes 1179652
  11.3 50.4 %collective-permute-start.6 = (bf16[8,2,384,256]{3,2,1,0:T(8,128)(2,1)S(1)}, bf16[8,2,384,256]{3,2,1,0:T(8,128)(2,1)}, u32[]{:S(2)}, u32[]{:S(2)}) collective-permute-start(bf16[8,2,384,256]{3,2,1,0:T(8,128)(2,1)S(1)} %copy-done), channel_id=1, source_target_pairs={{16,0},{504,8},{32,16},{8,24},{48,32},{24,40},{64,48},{40,56},{80,... | collective-permute-start | bytes 9437192 | tf_op jit(solution)/shard_map/ppermute | solution.py:261
  16.3 36.1 %collective-permute-start.4 = (bf16[6,2,384,256]{3,2,1,0:T(8,128)(2,1)}, bf16[6,2,384,256]{3,2,1,0:T(8,128)(2,1)}, u32[]{:S(2)}, u32[]{:S(2)}) collective-permute-start(bf16[6,2,384,256]{3,2,1,0:T(8,128)(2,1)} %slice.12), channel_id=1, source_target_pairs={{8,0},{0,8},{24,16},{16,24},{40,32},{32,40},{56,48},{48,56},{72,64... | collective-permute-start | bytes 7077896 | tf_op jit(solution)/shard_map/ppermute | solution.py:262
  28.6 8.5 %collective-permute-start.1 = (bf16[384,256]{1,0:T(8,128)(2,1)S(1)}, bf16[384,256]{1,0:T(8,128)(2,1)S(1)}, u32[]{:S(2)}, u32[]{:S(2)}) collective-permute-start(bf16[384,256]{1,0:T(8,128)(2,1)S(1)} %fusion), channel_id=1, source_target_pairs={{0,1},{1,0},{2,3},{3,2},{4,5},{5,4},{6,7},{7,6},{8,9},{9,8},{10,11... | collective-permute-start | bytes 589832 | tf_op jit(solution)/shard_map/ppermute | solution.py:242
  31.8 20.6 %collective-permute-start.5 = (bf16[2,2,384,256]{3,2,1,0:T(8,128)(2,1)}, bf16[2,2,384,256]{3,2,1,0:T(8,128)(2,1)}, u32[]{:S(2)}, u32[]{:S(2)}) collective-permute-start(bf16[2,2,384,256]{3,2,1,0:T(8,128)(2,1)} %slice.13), channel_id=1, source_target_pairs={{8,0},{0,8},{24,16},{16,24},{40,32},{32,40},{56,48},{48,56},{72,64... | collective-permute-start | bytes 2359304 | tf_op jit(solution)/shard_map/ppermute | solution.py:262
  37.2 9.0 %collective-permute-start.2 = (bf16[384,256]{1,0:T(8,128)(2,1)S(1)}, bf16[384,256]{1,0:T(8,128)(2,1)S(1)}, u32[]{:S(2)}, u32[]{:S(2)}) collective-permute-start(bf16[384,256]{1,0:T(8,128)(2,1)S(1)} %fusion.1), channel_id=1, source_target_pairs={{0,3},{1,2},{2,1},{3,0},{4,7},{5,6},{6,5},{7,4},{8,11},{9,10},{10,... | collective-permute-start | bytes 589832 | tf_op jit(solution)/shard_map/ppermute | solution.py:242
  47.0 5.3 %collective-permute-start.3 = (bf16[384,256]{1,0:T(8,128)(2,1)}, bf16[384,256]{1,0:T(8,128)(2,1)}, u32[]{:S(2)}, u32[]{:S(2)}) collective-permute-start(bf16[384,256]{1,0:T(8,128)(2,1)} %get-tuple-element.19), channel_id=1, source_target_pairs={{8,0},{0,8},{24,16},{16,24},{40,32},{32,40},{56,48},{48,56},{72,64... | collective-permute-start | bytes 589832 | tf_op jit(solution)/shard_map/ppermute | solution.py:267
  50.4 11.2 %collective-permute-start.7 = (bf16[384,256]{1,0:T(8,128)(2,1)}, bf16[384,256]{1,0:T(8,128)(2,1)}, u32[]{:S(2)}, u32[]{:S(2)}) collective-permute-start(bf16[384,256]{1,0:T(8,128)(2,1)} %get-tuple-element.19), channel_id=1, source_target_pairs={{16,0},{504,8},{32,16},{8,24},{48,32},{24,40},{64,48},{40,56},{80,... | collective-permute-start | bytes 589832 | tf_op jit(solution)/shard_map/ppermute | solution.py:268
  68.1 51.2 %copy-start.1 = (bf16[512,2048]{1,0:T(8,128)(2,1)S(1)}, bf16[512,2048]{1,0:T(8,128)(2,1)}, u32[]{:S(2)}) copy-start(bf16[512,2048]{1,0:T(8,128)(2,1)} %constant.28.clone.matrix_ref) | copy-start | bytes 6291460
  136.9 10.1 %collective-permute-start.9 = (bf16[8,4,32,256]{3,2,1,0:T(8,128)(2,1)S(1)}, bf16[8,4,32,256]{3,2,1,0:T(8,128)(2,1)S(1)}, u32[]{:S(2)}, u32[]{:S(2)}) collective-permute-start(bf16[8,4,32,256]{3,2,1,0:T(8,128)(2,1)S(1)} %get-tuple-element.21), channel_id=1, source_target_pairs={{0,0},{24,8},{16,16},{40,24},{32,32},{56,40},{48,48},{72,56},{64,6... | collective-permute-start | bytes 1572872 | tf_op jit(solution)/shard_map/ppermute | solution.py:273
  138.9 9.7 %collective-permute-start.8 = (bf16[8,4,32,256]{3,2,1,0:T(8,128)(2,1)S(1)}, bf16[8,4,32,256]{3,2,1,0:T(8,128)(2,1)S(1)}, u32[]{:S(2)}, u32[]{:S(2)}) collective-permute-start(bf16[8,4,32,256]{3,2,1,0:T(8,128)(2,1)S(1)} %get-tuple-element.22), channel_id=1, source_target_pairs={{8,0},{0,8},{24,16},{16,24},{40,32},{32,40},{56,48},{48,56},{72,64... | collective-permute-start | bytes 1572872 | tf_op jit(solution)/shard_map/ppermute | solution.py:273

commit v5 on v4

--- a/solution.py
+++ b/solution.py
@@ -80,7 +80,7 @@
             store(out_ref.at[:, 2 * index : 2 * index + 2], product(nw_ref[f], sw_ref[f]))
 
 
-def far_kernel(first, odd_ref, own_ref, near_ref, u_ref, fs_ref, fn_ref, fu_ref, _, out_ref, held_ref, send_ref, in_sem, out_sem):
+def far_kernel(first, odd_ref, own_ref, near_ref, u_ref, fs_any, fn_any, fu_any, _, out_ref, held_ref, fs_ref, fn_ref, fu_ref, send_ref, in_sem, factor_sem, out_sem):
     bins = u_ref.shape[0]
     odd = odd_ref[0]
 
@@ -99,8 +99,26 @@
         store(send_ref.at[:, pl.ds(2 * f, 2), :, pl.ds(part * BLOCK, BLOCK)], product(left, right))
         put(f, part).start()
 
-    for f in range(bins):
+    def factor(index):
+        pairs = ((fu_any, fu_ref), (fs_any, fs_ref), (fn_any, fn_ref))
+        return pltpu.make_async_copy(*pairs[index], factor_sem.at[index])
+
+    factor(0).start()
+    fetch(0).start()
+
+    @pl.when(odd == 0)
+    def _():
+        factor(1).start()
+        factor(2).start()
+
+    for f in range(1, bins):
         fetch(f).start()
+    factor(0).wait()
+
+    @pl.when(odd == 0)
+    def _():
+        factor(1).wait()
+        factor(2).wait()
 
     def step(f, carry):
         fetch(f).wait()
@@ -169,13 +187,17 @@
     anywhere = pl.BlockSpec(memory_space=pl.ANY)
     return pl.pallas_call(
         functools.partial(far_kernel, first),
-        in_specs=[flag_spec(), held_spec(), held_spec(), anywhere] + [held_spec()] * 3 + [anywhere],
+        in_specs=[flag_spec(), held_spec(), held_spec()] + [anywhere] * 5,
         out_specs=anywhere,
         out_shape=pltpu.HBM(SEND, BF16),
         scratch_shapes=[
             pltpu.VMEM((bins, 2, WIN, BLOCK), BF16),
+            pltpu.VMEM((WIN, BLOCK), fs.dtype),
+            pltpu.VMEM((WIN, BLOCK), fn.dtype),
+            pltpu.VMEM((WIN, BLOCK), fu.dtype),
             pltpu.VMEM((8, 2 * bins, 32, 2 * BLOCK), BF16),
             pltpu.SemaphoreType.DMA((bins,)),
+            pltpu.SemaphoreType.DMA((3,)),
             pltpu.SemaphoreType.DMA((2, bins)),
         ],
         input_output_aliases={7: 0},

time: 150 us -> 149 us (level)
  no operation moved by 1% of the time
where the time goes in v5:
time: 149 us
  blocking collectives  66.3 us (44%)
  starting transfers between devices  48.2 us (32%)
  Pallas kernels  15.3 us (10%)
  waiting for transfers between devices  12.4 us (8%)
  other arithmetic  3.7 us (2%)
  local copies, waits for them, and re-layouts  2.61 us (2%)
    all_to_all x2, blocking collectives, regroup(): lax.all_to_all(block, 'band', split_axis=0, concat_axis=0, tiled=True)  66.3 us
    ppermute x2, starting transfers between devices, shards(): pieces = [lax.ppermute(piece, 'pair', swap) for piece in pieces]  14.4 us
    ppermute x3, starting transfers between devices, exchange(): return lax.ppermute(value, 'band', route)  13.3 us
    ppermute x1, starting transfers between devices, shards(): lax.ppermute(own[:, 0], 'pair', swap)  8.17 us
    ppermute x3, waiting for transfers between devices, exchange(): return lax.ppermute(value, 'band', route)  7.97 us
    pallas_call x1, Pallas kernels, near_spectra(): pl.pallas_call(functools.partial(near_kernel, starts), grid=(8 // STEP,),...  6.35 us
    pallas_call x1, Pallas kernels, far_spectra(): pl.pallas_call(functools.partial(far_kernel, first), in_specs=[flag_spec(...  5.6 us
    ppermute x1, starting transfers between devices, shards(): u = lax.ppermute(whole, 'pair', across)  5 us
  transfers between devices with their start and end apart: 10, of which 5 were waited for; matrix products, arithmetic and copies ran while one was open for 2% of the time, Pallas kernels for 4%

profile of v5, /device:TPU:1, one launch (start us, length us, event | category | flops | bytes accessed | tf_op | source)
XLA Modules:
  0.0 148.7 jit_solution(16472091829446563063)
XLA Ops:
  0.0 0.0 copy-start
  0.0 2.7 %multiply_reduce_fusion = f32[384,256]{1,0:T(8,128)S(1)} fusion(bf16[8,2,384,256]{3,2,1,0:T(8,128)(2,1)} %s_ref.1), kind=kLoop, calls=%fused_computation | loop fusion | flops 4620288 | bytes 3538944 | tf_op jit(solution)/shard_map/reduce_sum | solution.py:280
  2.7 5.5 %collective-permute-start = (bf16[384,256]{1,0:T(8,128)(2,1)S(1)}, bf16[384,256]{1,0:T(8,128)(2,1)S(1)}, u32[]{:S(2)}, u32[]{:S(2)}) collective-permute-start(bf16[384,256]{1,0:T(8,128)(2,1)S(1)} %convert_element_type.30), channel_id=1, source_target_pairs={{0,4},{1,5},{2,6},{3,7},{4,0},{5,1},{6,2},{7,3},{8,12},{9,13},{10,... | collective-permute-start | bytes 589832 | tf_op jit(solution)/shard_map/ppermute | solution.py:264
  8.2 0.0 copy-done
  8.2 0.9 slice.13
  9.2 0.0 copy-start.2
  9.2 1.6 %slice.12 = bf16[6,2,384,256]{3,2,1,0:T(8,128)(2,1)} slice(bf16[8,2,384,256]{3,2,1,0:T(8,128)(2,1)S(1)} %copy-done), slice={[0:6], [0:2], [0:384], [0:256]} | slice | bytes 4718592 | tf_op jit(solution)/shard_map/slice | solution.py:281
  10.7 0.5 collective-permute-done
  11.3 5.0 %collective-permute-start.6 = (bf16[8,2,384,256]{3,2,1,0:T(8,128)(2,1)S(1)}, bf16[8,2,384,256]{3,2,1,0:T(8,128)(2,1)}, u32[]{:S(2)}, u32[]{:S(2)}) collective-permute-start(bf16[8,2,384,256]{3,2,1,0:T(8,128)(2,1)S(1)} %copy-done), channel_id=1, source_target_pairs={{16,0},{504,8},{32,16},{8,24},{48,32},{24,40},{64,48},{40,56},{80,... | collective-permute-start | bytes 9437192 | tf_op jit(solution)/shard_map/ppermute | solution.py:283
  16.3 12.2 %collective-permute-start.4 = (bf16[6,2,384,256]{3,2,1,0:T(8,128)(2,1)}, bf16[6,2,384,256]{3,2,1,0:T(8,128)(2,1)}, u32[]{:S(2)}, u32[]{:S(2)}) collective-permute-start(bf16[6,2,384,256]{3,2,1,0:T(8,128)(2,1)} %slice.12), channel_id=1, source_target_pairs={{8,0},{0,8},{24,16},{16,24},{40,32},{32,40},{56,48},{48,56},{72,64... | collective-permute-start | bytes 7077896 | tf_op jit(solution)/shard_map/ppermute | solution.py:284
  28.6 3.2 %collective-permute-start.1 = (bf16[384,256]{1,0:T(8,128)(2,1)S(1)}, bf16[384,256]{1,0:T(8,128)(2,1)S(1)}, u32[]{:S(2)}, u32[]{:S(2)}) collective-permute-start(bf16[384,256]{1,0:T(8,128)(2,1)S(1)} %fusion), channel_id=1, source_target_pairs={{0,1},{1,0},{2,3},{3,2},{4,5},{5,4},{6,7},{7,6},{8,9},{9,8},{10,11... | collective-permute-start | bytes 589832 | tf_op jit(solution)/shard_map/ppermute | solution.py:264
  31.8 2.2 %collective-permute-start.5 = (bf16[2,2,384,256]{3,2,1,0:T(8,128)(2,1)}, bf16[2,2,384,256]{3,2,1,0:T(8,128)(2,1)}, u32[]{:S(2)}, u32[]{:S(2)}) collective-permute-start(bf16[2,2,384,256]{3,2,1,0:T(8,128)(2,1)} %slice.13), channel_id=1, source_target_pairs={{8,0},{0,8},{24,16},{16,24},{40,32},{32,40},{56,48},{48,56},{72,64... | collective-permute-start | bytes 2359304 | tf_op jit(solution)/shard_map/ppermute | solution.py:284
  34.0 3.1 %collective-permute-done.1 = bf16[384,256]{1,0:T(8,128)(2,1)S(1)} collective-permute-done((bf16[384,256]{1,0:T(8,128)(2,1)S(1)}, bf16[384,256]{1,0:T(8,128)(2,1)S(1)}, u32[]{:S(2)}, u32[]{:S(2)}) %collective-permute-start.1) | collective-permute-done | bytes 196640 | tf_op jit(solution)/shard_map/ppermute | solution.py:264
  37.1 0.1 fusion.1
  37.2 4.6 %collective-permute-start.2 = (bf16[384,256]{1,0:T(8,128)(2,1)S(1)}, bf16[384,256]{1,0:T(8,128)(2,1)S(1)}, u32[]{:S(2)}, u32[]{:S(2)}) collective-permute-start(bf16[384,256]{1,0:T(8,128)(2,1)S(1)} %fusion.1), channel_id=1, source_target_pairs={{0,3},{1,2},{2,1},{3,0},{4,7},{5,6},{6,5},{7,4},{8,11},{9,10},{10,... | collective-permute-start | bytes 589832 | tf_op jit(solution)/shard_map/ppermute | solution.py:264
  41.8 4.4 %collective-permute-done.2 = bf16[384,256]{1,0:T(8,128)(2,1)S(1)} collective-permute-done((bf16[384,256]{1,0:T(8,128)(2,1)S(1)}, bf16[384,256]{1,0:T(8,128)(2,1)S(1)}, u32[]{:S(2)}, u32[]{:S(2)}) %collective-permute-start.2) | collective-permute-done | bytes 196640 | tf_op jit(solution)/shard_map/ppermute | solution.py:264
  46.2 0.0 copy-done.2
  46.2 0.9 fusion.2
  47.0 3.4 %collective-permute-start.3 = (bf16[384,256]{1,0:T(8,128)(2,1)}, bf16[384,256]{1,0:T(8,128)(2,1)}, u32[]{:S(2)}, u32[]{:S(2)}) collective-permute-start(bf16[384,256]{1,0:T(8,128)(2,1)} %get-tuple-element.19), channel_id=1, source_target_pairs={{8,0},{0,8},{24,16},{16,24},{40,32},{32,40},{56,48},{48,56},{72,64... | collective-permute-start | bytes 589832 | tf_op jit(solution)/shard_map/ppermute | solution.py:289
  50.4 1.9 %collective-permute-start.7 = (bf16[384,256]{1,0:T(8,128)(2,1)}, bf16[384,256]{1,0:T(8,128)(2,1)}, u32[]{:S(2)}, u32[]{:S(2)}) collective-permute-start(bf16[384,256]{1,0:T(8,128)(2,1)} %get-tuple-element.19), channel_id=1, source_target_pairs={{16,0},{504,8},{32,16},{8,24},{48,32},{24,40},{64,48},{40,56},{80,... | collective-permute-start | bytes 589832 | tf_op jit(solution)/shard_map/ppermute | solution.py:290
  52.4 0.0 collective-permute-done.3.fn_ref.fn_any
  52.4 0.0 collective-permute-done.5.refs_1_
  52.4 0.0 collective-permute-done.4.refs_0_
  52.4 6.3 %near_spectra.1 = (bf16[8,2,384,256]{3,2,1,0:T(8,128)(2,1)S(1)}, bf16[8,2,384,256]{3,2,1,0:T(8,128)(2,1)S(1)}, bf16[8,16,32,512]{3,2,1,0:T(8,128)(2,1)}) custom-call(s32[1]{0:T(128)} %bitcast.odd_ref, bf16[8,2,384,256]{3,2,1,0:T(8,128)(2,1)S(1)} %copy-done, f32[384,256]{1,0:T(8,128)S(1)} %get-tuple-element.20.fs_ref.fs_any, ...), custom_call_target="tpu_custom_call" | custom-call | tf_op jit(solution)/shard_map/near_spectra/pallas_call | solution.py:172
  58.7 2.9 %collective-permute-done.7.fu_any = bf16[384,256]{1,0:T(8,128)(2,1)} collective-permute-done((bf16[384,256]{1,0:T(8,128)(2,1)}, bf16[384,256]{1,0:T(8,128)(2,1)}, u32[]{:S(2)}, u32[]{:S(2)}) %collective-permute-start.7) | collective-permute-done | bytes 196640 | tf_op jit(solution)/shard_map/ppermute | solution.py:290
  61.6 0.0 collective-permute-done.6.u_ref
  61.6 5.6 %far0.1 = bf16[8,16,32,512]{3,2,1,0:T(8,128)(2,1)} custom-call(s32[1]{0:T(128)} %bitcast.odd_ref, bf16[8,2,384,256]{3,2,1,0:T(8,128)(2,1)S(1)} %get-tuple-element.15.own_ref, bf16[8,2,384,256]{3,2,1,0:T(8,128)(2,1)S(1)} %get-tuple-element.16.near_ref, bf16[8,2,384,256]{3,2,1,0:T(8,128)(2,1)} %collective-permute-done.6.u_ref, ...), custom_call_target="tpu_custom_call", output_to_operand_aliasing={{}: (7, {})} | custom-call | flops 3221225472 | bytes 8388608 | tf_op jit(solution)/shard_map/far0/pallas_call | solution.py:188
  67.2 0.0 copy-start.1
  67.3 50.9 %all_to_all.10.cross_ref = bf16[8,16,32,512]{3,2,1,0:T(8,128)(2,1)S(1)} all-to-all(bf16[8,16,32,512]{3,2,1,0:T(8,128)(2,1)} %far0.1), channel_id=1, replica_groups=mesh['pair'=64,'band'=8] {'band'}, dimensions={0} | all-to-all | bytes 8388608 | tf_op jit(solution)/shard_map/all_to_all | solution.py:268
  118.2 0.0 copy-done.1
  118.2 2.3 %to_lags.1 = bf16[8,2,4,32,256]{4,3,2,1,0:T(8,128)(2,1)S(1)} custom-call(bf16[512,2048]{1,0:T(8,128)(2,1)S(1)} %copy-done.1, bf16[8,16,32,512]{3,2,1,0:T(8,128)(2,1)S(1)} %all_to_all.10.cross_ref), custom_call_target="tpu_custom_call" | custom-call | flops 2147483648 | bytes 7340032 | tf_op jit(solution)/shard_map/to_lags/pallas_call | solution.py:230
  120.5 15.4 %all_to_all.11 = bf16[8,2,4,32,256]{4,3,2,1,0:T(8,128)(2,1)S(1)} all-to-all(bf16[8,2,4,32,256]{4,3,2,1,0:T(8,128)(2,1)S(1)} %to_lags.1), channel_id=1, replica_groups=mesh['pair'=64,'band'=8] {'band'}, dimensions={0} | all-to-all | bytes 2097152 | tf_op jit(solution)/shard_map/all_to_all | solution.py:268
  135.9 0.1 slice_bitcast_fusion
  136.0 1.9 %collective-permute-start.9 = (bf16[8,4,32,256]{3,2,1,0:T(8,128)(2,1)S(1)}, bf16[8,4,32,256]{3,2,1,0:T(8,128)(2,1)S(1)}, u32[]{:S(2)}, u32[]{:S(2)}) collective-permute-start(bf16[8,4,32,256]{3,2,1,0:T(8,128)(2,1)S(1)} %get-tuple-element.21), channel_id=1, source_target_pairs={{0,0},{24,8},{16,16},{40,24},{32,32},{56,40},{48,48},{72,56},{64,6... | collective-permute-start | bytes 1572872 | tf_op jit(solution)/shard_map/ppermute | solution.py:295
  138.0 8.2 %collective-permute-start.8 = (bf16[8,4,32,256]{3,2,1,0:T(8,128)(2,1)S(1)}, bf16[8,4,32,256]{3,2,1,0:T(8,128)(2,1)S(1)}, u32[]{:S(2)}, u32[]{:S(2)}) collective-permute-start(bf16[8,4,32,256]{3,2,1,0:T(8,128)(2,1)S(1)} %get-tuple-element.22), channel_id=1, source_target_pairs={{8,0},{0,8},{24,16},{16,24},{40,32},{32,40},{56,48},{48,56},{72,64... | collective-permute-start | bytes 1572872 | tf_op jit(solution)/shard_map/ppermute | solution.py:295
  146.1 0.0 collective-permute-done.9.two_ref
  146.2 1.5 %collective-permute-done.8.one_ref = bf16[8,4,32,256]{3,2,1,0:T(8,128)(2,1)S(1)} collective-permute-done((bf16[8,4,32,256]{3,2,1,0:T(8,128)(2,1)S(1)}, bf16[8,4,32,256]{3,2,1,0:T(8,128)(2,1)S(1)}, u32[]{:S(2)}, u32[]{:S(2)}) %collective-permute-start.8) | collective-permute-done | bytes 524320 | tf_op jit(solution)/shard_map/ppermute | solution.py:295
  147.7 1.0 assemble.1
  (2 shorter events, 0.1 us)
Async XLA Ops:
  0.0 8.2 %copy-start = (bf16[8,2,384,256]{3,2,1,0:T(8,128)(2,1)S(1)}, bf16[8,2,384,256]{3,2,1,0:T(8,128)(2,1)}, u32[]{:S(2)}) copy-start(bf16[8,2,384,256]{3,2,1,0:T(8,128)(2,1)} %s_ref.1) | copy-start | bytes 9437188
  2.7 8.5 %collective-permute-start = (bf16[384,256]{1,0:T(8,128)(2,1)S(1)}, bf16[384,256]{1,0:T(8,128)(2,1)S(1)}, u32[]{:S(2)}, u32[]{:S(2)}) collective-permute-start(bf16[384,256]{1,0:T(8,128)(2,1)S(1)} %convert_element_type.30), channel_id=1, source_target_pairs={{0,4},{1,5},{2,6},{3,7},{4,0},{5,1},{6,2},{7,3},{8,12},{9,13},{10,... | collective-permute-start | bytes 589832 | tf_op jit(solution)/shard_map/ppermute | solution.py:264
  9.2 37.0 %copy-start.2 = (s32[384,256]{1,0:T(8,128)S(1)}, s32[384,256]{1,0:T(8,128)}, u32[]{:S(2)}) copy-start(s32[384,256]{1,0:T(8,128)} %param.4) | copy-start | bytes 1179652
  11.3 50.4 %collective-permute-start.6 = (bf16[8,2,384,256]{3,2,1,0:T(8,128)(2,1)S(1)}, bf16[8,2,384,256]{3,2,1,0:T(8,128)(2,1)}, u32[]{:S(2)}, u32[]{:S(2)}) collective-permute-start(bf16[8,2,384,256]{3,2,1,0:T(8,128)(2,1)S(1)} %copy-done), channel_id=1, source_target_pairs={{16,0},{504,8},{32,16},{8,24},{48,32},{24,40},{64,48},{40,56},{80,... | collective-permute-start | bytes 9437192 | tf_op jit(solution)/shard_map/ppermute | solution.py:283
  16.3 36.1 %collective-permute-start.4 = (bf16[6,2,384,256]{3,2,1,0:T(8,128)(2,1)}, bf16[6,2,384,256]{3,2,1,0:T(8,128)(2,1)}, u32[]{:S(2)}, u32[]{:S(2)}) collective-permute-start(bf16[6,2,384,256]{3,2,1,0:T(8,128)(2,1)} %slice.12), channel_id=1, source_target_pairs={{8,0},{0,8},{24,16},{16,24},{40,32},{32,40},{56,48},{48,56},{72,64... | collective-permute-start | bytes 7077896 | tf_op jit(solution)/shard_map/ppermute | solution.py:284
  28.6 8.5 %collective-permute-start.1 = (bf16[384,256]{1,0:T(8,128)(2,1)S(1)}, bf16[384,256]{1,0:T(8,128)(2,1)S(1)}, u32[]{:S(2)}, u32[]{:S(2)}) collective-permute-start(bf16[384,256]{1,0:T(8,128)(2,1)S(1)} %fusion), channel_id=1, source_target_pairs={{0,1},{1,0},{2,3},{3,2},{4,5},{5,4},{6,7},{7,6},{8,9},{9,8},{10,11... | collective-permute-start | bytes 589832 | tf_op jit(solution)/shard_map/ppermute | solution.py:264
  31.8 20.6 %collective-permute-start.5 = (bf16[2,2,384,256]{3,2,1,0:T(8,128)(2,1)}, bf16[2,2,384,256]{3,2,1,0:T(8,128)(2,1)}, u32[]{:S(2)}, u32[]{:S(2)}) collective-permute-start(bf16[2,2,384,256]{3,2,1,0:T(8,128)(2,1)} %slice.13), channel_id=1, source_target_pairs={{8,0},{0,8},{24,16},{16,24},{40,32},{32,40},{56,48},{48,56},{72,64... | collective-permute-start | bytes 2359304 | tf_op jit(solution)/shard_map/ppermute | solution.py:284
  37.2 9.0 %collective-permute-start.2 = (bf16[384,256]{1,0:T(8,128)(2,1)S(1)}, bf16[384,256]{1,0:T(8,128)(2,1)S(1)}, u32[]{:S(2)}, u32[]{:S(2)}) collective-permute-start(bf16[384,256]{1,0:T(8,128)(2,1)S(1)} %fusion.1), channel_id=1, source_target_pairs={{0,3},{1,2},{2,1},{3,0},{4,7},{5,6},{6,5},{7,4},{8,11},{9,10},{10,... | collective-permute-start | bytes 589832 | tf_op jit(solution)/shard_map/ppermute | solution.py:264
  47.0 5.3 %collective-permute-start.3 = (bf16[384,256]{1,0:T(8,128)(2,1)}, bf16[384,256]{1,0:T(8,128)(2,1)}, u32[]{:S(2)}, u32[]{:S(2)}) collective-permute-start(bf16[384,256]{1,0:T(8,128)(2,1)} %get-tuple-element.19), channel_id=1, source_target_pairs={{8,0},{0,8},{24,16},{16,24},{40,32},{32,40},{56,48},{48,56},{72,64... | collective-permute-start | bytes 589832 | tf_op jit(solution)/shard_map/ppermute | solution.py:289
  50.4 11.2 %collective-permute-start.7 = (bf16[384,256]{1,0:T(8,128)(2,1)}, bf16[384,256]{1,0:T(8,128)(2,1)}, u32[]{:S(2)}, u32[]{:S(2)}) collective-permute-start(bf16[384,256]{1,0:T(8,128)(2,1)} %get-tuple-element.19), channel_id=1, source_target_pairs={{16,0},{504,8},{32,16},{8,24},{48,32},{24,40},{64,48},{40,56},{80,... | collective-permute-start | bytes 589832 | tf_op jit(solution)/shard_map/ppermute | solution.py:290
  67.2 50.9 %copy-start.1 = (bf16[512,2048]{1,0:T(8,128)(2,1)S(1)}, bf16[512,2048]{1,0:T(8,128)(2,1)}, u32[]{:S(2)}) copy-start(bf16[512,2048]{1,0:T(8,128)(2,1)} %constant.28.clone.matrix_ref) | copy-start | bytes 6291460
  136.0 10.1 %collective-permute-start.9 = (bf16[8,4,32,256]{3,2,1,0:T(8,128)(2,1)S(1)}, bf16[8,4,32,256]{3,2,1,0:T(8,128)(2,1)S(1)}, u32[]{:S(2)}, u32[]{:S(2)}) collective-permute-start(bf16[8,4,32,256]{3,2,1,0:T(8,128)(2,1)S(1)} %get-tuple-element.21), channel_id=1, source_target_pairs={{0,0},{24,8},{16,16},{40,24},{32,32},{56,40},{48,48},{72,56},{64,6... | collective-permute-start | bytes 1572872 | tf_op jit(solution)/shard_map/ppermute | solution.py:295
  138.0 9.7 %collective-permute-start.8 = (bf16[8,4,32,256]{3,2,1,0:T(8,128)(2,1)S(1)}, bf16[8,4,32,256]{3,2,1,0:T(8,128)(2,1)S(1)}, u32[]{:S(2)}, u32[]{:S(2)}) collective-permute-start(bf16[8,4,32,256]{3,2,1,0:T(8,128)(2,1)S(1)} %get-tuple-element.22), channel_id=1, source_target_pairs={{8,0},{0,8},{24,16},{16,24},{40,32},{32,40},{56,48},{48,56},{72,64... | collective-permute-start | bytes 1572872 | tf_op jit(solution)/shard_map/ppermute | solution.py:295

commit v6 on v5

--- a/solution.py
+++ b/solution.py
@@ -69,13 +69,10 @@
             def _():
                 nw_ref[f] = n_ref[index]
 
-        @pl.when(odd_ref[0] == 0)
-        def _():
-            sw_ref[f] = s_ref[f]
+        sw_ref[f] = whiten(s_ref[f], fs_ref[...])
 
         @pl.when(odd_ref[0] != 0)
         def _():
-            sw_ref[f] = whiten(s_ref[f], fs_ref[...])
             nw_ref[f] = whiten(nw_ref[f], fn_ref[...])
             store(out_ref.at[:, 2 * index : 2 * index + 2], product(nw_ref[f], sw_ref[f]))
 
@@ -127,7 +124,7 @@
         @pl.when(odd == 0)
         def _():
             made(f, 0, whiten(near_ref[first + f], fn_ref[...]), far)
-            made(f, 1, whiten(own_ref[first + f], fs_ref[...]), far)
+            made(f, 1, own_ref[first + f], far)
 
         @pl.when(odd != 0)
         def _():
@@ -135,7 +132,7 @@
 
         return carry
 
-    lax.fori_loop(0, bins, step, 0)
+    lax.fori_loop(0, bins, step, 0, unroll=2)
     for f in range(bins):
         put(f, 1).wait()
 

time: 149 us -> 149 us (level)
  no operation moved by 1% of the time
where the time goes in v6:
time: 149 us
  blocking collectives  66.4 us (45%)
  starting transfers between devices  48.2 us (32%)
  Pallas kernels  15.6 us (10%)
  waiting for transfers between devices  12.1 us (8%)
  other arithmetic  3.7 us (2%)
  local copies, waits for them, and re-layouts  2.61 us (2%)
    all_to_all x2, blocking collectives, regroup(): lax.all_to_all(block, 'band', split_axis=0, concat_axis=0, tiled=True)  66.4 us
    ppermute x2, starting transfers between devices, shards(): pieces = [lax.ppermute(piece, 'pair', swap) for piece in pieces]  14.4 us
    ppermute x3, starting transfers between devices, exchange(): return lax.ppermute(value, 'band', route)  13.3 us
    ppermute x1, starting transfers between devices, shards(): lax.ppermute(own[:, 0], 'pair', swap)  8.16 us
    ppermute x3, waiting for transfers between devices, exchange(): return lax.ppermute(value, 'band', route)  7.97 us
    pallas_call x1, Pallas kernels, near_spectra(): pl.pallas_call(functools.partial(near_kernel, starts), grid=(8 // STEP,),...  6.62 us
    pallas_call x1, Pallas kernels, far_spectra(): pl.pallas_call(functools.partial(far_kernel, first), in_specs=[flag_spec(...  5.61 us
    ppermute x1, starting transfers between devices, shards(): u = lax.ppermute(whole, 'pair', across)  5 us
  transfers between devices with their start and end apart: 10, of which 5 were waited for; matrix products, arithmetic and copies ran while one was open for 2% of the time, Pallas kernels for 4%

profile of v6, /device:TPU:1, one launch (start us, length us, event | category | flops | bytes accessed | tf_op | source)
XLA Modules:
  0.0 148.7 jit_solution(5440281593402711914)
XLA Ops:
  0.0 0.0 copy-start
  0.0 2.7 %multiply_reduce_fusion = f32[384,256]{1,0:T(8,128)S(1)} fusion(bf16[8,2,384,256]{3,2,1,0:T(8,128)(2,1)} %s_ref.1), kind=kLoop, calls=%fused_computation | loop fusion | flops 4620288 | bytes 3538944 | tf_op jit(solution)/shard_map/reduce_sum | solution.py:277
  2.7 5.5 %collective-permute-start = (bf16[384,256]{1,0:T(8,128)(2,1)S(1)}, bf16[384,256]{1,0:T(8,128)(2,1)S(1)}, u32[]{:S(2)}, u32[]{:S(2)}) collective-permute-start(bf16[384,256]{1,0:T(8,128)(2,1)S(1)} %convert_element_type.30), channel_id=1, source_target_pairs={{0,4},{1,5},{2,6},{3,7},{4,0},{5,1},{6,2},{7,3},{8,12},{9,13},{10,... | collective-permute-start | bytes 589832 | tf_op jit(solution)/shard_map/ppermute | solution.py:261
  8.2 0.0 copy-done
  8.2 0.9 slice.13
  9.2 0.0 copy-start.2
  9.2 1.6 %slice.12 = bf16[6,2,384,256]{3,2,1,0:T(8,128)(2,1)} slice(bf16[8,2,384,256]{3,2,1,0:T(8,128)(2,1)S(1)} %copy-done), slice={[0:6], [0:2], [0:384], [0:256]} | slice | bytes 4718592 | tf_op jit(solution)/shard_map/slice | solution.py:278
  10.7 0.5 collective-permute-done
  11.3 5.0 %collective-permute-start.6 = (bf16[8,2,384,256]{3,2,1,0:T(8,128)(2,1)S(1)}, bf16[8,2,384,256]{3,2,1,0:T(8,128)(2,1)}, u32[]{:S(2)}, u32[]{:S(2)}) collective-permute-start(bf16[8,2,384,256]{3,2,1,0:T(8,128)(2,1)S(1)} %copy-done), channel_id=1, source_target_pairs={{16,0},{504,8},{32,16},{8,24},{48,32},{24,40},{64,48},{40,56},{80,... | collective-permute-start | bytes 9437192 | tf_op jit(solution)/shard_map/ppermute | solution.py:280
  16.3 12.2 %collective-permute-start.4 = (bf16[6,2,384,256]{3,2,1,0:T(8,128)(2,1)}, bf16[6,2,384,256]{3,2,1,0:T(8,128)(2,1)}, u32[]{:S(2)}, u32[]{:S(2)}) collective-permute-start(bf16[6,2,384,256]{3,2,1,0:T(8,128)(2,1)} %slice.12), channel_id=1, source_target_pairs={{8,0},{0,8},{24,16},{16,24},{40,32},{32,40},{56,48},{48,56},{72,64... | collective-permute-start | bytes 7077896 | tf_op jit(solution)/shard_map/ppermute | solution.py:281
  28.6 3.2 %collective-permute-start.1 = (bf16[384,256]{1,0:T(8,128)(2,1)S(1)}, bf16[384,256]{1,0:T(8,128)(2,1)S(1)}, u32[]{:S(2)}, u32[]{:S(2)}) collective-permute-start(bf16[384,256]{1,0:T(8,128)(2,1)S(1)} %fusion), channel_id=1, source_target_pairs={{0,1},{1,0},{2,3},{3,2},{4,5},{5,4},{6,7},{7,6},{8,9},{9,8},{10,11... | collective-permute-start | bytes 589832 | tf_op jit(solution)/shard_map/ppermute | solution.py:261
  31.8 2.2 %collective-permute-start.5 = (bf16[2,2,384,256]{3,2,1,0:T(8,128)(2,1)}, bf16[2,2,384,256]{3,2,1,0:T(8,128)(2,1)}, u32[]{:S(2)}, u32[]{:S(2)}) collective-permute-start(bf16[2,2,384,256]{3,2,1,0:T(8,128)(2,1)} %slice.13), channel_id=1, source_target_pairs={{8,0},{0,8},{24,16},{16,24},{40,32},{32,40},{56,48},{48,56},{72,64... | collective-permute-start | bytes 2359304 | tf_op jit(solution)/shard_map/ppermute | solution.py:281
  34.0 3.1 %collective-permute-done.1 = bf16[384,256]{1,0:T(8,128)(2,1)S(1)} collective-permute-done((bf16[384,256]{1,0:T(8,128)(2,1)S(1)}, bf16[384,256]{1,0:T(8,128)(2,1)S(1)}, u32[]{:S(2)}, u32[]{:S(2)}) %collective-permute-start.1) | collective-permute-done | bytes 196640 | tf_op jit(solution)/shard_map/ppermute | solution.py:261
  37.1 0.1 fusion.1
  37.2 4.6 %collective-permute-start.2 = (bf16[384,256]{1,0:T(8,128)(2,1)S(1)}, bf16[384,256]{1,0:T(8,128)(2,1)S(1)}, u32[]{:S(2)}, u32[]{:S(2)}) collective-permute-start(bf16[384,256]{1,0:T(8,128)(2,1)S(1)} %fusion.1), channel_id=1, source_target_pairs={{0,3},{1,2},{2,1},{3,0},{4,7},{5,6},{6,5},{7,4},{8,11},{9,10},{10,... | collective-permute-start | bytes 589832 | tf_op jit(solution)/shard_map/ppermute | solution.py:261
  41.8 4.4 %collective-permute-done.2 = bf16[384,256]{1,0:T(8,128)(2,1)S(1)} collective-permute-done((bf16[384,256]{1,0:T(8,128)(2,1)S(1)}, bf16[384,256]{1,0:T(8,128)(2,1)S(1)}, u32[]{:S(2)}, u32[]{:S(2)}) %collective-permute-start.2) | collective-permute-done | bytes 196640 | tf_op jit(solution)/shard_map/ppermute | solution.py:261
  46.2 0.0 copy-done.2
  46.2 0.9 fusion.2
  47.0 3.4 %collective-permute-start.3 = (bf16[384,256]{1,0:T(8,128)(2,1)}, bf16[384,256]{1,0:T(8,128)(2,1)}, u32[]{:S(2)}, u32[]{:S(2)}) collective-permute-start(bf16[384,256]{1,0:T(8,128)(2,1)} %get-tuple-element.19), channel_id=1, source_target_pairs={{8,0},{0,8},{24,16},{16,24},{40,32},{32,40},{56,48},{48,56},{72,64... | collective-permute-start | bytes 589832 | tf_op jit(solution)/shard_map/ppermute | solution.py:286
  50.4 1.9 %collective-permute-start.7 = (bf16[384,256]{1,0:T(8,128)(2,1)}, bf16[384,256]{1,0:T(8,128)(2,1)}, u32[]{:S(2)}, u32[]{:S(2)}) collective-permute-start(bf16[384,256]{1,0:T(8,128)(2,1)} %get-tuple-element.19), channel_id=1, source_target_pairs={{16,0},{504,8},{32,16},{8,24},{48,32},{24,40},{64,48},{40,56},{80,... | collective-permute-start | bytes 589832 | tf_op jit(solution)/shard_map/ppermute | solution.py:287
  52.4 0.0 collective-permute-done.3.fn_ref.fn_any
  52.4 0.0 collective-permute-done.5.refs_1_
  52.4 0.0 collective-permute-done.4.refs_0_
  52.4 6.6 %near_spectra.1 = (bf16[8,2,384,256]{3,2,1,0:T(8,128)(2,1)S(1)}, bf16[8,2,384,256]{3,2,1,0:T(8,128)(2,1)S(1)}, bf16[8,16,32,512]{3,2,1,0:T(8,128)(2,1)}) custom-call(s32[1]{0:T(128)} %bitcast.odd_ref, bf16[8,2,384,256]{3,2,1,0:T(8,128)(2,1)S(1)} %copy-done, f32[384,256]{1,0:T(8,128)S(1)} %get-tuple-element.20.fs_ref.fs_any, ...), custom_call_target="tpu_custom_call" | custom-call | tf_op jit(solution)/shard_map/near_spectra/pallas_call | solution.py:169
  59.0 2.6 %collective-permute-done.7.fu_any = bf16[384,256]{1,0:T(8,128)(2,1)} collective-permute-done((bf16[384,256]{1,0:T(8,128)(2,1)}, bf16[384,256]{1,0:T(8,128)(2,1)}, u32[]{:S(2)}, u32[]{:S(2)}) %collective-permute-start.7) | collective-permute-done | bytes 196640 | tf_op jit(solution)/shard_map/ppermute | solution.py:287
  61.6 0.0 collective-permute-done.6.u_ref
  61.6 5.6 %far0.1 = bf16[8,16,32,512]{3,2,1,0:T(8,128)(2,1)} custom-call(s32[1]{0:T(128)} %bitcast.odd_ref, bf16[8,2,384,256]{3,2,1,0:T(8,128)(2,1)S(1)} %get-tuple-element.15.own_ref, bf16[8,2,384,256]{3,2,1,0:T(8,128)(2,1)S(1)} %get-tuple-element.16.near_ref, bf16[8,2,384,256]{3,2,1,0:T(8,128)(2,1)} %collective-permute-done.6.u_ref, ...), custom_call_target="tpu_custom_call", output_to_operand_aliasing={{}: (7, {})} | custom-call | flops 3221225472 | bytes 8388608 | tf_op jit(solution)/shard_map/far0/pallas_call | solution.py:185
  67.3 0.0 copy-start.1
  67.3 51.2 %all_to_all.10.cross_ref = bf16[8,16,32,512]{3,2,1,0:T(8,128)(2,1)S(1)} all-to-all(bf16[8,16,32,512]{3,2,1,0:T(8,128)(2,1)} %far0.1), channel_id=1, replica_groups=mesh['pair'=64,'band'=8] {'band'}, dimensions={0} | all-to-all | bytes 8388608 | tf_op jit(solution)/shard_map/all_to_all | solution.py:265
  118.5 0.0 copy-done.1
  118.5 2.3 %to_lags.1 = bf16[8,2,4,32,256]{4,3,2,1,0:T(8,128)(2,1)S(1)} custom-call(bf16[512,2048]{1,0:T(8,128)(2,1)S(1)} %copy-done.1, bf16[8,16,32,512]{3,2,1,0:T(8,128)(2,1)S(1)} %all_to_all.10.cross_ref), custom_call_target="tpu_custom_call" | custom-call | flops 2147483648 | bytes 7340032 | tf_op jit(solution)/shard_map/to_lags/pallas_call | solution.py:227
  120.8 15.1 %all_to_all.11 = bf16[8,2,4,32,256]{4,3,2,1,0:T(8,128)(2,1)S(1)} all-to-all(bf16[8,2,4,32,256]{4,3,2,1,0:T(8,128)(2,1)S(1)} %to_lags.1), channel_id=1, replica_groups=mesh['pair'=64,'band'=8] {'band'}, dimensions={0} | all-to-all | bytes 2097152 | tf_op jit(solution)/shard_map/all_to_all | solution.py:265
  136.0 0.1 slice_bitcast_fusion
  136.1 1.9 %collective-permute-start.9 = (bf16[8,4,32,256]{3,2,1,0:T(8,128)(2,1)S(1)}, bf16[8,4,32,256]{3,2,1,0:T(8,128)(2,1)S(1)}, u32[]{:S(2)}, u32[]{:S(2)}) collective-permute-start(bf16[8,4,32,256]{3,2,1,0:T(8,128)(2,1)S(1)} %get-tuple-element.21), channel_id=1, source_target_pairs={{0,0},{24,8},{16,16},{40,24},{32,32},{56,40},{48,48},{72,56},{64,6... | collective-permute-start | bytes 1572872 | tf_op jit(solution)/shard_map/ppermute | solution.py:292
  138.0 8.2 %collective-permute-start.8 = (bf16[8,4,32,256]{3,2,1,0:T(8,128)(2,1)S(1)}, bf16[8,4,32,256]{3,2,1,0:T(8,128)(2,1)S(1)}, u32[]{:S(2)}, u32[]{:S(2)}) collective-permute-start(bf16[8,4,32,256]{3,2,1,0:T(8,128)(2,1)S(1)} %get-tuple-element.22), channel_id=1, source_target_pairs={{8,0},{0,8},{24,16},{16,24},{40,32},{32,40},{56,48},{48,56},{72,64... | collective-permute-start | bytes 1572872 | tf_op jit(solution)/shard_map/ppermute | solution.py:292
  146.2 0.0 collective-permute-done.9.two_ref
  146.2 1.5 %collective-permute-done.8.one_ref = bf16[8,4,32,256]{3,2,1,0:T(8,128)(2,1)S(1)} collective-permute-done((bf16[8,4,32,256]{3,2,1,0:T(8,128)(2,1)S(1)}, bf16[8,4,32,256]{3,2,1,0:T(8,128)(2,1)S(1)}, u32[]{:S(2)}, u32[]{:S(2)}) %collective-permute-start.8) | collective-permute-done | bytes 524320 | tf_op jit(solution)/shard_map/ppermute | solution.py:292
  147.7 1.0 assemble.1
  (2 shorter events, 0.1 us)
Async XLA Ops:
  0.0 8.2 %copy-start = (bf16[8,2,384,256]{3,2,1,0:T(8,128)(2,1)S(1)}, bf16[8,2,384,256]{3,2,1,0:T(8,128)(2,1)}, u32[]{:S(2)}) copy-start(bf16[8,2,384,256]{3,2,1,0:T(8,128)(2,1)} %s_ref.1) | copy-start | bytes 9437188
  2.7 8.5 %collective-permute-start = (bf16[384,256]{1,0:T(8,128)(2,1)S(1)}, bf16[384,256]{1,0:T(8,128)(2,1)S(1)}, u32[]{:S(2)}, u32[]{:S(2)}) collective-permute-start(bf16[384,256]{1,0:T(8,128)(2,1)S(1)} %convert_element_type.30), channel_id=1, source_target_pairs={{0,4},{1,5},{2,6},{3,7},{4,0},{5,1},{6,2},{7,3},{8,12},{9,13},{10,... | collective-permute-start | bytes 589832 | tf_op jit(solution)/shard_map/ppermute | solution.py:261
  9.2 37.0 %copy-start.2 = (s32[384,256]{1,0:T(8,128)S(1)}, s32[384,256]{1,0:T(8,128)}, u32[]{:S(2)}) copy-start(s32[384,256]{1,0:T(8,128)} %param.4) | copy-start | bytes 1179652
  11.3 50.4 %collective-permute-start.6 = (bf16[8,2,384,256]{3,2,1,0:T(8,128)(2,1)S(1)}, bf16[8,2,384,256]{3,2,1,0:T(8,128)(2,1)}, u32[]{:S(2)}, u32[]{:S(2)}) collective-permute-start(bf16[8,2,384,256]{3,2,1,0:T(8,128)(2,1)S(1)} %copy-done), channel_id=1, source_target_pairs={{16,0},{504,8},{32,16},{8,24},{48,32},{24,40},{64,48},{40,56},{80,... | collective-permute-start | bytes 9437192 | tf_op jit(solution)/shard_map/ppermute | solution.py:280
  16.3 36.1 %collective-permute-start.4 = (bf16[6,2,384,256]{3,2,1,0:T(8,128)(2,1)}, bf16[6,2,384,256]{3,2,1,0:T(8,128)(2,1)}, u32[]{:S(2)}, u32[]{:S(2)}) collective-permute-start(bf16[6,2,384,256]{3,2,1,0:T(8,128)(2,1)} %slice.12), channel_id=1, source_target_pairs={{8,0},{0,8},{24,16},{16,24},{40,32},{32,40},{56,48},{48,56},{72,64... | collective-permute-start | bytes 7077896 | tf_op jit(solution)/shard_map/ppermute | solution.py:281
  28.6 8.5 %collective-permute-start.1 = (bf16[384,256]{1,0:T(8,128)(2,1)S(1)}, bf16[384,256]{1,0:T(8,128)(2,1)S(1)}, u32[]{:S(2)}, u32[]{:S(2)}) collective-permute-start(bf16[384,256]{1,0:T(8,128)(2,1)S(1)} %fusion), channel_id=1, source_target_pairs={{0,1},{1,0},{2,3},{3,2},{4,5},{5,4},{6,7},{7,6},{8,9},{9,8},{10,11... | collective-permute-start | bytes 589832 | tf_op jit(solution)/shard_map/ppermute | solution.py:261
  31.8 20.6 %collective-permute-start.5 = (bf16[2,2,384,256]{3,2,1,0:T(8,128)(2,1)}, bf16[2,2,384,256]{3,2,1,0:T(8,128)(2,1)}, u32[]{:S(2)}, u32[]{:S(2)}) collective-permute-start(bf16[2,2,384,256]{3,2,1,0:T(8,128)(2,1)} %slice.13), channel_id=1, source_target_pairs={{8,0},{0,8},{24,16},{16,24},{40,32},{32,40},{56,48},{48,56},{72,64... | collective-permute-start | bytes 2359304 | tf_op jit(solution)/shard_map/ppermute | solution.py:281
  37.2 9.0 %collective-permute-start.2 = (bf16[384,256]{1,0:T(8,128)(2,1)S(1)}, bf16[384,256]{1,0:T(8,128)(2,1)S(1)}, u32[]{:S(2)}, u32[]{:S(2)}) collective-permute-start(bf16[384,256]{1,0:T(8,128)(2,1)S(1)} %fusion.1), channel_id=1, source_target_pairs={{0,3},{1,2},{2,1},{3,0},{4,7},{5,6},{6,5},{7,4},{8,11},{9,10},{10,... | collective-permute-start | bytes 589832 | tf_op jit(solution)/shard_map/ppermute | solution.py:261
  47.0 5.3 %collective-permute-start.3 = (bf16[384,256]{1,0:T(8,128)(2,1)}, bf16[384,256]{1,0:T(8,128)(2,1)}, u32[]{:S(2)}, u32[]{:S(2)}) collective-permute-start(bf16[384,256]{1,0:T(8,128)(2,1)} %get-tuple-element.19), channel_id=1, source_target_pairs={{8,0},{0,8},{24,16},{16,24},{40,32},{32,40},{56,48},{48,56},{72,64... | collective-permute-start | bytes 589832 | tf_op jit(solution)/shard_map/ppermute | solution.py:286
  50.4 11.2 %collective-permute-start.7 = (bf16[384,256]{1,0:T(8,128)(2,1)}, bf16[384,256]{1,0:T(8,128)(2,1)}, u32[]{:S(2)}, u32[]{:S(2)}) collective-permute-start(bf16[384,256]{1,0:T(8,128)(2,1)} %get-tuple-element.19), channel_id=1, source_target_pairs={{16,0},{504,8},{32,16},{8,24},{48,32},{24,40},{64,48},{40,56},{80,... | collective-permute-start | bytes 589832 | tf_op jit(solution)/shard_map/ppermute | solution.py:287
  67.3 51.2 %copy-start.1 = (bf16[512,2048]{1,0:T(8,128)(2,1)S(1)}, bf16[512,2048]{1,0:T(8,128)(2,1)}, u32[]{:S(2)}) copy-start(bf16[512,2048]{1,0:T(8,128)(2,1)} %constant.28.clone.matrix_ref) | copy-start | bytes 6291460
  136.1 10.1 %collective-permute-start.9 = (bf16[8,4,32,256]{3,2,1,0:T(8,128)(2,1)S(1)}, bf16[8,4,32,256]{3,2,1,0:T(8,128)(2,1)S(1)}, u32[]{:S(2)}, u32[]{:S(2)}) collective-permute-start(bf16[8,4,32,256]{3,2,1,0:T(8,128)(2,1)S(1)} %get-tuple-element.21), channel_id=1, source_target_pairs={{0,0},{24,8},{16,16},{40,24},{32,32},{56,40},{48,48},{72,56},{64,6... | collective-permute-start | bytes 1572872 | tf_op jit(solution)/shard_map/ppermute | solution.py:292
  138.0 9.7 %collective-permute-start.8 = (bf16[8,4,32,256]{3,2,1,0:T(8,128)(2,1)S(1)}, bf16[8,4,32,256]{3,2,1,0:T(8,128)(2,1)S(1)}, u32[]{:S(2)}, u32[]{:S(2)}) collective-permute-start(bf16[8,4,32,256]{3,2,1,0:T(8,128)(2,1)S(1)} %get-tuple-element.22), channel_id=1, source_target_pairs={{8,0},{0,8},{24,16},{16,24},{40,32},{32,40},{56,48},{48,56},{72,64... | collective-permute-start | bytes 1572872 | tf_op jit(solution)/shard_map/ppermute | solution.py:292

commit v7 on v6

--- a/solution.py
+++ b/solution.py
@@ -77,7 +77,7 @@
             store(out_ref.at[:, 2 * index : 2 * index + 2], product(nw_ref[f], sw_ref[f]))
 
 
-def far_kernel(first, odd_ref, own_ref, near_ref, u_ref, fs_any, fn_any, fu_any, _, out_ref, held_ref, fs_ref, fn_ref, fu_ref, send_ref, in_sem, factor_sem, out_sem):
+def far_kernel(first, odd_ref, own_ref, near_ref, u_ref, fn_any, fu_any, _, out_ref, held_ref, fn_ref, fu_ref, send_ref, in_sem, factor_sem, out_sem):
     bins = u_ref.shape[0]
     odd = odd_ref[0]
 
@@ -97,7 +97,7 @@
         put(f, part).start()
 
     def factor(index):
-        pairs = ((fu_any, fu_ref), (fs_any, fs_ref), (fn_any, fn_ref))
+        pairs = ((fu_any, fu_ref), (fn_any, fn_ref))
         return pltpu.make_async_copy(*pairs[index], factor_sem.at[index])
 
     factor(0).start()
@@ -106,7 +106,6 @@
     @pl.when(odd == 0)
     def _():
         factor(1).start()
-        factor(2).start()
 
     for f in range(1, bins):
         fetch(f).start()
@@ -115,7 +114,6 @@
     @pl.when(odd == 0)
     def _():
         factor(1).wait()
-        factor(2).wait()
 
     def step(f, carry):
         fetch(f).wait()
@@ -179,31 +177,30 @@
     )(odd, s, fs, fn, *pieces)
 
 
-def far_spectra(first, odd, own, near, u, fs, fn, fu, filled):
+def far_spectra(first, odd, own, near, u, fn, fu, filled):
     bins = u.shape[0]
     anywhere = pl.BlockSpec(memory_space=pl.ANY)
     return pl.pallas_call(
         functools.partial(far_kernel, first),
-        in_specs=[flag_spec(), held_spec(), held_spec()] + [anywhere] * 5,
+        in_specs=[flag_spec(), held_spec(), held_spec()] + [anywhere] * 4,
         out_specs=anywhere,
         out_shape=pltpu.HBM(SEND, BF16),
         scratch_shapes=[
             pltpu.VMEM((bins, 2, WIN, BLOCK), BF16),
-            pltpu.VMEM((WIN, BLOCK), fs.dtype),
             pltpu.VMEM((WIN, BLOCK), fn.dtype),
             pltpu.VMEM((WIN, BLOCK), fu.dtype),
             pltpu.VMEM((8, 2 * bins, 32, 2 * BLOCK), BF16),
             pltpu.SemaphoreType.DMA((bins,)),
-            pltpu.SemaphoreType.DMA((3,)),
+            pltpu.SemaphoreType.DMA((2,)),
             pltpu.SemaphoreType.DMA((2, bins)),
         ],
-        input_output_aliases={7: 0},
+        input_output_aliases={6: 0},
         compiler_params=params(),
         cost_estimate=pl.CostEstimate(
             flops=bins * 2 * 2 * 768 * 256 * 512, bytes_accessed=bins << 20, transcendentals=0
         ),
         name="far" + str(first),
-    )(odd, own, near, u, fs, fn, fu, filled)
+    )(odd, own, near, u, fn, fu, filled)
 
 
 def lags_kernel(scale, matrix_ref, cross_ref, out_ref):
@@ -287,7 +284,7 @@
     fu = lax.ppermute(fs.astype(BF16), "pair", across)
 
     sw, nw, cross = near_spectra(flag, spectra, fs, fn, pieces)
-    cross = far_spectra(0, flag, sw, nw, u, fs, fn, fu, cross)
+    cross = far_spectra(0, flag, sw, nw, u, fn, fu, cross)
     own = regroup(to_lags(regroup(cross)))
     return assemble(lax.ppermute(own[:, 0], "pair", swap), lax.ppermute(own[:, 1], "pair", back))
 

time: 149 us -> 150 us (level)
  no operation moved by 1% of the time
where the time goes in v7:
time: 150 us; the launch traced here: 149 us
  blocking collectives  66.4 us (44%)
  starting transfers between devices  48.2 us (32%)
  Pallas kernels  16.1 us (11%)
  waiting for transfers between devices  12.1 us (8%)
  other arithmetic  3.7 us (2%)
  local copies, waits for them, and re-layouts  2.61 us (2%)
    all_to_all x2, blocking collectives, regroup(): lax.all_to_all(block, 'band', split_axis=0, concat_axis=0, tiled=True)  66.4 us
    ppermute x2, starting transfers between devices, shards(): pieces = [lax.ppermute(piece, 'pair', swap) for piece in pieces]  14.4 us
    ppermute x3, starting transfers between devices, exchange(): return lax.ppermute(value, 'band', route)  13.3 us
    ppermute x1, starting transfers between devices, shards(): lax.ppermute(own[:, 0], 'pair', swap)  8.17 us
    ppermute x3, waiting for transfers between devices, exchange(): return lax.ppermute(value, 'band', route)  7.97 us
    pallas_call x1, Pallas kernels, near_spectra(): pl.pallas_call(functools.partial(near_kernel, starts), grid=(8 // STEP,),...  6.62 us
    pallas_call x1, Pallas kernels, far_spectra(): pl.pallas_call(functools.partial(far_kernel, first), in_specs=[flag_spec(...  6.14 us
    ppermute x1, starting transfers between devices, shards(): u = lax.ppermute(whole, 'pair', across)  5 us
  transfers between devices with their start and end apart: 10, of which 5 were waited for; matrix products, arithmetic and copies ran while one was open for 2% of the time, Pallas kernels for 4%

profile of v7, /device:TPU:1, one launch (start us, length us, event | category | flops | bytes accessed | tf_op | source)
XLA Modules:
  0.0 149.2 jit_solution(10731513386803498859)
XLA Ops:
  0.0 0.0 copy-start
  0.0 2.7 %multiply_reduce_fusion = f32[384,256]{1,0:T(8,128)S(1)} fusion(bf16[8,2,384,256]{3,2,1,0:T(8,128)(2,1)} %s_ref.1), kind=kLoop, calls=%fused_computation | loop fusion | flops 4620288 | bytes 3538944 | tf_op jit(solution)/shard_map/reduce_sum | solution.py:274
  2.7 5.5 %collective-permute-start = (bf16[384,256]{1,0:T(8,128)(2,1)S(1)}, bf16[384,256]{1,0:T(8,128)(2,1)S(1)}, u32[]{:S(2)}, u32[]{:S(2)}) collective-permute-start(bf16[384,256]{1,0:T(8,128)(2,1)S(1)} %convert_element_type.30), channel_id=1, source_target_pairs={{0,4},{1,5},{2,6},{3,7},{4,0},{5,1},{6,2},{7,3},{8,12},{9,13},{10,... | collective-permute-start | bytes 589832 | tf_op jit(solution)/shard_map/ppermute | solution.py:258
  8.2 0.0 copy-done
  8.2 0.9 slice.13
  9.2 0.0 copy-start.2
  9.2 1.6 %slice.12 = bf16[6,2,384,256]{3,2,1,0:T(8,128)(2,1)} slice(bf16[8,2,384,256]{3,2,1,0:T(8,128)(2,1)S(1)} %copy-done), slice={[0:6], [0:2], [0:384], [0:256]} | slice | bytes 4718592 | tf_op jit(solution)/shard_map/slice | solution.py:275
  10.7 0.5 collective-permute-done
  11.3 5.0 %collective-permute-start.6 = (bf16[8,2,384,256]{3,2,1,0:T(8,128)(2,1)S(1)}, bf16[8,2,384,256]{3,2,1,0:T(8,128)(2,1)}, u32[]{:S(2)}, u32[]{:S(2)}) collective-permute-start(bf16[8,2,384,256]{3,2,1,0:T(8,128)(2,1)S(1)} %copy-done), channel_id=1, source_target_pairs={{16,0},{504,8},{32,16},{8,24},{48,32},{24,40},{64,48},{40,56},{80,... | collective-permute-start | bytes 9437192 | tf_op jit(solution)/shard_map/ppermute | solution.py:277
  16.3 12.2 %collective-permute-start.4 = (bf16[6,2,384,256]{3,2,1,0:T(8,128)(2,1)}, bf16[6,2,384,256]{3,2,1,0:T(8,128)(2,1)}, u32[]{:S(2)}, u32[]{:S(2)}) collective-permute-start(bf16[6,2,384,256]{3,2,1,0:T(8,128)(2,1)} %slice.12), channel_id=1, source_target_pairs={{8,0},{0,8},{24,16},{16,24},{40,32},{32,40},{56,48},{48,56},{72,64... | collective-permute-start | bytes 7077896 | tf_op jit(solution)/shard_map/ppermute | solution.py:278
  28.6 3.2 %collective-permute-start.1 = (bf16[384,256]{1,0:T(8,128)(2,1)S(1)}, bf16[384,256]{1,0:T(8,128)(2,1)S(1)}, u32[]{:S(2)}, u32[]{:S(2)}) collective-permute-start(bf16[384,256]{1,0:T(8,128)(2,1)S(1)} %fusion), channel_id=1, source_target_pairs={{0,1},{1,0},{2,3},{3,2},{4,5},{5,4},{6,7},{7,6},{8,9},{9,8},{10,11... | collective-permute-start | bytes 589832 | tf_op jit(solution)/shard_map/ppermute | solution.py:258
  31.8 2.2 %collective-permute-start.5 = (bf16[2,2,384,256]{3,2,1,0:T(8,128)(2,1)}, bf16[2,2,384,256]{3,2,1,0:T(8,128)(2,1)}, u32[]{:S(2)}, u32[]{:S(2)}) collective-permute-start(bf16[2,2,384,256]{3,2,1,0:T(8,128)(2,1)} %slice.13), channel_id=1, source_target_pairs={{8,0},{0,8},{24,16},{16,24},{40,32},{32,40},{56,48},{48,56},{72,64... | collective-permute-start | bytes 2359304 | tf_op jit(solution)/shard_map/ppermute | solution.py:278
  34.0 3.1 %collective-permute-done.1 = bf16[384,256]{1,0:T(8,128)(2,1)S(1)} collective-permute-done((bf16[384,256]{1,0:T(8,128)(2,1)S(1)}, bf16[384,256]{1,0:T(8,128)(2,1)S(1)}, u32[]{:S(2)}, u32[]{:S(2)}) %collective-permute-start.1) | collective-permute-done | bytes 196640 | tf_op jit(solution)/shard_map/ppermute | solution.py:258
  37.1 0.1 fusion.1
  37.2 4.6 %collective-permute-start.2 = (bf16[384,256]{1,0:T(8,128)(2,1)S(1)}, bf16[384,256]{1,0:T(8,128)(2,1)S(1)}, u32[]{:S(2)}, u32[]{:S(2)}) collective-permute-start(bf16[384,256]{1,0:T(8,128)(2,1)S(1)} %fusion.1), channel_id=1, source_target_pairs={{0,3},{1,2},{2,1},{3,0},{4,7},{5,6},{6,5},{7,4},{8,11},{9,10},{10,... | collective-permute-start | bytes 589832 | tf_op jit(solution)/shard_map/ppermute | solution.py:258
  41.8 4.4 %collective-permute-done.2 = bf16[384,256]{1,0:T(8,128)(2,1)S(1)} collective-permute-done((bf16[384,256]{1,0:T(8,128)(2,1)S(1)}, bf16[384,256]{1,0:T(8,128)(2,1)S(1)}, u32[]{:S(2)}, u32[]{:S(2)}) %collective-permute-start.2) | collective-permute-done | bytes 196640 | tf_op jit(solution)/shard_map/ppermute | solution.py:258
  46.2 0.0 copy-done.2
  46.2 0.9 fusion.2
  47.0 3.4 %collective-permute-start.3 = (bf16[384,256]{1,0:T(8,128)(2,1)}, bf16[384,256]{1,0:T(8,128)(2,1)}, u32[]{:S(2)}, u32[]{:S(2)}) collective-permute-start(bf16[384,256]{1,0:T(8,128)(2,1)} %get-tuple-element.19), channel_id=1, source_target_pairs={{8,0},{0,8},{24,16},{16,24},{40,32},{32,40},{56,48},{48,56},{72,64... | collective-permute-start | bytes 589832 | tf_op jit(solution)/shard_map/ppermute | solution.py:283
  50.4 1.9 %collective-permute-start.7 = (bf16[384,256]{1,0:T(8,128)(2,1)}, bf16[384,256]{1,0:T(8,128)(2,1)}, u32[]{:S(2)}, u32[]{:S(2)}) collective-permute-start(bf16[384,256]{1,0:T(8,128)(2,1)} %get-tuple-element.19), channel_id=1, source_target_pairs={{16,0},{504,8},{32,16},{8,24},{48,32},{24,40},{64,48},{40,56},{80,... | collective-permute-start | bytes 589832 | tf_op jit(solution)/shard_map/ppermute | solution.py:284
  52.4 0.0 collective-permute-done.3.fn_ref.fn_any
  52.4 0.0 collective-permute-done.5.refs_1_
  52.4 0.0 collective-permute-done.4.refs_0_
  52.4 6.6 %near_spectra.1 = (bf16[8,2,384,256]{3,2,1,0:T(8,128)(2,1)S(1)}, bf16[8,2,384,256]{3,2,1,0:T(8,128)(2,1)S(1)}, bf16[8,16,32,512]{3,2,1,0:T(8,128)(2,1)}) custom-call(s32[1]{0:T(128)} %bitcast.odd_ref, bf16[8,2,384,256]{3,2,1,0:T(8,128)(2,1)S(1)} %copy-done, f32[384,256]{1,0:T(8,128)S(1)} %get-tuple-element.20.fs_ref, ...), custom_call_target="tpu_custom_call" | custom-call | tf_op jit(solution)/shard_map/near_spectra/pallas_call | solution.py:167
  59.0 2.6 %collective-permute-done.7.fu_any = bf16[384,256]{1,0:T(8,128)(2,1)} collective-permute-done((bf16[384,256]{1,0:T(8,128)(2,1)}, bf16[384,256]{1,0:T(8,128)(2,1)}, u32[]{:S(2)}, u32[]{:S(2)}) %collective-permute-start.7) | collective-permute-done | bytes 196640 | tf_op jit(solution)/shard_map/ppermute | solution.py:284
  61.6 0.0 collective-permute-done.6.u_ref
  61.6 6.1 %far0.1 = bf16[8,16,32,512]{3,2,1,0:T(8,128)(2,1)} custom-call(s32[1]{0:T(128)} %bitcast.odd_ref, bf16[8,2,384,256]{3,2,1,0:T(8,128)(2,1)S(1)} %get-tuple-element.15.own_ref, bf16[8,2,384,256]{3,2,1,0:T(8,128)(2,1)S(1)} %get-tuple-element.16.near_ref, bf16[8,2,384,256]{3,2,1,0:T(8,128)(2,1)} %collective-permute-done.6.u_ref, ...), custom_call_target="tpu_custom_call", output_to_operand_aliasing={{}: (6, {})} | custom-call | flops 3221225472 | bytes 8388608 | tf_op jit(solution)/shard_map/far0/pallas_call | solution.py:183
  67.8 0.0 copy-start.1
  67.8 51.1 %all_to_all.10.cross_ref = bf16[8,16,32,512]{3,2,1,0:T(8,128)(2,1)S(1)} all-to-all(bf16[8,16,32,512]{3,2,1,0:T(8,128)(2,1)} %far0.1), channel_id=1, replica_groups=mesh['pair'=64,'band'=8] {'band'}, dimensions={0} | all-to-all | bytes 8388608 | tf_op jit(solution)/shard_map/all_to_all | solution.py:262
  118.9 0.0 copy-done.1
  118.9 2.3 %to_lags.1 = bf16[8,2,4,32,256]{4,3,2,1,0:T(8,128)(2,1)S(1)} custom-call(bf16[512,2048]{1,0:T(8,128)(2,1)S(1)} %copy-done.1, bf16[8,16,32,512]{3,2,1,0:T(8,128)(2,1)S(1)} %all_to_all.10.cross_ref), custom_call_target="tpu_custom_call" | custom-call | flops 2147483648 | bytes 7340032 | tf_op jit(solution)/shard_map/to_lags/pallas_call | solution.py:224
  121.3 15.2 %all_to_all.11 = bf16[8,2,4,32,256]{4,3,2,1,0:T(8,128)(2,1)S(1)} all-to-all(bf16[8,2,4,32,256]{4,3,2,1,0:T(8,128)(2,1)S(1)} %to_lags.1), channel_id=1, replica_groups=mesh['pair'=64,'band'=8] {'band'}, dimensions={0} | all-to-all | bytes 2097152 | tf_op jit(solution)/shard_map/all_to_all | solution.py:262
  136.5 0.1 slice_bitcast_fusion
  136.6 1.9 %collective-permute-start.9 = (bf16[8,4,32,256]{3,2,1,0:T(8,128)(2,1)S(1)}, bf16[8,4,32,256]{3,2,1,0:T(8,128)(2,1)S(1)}, u32[]{:S(2)}, u32[]{:S(2)}) collective-permute-start(bf16[8,4,32,256]{3,2,1,0:T(8,128)(2,1)S(1)} %get-tuple-element.21), channel_id=1, source_target_pairs={{0,0},{24,8},{16,16},{40,24},{32,32},{56,40},{48,48},{72,56},{64,6... | collective-permute-start | bytes 1572872 | tf_op jit(solution)/shard_map/ppermute | solution.py:289
  138.5 8.2 %collective-permute-start.8 = (bf16[8,4,32,256]{3,2,1,0:T(8,128)(2,1)S(1)}, bf16[8,4,32,256]{3,2,1,0:T(8,128)(2,1)S(1)}, u32[]{:S(2)}, u32[]{:S(2)}) collective-permute-start(bf16[8,4,32,256]{3,2,1,0:T(8,128)(2,1)S(1)} %get-tuple-element.22), channel_id=1, source_target_pairs={{8,0},{0,8},{24,16},{16,24},{40,32},{32,40},{56,48},{48,56},{72,64... | collective-permute-start | bytes 1572872 | tf_op jit(solution)/shard_map/ppermute | solution.py:289
  146.7 0.0 collective-permute-done.9.two_ref
  146.7 1.5 %collective-permute-done.8.one_ref = bf16[8,4,32,256]{3,2,1,0:T(8,128)(2,1)S(1)} collective-permute-done((bf16[8,4,32,256]{3,2,1,0:T(8,128)(2,1)S(1)}, bf16[8,4,32,256]{3,2,1,0:T(8,128)(2,1)S(1)}, u32[]{:S(2)}, u32[]{:S(2)}) %collective-permute-start.8) | collective-permute-done | bytes 524320 | tf_op jit(solution)/shard_map/ppermute | solution.py:289
  148.2 1.0 assemble.1
  (2 shorter events, 0.1 us)
Async XLA Ops:
  0.0 8.2 %copy-start = (bf16[8,2,384,256]{3,2,1,0:T(8,128)(2,1)S(1)}, bf16[8,2,384,256]{3,2,1,0:T(8,128)(2,1)}, u32[]{:S(2)}) copy-start(bf16[8,2,384,256]{3,2,1,0:T(8,128)(2,1)} %s_ref.1) | copy-start | bytes 9437188
  2.7 8.5 %collective-permute-start = (bf16[384,256]{1,0:T(8,128)(2,1)S(1)}, bf16[384,256]{1,0:T(8,128)(2,1)S(1)}, u32[]{:S(2)}, u32[]{:S(2)}) collective-permute-start(bf16[384,256]{1,0:T(8,128)(2,1)S(1)} %convert_element_type.30), channel_id=1, source_target_pairs={{0,4},{1,5},{2,6},{3,7},{4,0},{5,1},{6,2},{7,3},{8,12},{9,13},{10,... | collective-permute-start | bytes 589832 | tf_op jit(solution)/shard_map/ppermute | solution.py:258
  9.2 37.0 %copy-start.2 = (s32[384,256]{1,0:T(8,128)S(1)}, s32[384,256]{1,0:T(8,128)}, u32[]{:S(2)}) copy-start(s32[384,256]{1,0:T(8,128)} %param.4) | copy-start | bytes 1179652
  11.3 50.4 %collective-permute-start.6 = (bf16[8,2,384,256]{3,2,1,0:T(8,128)(2,1)S(1)}, bf16[8,2,384,256]{3,2,1,0:T(8,128)(2,1)}, u32[]{:S(2)}, u32[]{:S(2)}) collective-permute-start(bf16[8,2,384,256]{3,2,1,0:T(8,128)(2,1)S(1)} %copy-done), channel_id=1, source_target_pairs={{16,0},{504,8},{32,16},{8,24},{48,32},{24,40},{64,48},{40,56},{80,... | collective-permute-start | bytes 9437192 | tf_op jit(solution)/shard_map/ppermute | solution.py:277
  16.3 36.1 %collective-permute-start.4 = (bf16[6,2,384,256]{3,2,1,0:T(8,128)(2,1)}, bf16[6,2,384,256]{3,2,1,0:T(8,128)(2,1)}, u32[]{:S(2)}, u32[]{:S(2)}) collective-permute-start(bf16[6,2,384,256]{3,2,1,0:T(8,128)(2,1)} %slice.12), channel_id=1, source_target_pairs={{8,0},{0,8},{24,16},{16,24},{40,32},{32,40},{56,48},{48,56},{72,64... | collective-permute-start | bytes 7077896 | tf_op jit(solution)/shard_map/ppermute | solution.py:278
  28.6 8.5 %collective-permute-start.1 = (bf16[384,256]{1,0:T(8,128)(2,1)S(1)}, bf16[384,256]{1,0:T(8,128)(2,1)S(1)}, u32[]{:S(2)}, u32[]{:S(2)}) collective-permute-start(bf16[384,256]{1,0:T(8,128)(2,1)S(1)} %fusion), channel_id=1, source_target_pairs={{0,1},{1,0},{2,3},{3,2},{4,5},{5,4},{6,7},{7,6},{8,9},{9,8},{10,11... | collective-permute-start | bytes 589832 | tf_op jit(solution)/shard_map/ppermute | solution.py:258
  31.8 20.6 %collective-permute-start.5 = (bf16[2,2,384,256]{3,2,1,0:T(8,128)(2,1)}, bf16[2,2,384,256]{3,2,1,0:T(8,128)(2,1)}, u32[]{:S(2)}, u32[]{:S(2)}) collective-permute-start(bf16[2,2,384,256]{3,2,1,0:T(8,128)(2,1)} %slice.13), channel_id=1, source_target_pairs={{8,0},{0,8},{24,16},{16,24},{40,32},{32,40},{56,48},{48,56},{72,64... | collective-permute-start | bytes 2359304 | tf_op jit(solution)/shard_map/ppermute | solution.py:278
  37.2 9.0 %collective-permute-start.2 = (bf16[384,256]{1,0:T(8,128)(2,1)S(1)}, bf16[384,256]{1,0:T(8,128)(2,1)S(1)}, u32[]{:S(2)}, u32[]{:S(2)}) collective-permute-start(bf16[384,256]{1,0:T(8,128)(2,1)S(1)} %fusion.1), channel_id=1, source_target_pairs={{0,3},{1,2},{2,1},{3,0},{4,7},{5,6},{6,5},{7,4},{8,11},{9,10},{10,... | collective-permute-start | bytes 589832 | tf_op jit(solution)/shard_map/ppermute | solution.py:258
  47.0 5.3 %collective-permute-start.3 = (bf16[384,256]{1,0:T(8,128)(2,1)}, bf16[384,256]{1,0:T(8,128)(2,1)}, u32[]{:S(2)}, u32[]{:S(2)}) collective-permute-start(bf16[384,256]{1,0:T(8,128)(2,1)} %get-tuple-element.19), channel_id=1, source_target_pairs={{8,0},{0,8},{24,16},{16,24},{40,32},{32,40},{56,48},{48,56},{72,64... | collective-permute-start | bytes 589832 | tf_op jit(solution)/shard_map/ppermute | solution.py:283
  50.4 11.2 %collective-permute-start.7 = (bf16[384,256]{1,0:T(8,128)(2,1)}, bf16[384,256]{1,0:T(8,128)(2,1)}, u32[]{:S(2)}, u32[]{:S(2)}) collective-permute-start(bf16[384,256]{1,0:T(8,128)(2,1)} %get-tuple-element.19), channel_id=1, source_target_pairs={{16,0},{504,8},{32,16},{8,24},{48,32},{24,40},{64,48},{40,56},{80,... | collective-permute-start | bytes 589832 | tf_op jit(solution)/shard_map/ppermute | solution.py:284
  67.8 51.1 %copy-start.1 = (bf16[512,2048]{1,0:T(8,128)(2,1)S(1)}, bf16[512,2048]{1,0:T(8,128)(2,1)}, u32[]{:S(2)}) copy-start(bf16[512,2048]{1,0:T(8,128)(2,1)} %constant.28.clone.matrix_ref) | copy-start | bytes 6291460
  136.6 10.1 %collective-permute-start.9 = (bf16[8,4,32,256]{3,2,1,0:T(8,128)(2,1)S(1)}, bf16[8,4,32,256]{3,2,1,0:T(8,128)(2,1)S(1)}, u32[]{:S(2)}, u32[]{:S(2)}) collective-permute-start(bf16[8,4,32,256]{3,2,1,0:T(8,128)(2,1)S(1)} %get-tuple-element.21), channel_id=1, source_target_pairs={{0,0},{24,8},{16,16},{40,24},{32,32},{56,40},{48,48},{72,56},{64,6... | collective-permute-start | bytes 1572872 | tf_op jit(solution)/shard_map/ppermute | solution.py:289
  138.5 9.7 %collective-permute-start.8 = (bf16[8,4,32,256]{3,2,1,0:T(8,128)(2,1)S(1)}, bf16[8,4,32,256]{3,2,1,0:T(8,128)(2,1)S(1)}, u32[]{:S(2)}, u32[]{:S(2)}) collective-permute-start(bf16[8,4,32,256]{3,2,1,0:T(8,128)(2,1)S(1)} %get-tuple-element.22), channel_id=1, source_target_pairs={{8,0},{0,8},{24,16},{16,24},{40,32},{32,40},{56,48},{48,56},{72,64... | collective-permute-start | bytes 1572872 | tf_op jit(solution)/shard_map/ppermute | solution.py:289
